TPU v7x, 32 devices: a whole 2x2x4 slice. The times are simulated.
32 devices in a mesh: pipe: 4 (over y, x), seq: 8 (over z, core).
Axes of the slice: x: 2, y: 2, z: 4, core: 2. Of those that a mesh axis runs over, the one named last changes fastest.
Arguments:
- inputs: bfloat16 [4, 1024, 2048], P('pipe', 'seq'), may hold values from -6 to 6
- lengths: int32 [4, 32], replicated, may hold values from 1 to 128, 1024 in all within a row
- order: int32 [4], replicated, may hold values from 0 to 3, each once
- norm_gain: float32 [4, 2048], P('pipe'), may hold values from 0.25 to 1.75
- rate: float32 [4, 16, 2048], P('pipe'), may hold values from 0.004 to 0.15
- angle: float32 [4, 16, 2048], P('pipe'), may hold values from -3.140625 to 3.140625
- coef: float32 [4, 2, 16, 2048], P('pipe'), may hold values from -0.3 to 0.3
- skip: float32 [4, 2048], P('pipe'), may hold values from 0.5 to 1.5
- score_gains: float32 [4, 2, 2048], P('pipe'), may hold values from -3 to 4.6
- out_proj: bfloat16 [4, 2048, 2048], P('pipe', 'seq'), may hold values from -0.125 to 0.125
Outputs:
- outputs: bfloat16 [4, 1024, 2048], P('pipe', 'seq')
Inputs may be any that keep to these rules, and one draw needn't show every extreme that they name: Each row of lengths sums to 1024, and every row holds a document of exactly 128 positions. `order`: each packed row appears once.
All inputs are finite; a program needn't handle non-finite values.
Results may differ from a plain program's by a relative error of at most 0.02.
The roundings to bfloat16 on the way count: a program that leaves them out, or rounds other values in their place, can miss the bound.
Values may be sent and summed in bfloat16 or wider, within the bound.
No kernel may reach another device: no remote copies, remote signals or barrier semaphores. Data moves between devices by JAX's collectives and lax.ppermute only.
A program may use at most 128 MiB of HBM per device.

v0:
```python
import functools
import itertools
import math

import jax
import jax.numpy as jnp
import numpy as np
from jax import lax
from jax.experimental import pallas as pl
from jax.experimental.pallas import tpu as pltpu
from jax.sharding import PartitionSpec as P

HEAD_DIM = 128
norm_eps = 1e-06
masked_score = -1e30
lanes = 128
mode_group = 8
chunk_rows = 16
seq_far = 2
head_batch = 8
vector_rows = 4
row_tile = 16


def mixer_tables(rate_now, angle_now, coef_now, skip_now, vectors):
    magnitude = jnp.exp(-rate_now)
    turn_re = magnitude * jnp.cos(angle_now)
    turn_im = magnitude * jnp.sin(angle_now)
    pole_sum = 2.0 * turn_re
    pole_product = -(magnitude * magnitude)
    direct = 2.0 * coef_now[0]
    delayed = -2.0 * (coef_now[0] * turn_re + coef_now[1] * turn_im)
    through = jnp.broadcast_to(skip_now, vectors.shape)
    halves = jnp.stack([
        jnp.concatenate([pole_sum, pole_product, through]),
        jnp.concatenate([direct, delayed, vectors]),
    ])
    return halves.reshape(halves.shape[:2] + (-1, lanes))


def inverse_rms(values):
    return lax.rsqrt(jnp.mean(values * values, axis=1, keepdims=True) + norm_eps)


def fetch(sources, targets, arrived):
    copies = [
        pltpu.make_async_copy(source, target, arrived.at[index])
        for index, (source, target) in enumerate(zip(sources, targets))
    ]
    for copy in copies:
        copy.start()
    return copies


def times(rows, weights):
    return jnp.dot(rows, weights, preferred_element_type=jnp.float32)


def add_projection(place_ref, out_ref, middle_ref, attended_ref, wholes, halves, copies):
    pipe, core = place_ref[0], place_ref[1]
    quarter = wholes.shape[2]

    def put(index, total):
        where = pl.ds(pl.multiple_of(index * quarter, lanes), quarter)
        out_ref[:, where] = (middle_ref[:, where].astype(jnp.float32) + total).astype(jnp.bfloat16)

    for index, hops in zip(range(wholes.shape[0]), (0, 1 + core, 2 - core, 3)):
        copies[index].wait()
        put(pipe ^ hops, times(attended_ref[...], wholes[index]))
    if halves is None:
        return
    half = halves.shape[1]
    total = 0.0
    for index, first in enumerate((core * half, (1 - core) * half)):
        copies[3 + index].wait()
        rows = attended_ref[:, pl.ds(pl.multiple_of(first, lanes), half)]
        total = total + times(rows, halves[index])
    put(pipe ^ 3, total)


def mix_attend(
    keep_ref, broken_ref, doc_col_ref, doc_row_ref, x_ref, pole_ref, zero_ref, middle_ref,
    attended_refs, signal, mixed, queries, keys, with_halo, after_middle, after_half,
):
    rows, width = x_ref.shape
    own = rows // 2
    folds = width // lanes
    modes = (pole_ref.shape[0] - vector_rows) // 2
    heads = width // HEAD_DIM
    tiles = rows // row_tile
    first_chunk = broken_ref[rows // chunk_rows]
    first_tile = first_chunk // (2 * row_tile // chunk_rows) * 2

    def gain(row, fold):
        return zero_ref[2 * modes + row, fold : fold + 1, :]

    def in_pairs(body, first, last):
        def pair(index, carry):
            return body(2 * index + 1, body(2 * index, carry))

        lax.fori_loop(first // 2, last // 2, pair, 0)

    def spread(tile, carry):
        first = pl.multiple_of(tile * row_tile, row_tile)
        plain = x_ref[pl.ds(first, row_tile), :].astype(jnp.float32)
        scaled = plain * inverse_rms(plain)
        for fold in range(folds):
            where = pl.ds(first * folds + fold, row_tile, stride=folds)
            signal[where, :] = scaled[:, fold * lanes : (fold + 1) * lanes] * gain(0, fold)
        return carry

    in_pairs(spread, first_tile, tiles)

    def run_modes(group, opening):
        first_mode = group * mode_group
        coefs = [
            [
                ref[kind * modes + first_mode + index]
                for ref in (pole_ref, zero_ref)
                for kind in range(2)
            ]
            for index in range(mode_group)
        ]
        through = pole_ref[2 * modes] if opening else None

        def advance(chunk, state):
            def steps(state, masked):
                state = list(state)
                for step in range(chunk_rows):
                    row = chunk * chunk_rows + step
                    where = pl.ds(pl.multiple_of(row * folds, folds), folds)
                    entering = signal[where, :]
                    total = through * entering if opening else mixed[where, :]
                    for index in range(mode_group):
                        a1, a2, b0, b1 = coefs[index]
                        newer, older = state[2 * index], state[2 * index + 1]
                        if masked:
                            keep = keep_ref[row]
                            newer, older = newer * keep, older * keep
                        now = (entering + a2 * older) + a1 * newer
                        total = total + (b0 * now + b1 * newer)
                        state[2 * index], state[2 * index + 1] = now, newer
                    mixed[where, :] = total
                return tuple(state)

            return lax.cond(
                broken_ref[chunk] > 0,
                lambda held: steps(held, True),
                lambda held: steps(held, False),
                state,
            )

        zeros = jnp.zeros((folds, lanes), jnp.float32)
        lax.fori_loop(first_chunk, rows // chunk_rows, advance, (zeros,) * (2 * mode_group))

    run_modes(0, True)

    def later_modes(group, carry):
        run_modes(group, False)
        return carry

    lax.fori_loop(1, modes // mode_group, later_modes, 0)

    def gather_back(tile, carry):
        first = pl.multiple_of(tile * row_tile, row_tile)
        where_rows = pl.ds(first, row_tile)
        parts = [
            mixed[pl.ds(first * folds + fold, row_tile, stride=folds), :] for fold in range(folds)
        ]
        plain = x_ref[where_rows, :].astype(jnp.float32)
        middle = (plain + jnp.concatenate(parts, axis=1)).astype(jnp.bfloat16)
        middle_ref[where_rows, :] = middle
        wide = middle.astype(jnp.float32)
        normed = wide * inverse_rms(wide)
        for fold in range(folds):
            part = slice(fold * lanes, (fold + 1) * lanes)
            queries[where_rows, part] = (normed[:, part] * gain(1, fold)).astype(jnp.bfloat16)
            keys[where_rows, part] = (normed[:, part] * gain(2, fold)).astype(jnp.bfloat16)
        return carry

    def clear(tile, carry):
        first = pl.multiple_of(tile * row_tile, row_tile)
        for ref in (middle_ref, queries, keys):
            ref[pl.ds(first, row_tile), :] = jnp.zeros((row_tile, width), jnp.bfloat16)
        return carry

    in_pairs(clear, 0, first_tile)
    in_pairs(gather_back, first_tile, tiles)
    after_middle()

    query_pos = lax.broadcasted_iota(jnp.int32, (own, rows), 0) + own
    key_pos = lax.broadcasted_iota(jnp.int32, (own, rows), 1)
    allowed_own = (key_pos <= query_pos) & (doc_col_ref[own:, :] == doc_row_ref[...])
    allowed_halo = (key_pos[:, :own] <= query_pos[:, :own] - own) & (
        doc_col_ref[:own, :] == doc_row_ref[:, :own]
    )
    rate = HEAD_DIM ** (-0.5) * math.log2(math.e)
    blocks = [(own, rows, allowed_own)]
    if with_halo:
        blocks.insert(0, (0, own, allowed_halo))
    skipped = rows - own * len(blocks)
    for batch in range(0, heads, head_batch):
        jobs = [
            (head, first, count, allowed)
            for head in range(batch, batch + head_batch)
            for first, count, allowed in blocks
        ]
        raws = []
        for head, first, count, allowed in jobs:
            where = slice(head * HEAD_DIM, (head + 1) * HEAD_DIM)
            scores = lax.dot_general(
                queries[first : first + own, where], keys[:count, where], (((1,), (1,)), ((), ())),
                preferred_element_type=jnp.float32,
            )
            raws.append(jnp.where(allowed, scores, masked_score))
        tops = [jnp.max(raw, axis=1, keepdims=True) for raw in raws]
        raws = [jnp.exp2((raw - top) * rate) for raw, top in zip(raws, tops)]
        sums = [jnp.sum(raw, axis=1, keepdims=True) for raw in raws]
        raws = [(raw * (1.0 / total)).astype(jnp.bfloat16) for raw, total in zip(raws, sums)]
        for (head, first, count, _), weights in zip(jobs, raws):
            where = slice(head * HEAD_DIM, (head + 1) * HEAD_DIM)
            part, inner = divmod(head, heads // 2)
            placed = slice(inner * HEAD_DIM, (inner + 1) * HEAD_DIM)
            attended_refs[part][first - skipped : first - skipped + own, placed] = times(
                weights, middle_ref[:count, where]
            ).astype(jnp.bfloat16)
        if (batch + head_batch) % (heads // 2) == 0:
            after_half(batch // (heads // 2))


def section_kernel(wholes_count, halves_count, mixes, with_halo, *refs):
    refs = list(refs)

    def take(count):
        taken, refs[:count] = refs[:count], []
        return taken

    place_ref, = take(1)
    if mixes:
        keep_ref, broken_ref, doc_col_ref, doc_row_ref, tables_ref = take(5)
    sources, weights = take(2), take(wholes_count + halves_count)
    if mixes:
        middle_out, attended_out = take(2)
    else:
        out_ref, = take(1)
    arrived, = take(1)
    if mixes:
        x_ref, pole_ref, zero_ref, middle_ref, low_ref, high_ref, signal, mixed, queries, keys = take(10)
        copies = fetch(
            [tables_ref.at[place_ref[2]], tables_ref.at[place_ref[3]]], [pole_ref, zero_ref],
            arrived.at[pl.ds(10, 2)],
        )
    if weights:
        middle_in, attended_in, wholes = take(3)
        halves = take(1)[0] if halves_count else None
        skipped = sources[0].shape[0] - middle_in.shape[0]
        rows = pl.ds(skipped, middle_in.shape[0])
        inputs = fetch([source.at[rows] for source in sources], [middle_in, attended_in], arrived)
        targets = [wholes.at[index] for index in range(wholes_count)]
        targets += [halves.at[index] for index in range(halves_count)]
        pieces = fetch(weights, targets, arrived.at[pl.ds(2, 5)])
        for copy in inputs:
            copy.wait()
        target = x_ref if mixes else out_ref
        add_projection(place_ref, target, middle_in, attended_in, wholes, halves, pieces)
    else:
        own = x_ref.shape[0] // 2
        inputs = fetch(sources, [x_ref.at[pl.ds(0, own)], x_ref.at[pl.ds(own, own)]], arrived)
        for copy in inputs:
            copy.wait()
    if not mixes:
        return
    for copy in copies:
        copy.wait()
    skipped = middle_ref.shape[0] - middle_out.shape[0]
    half = low_ref.shape[1]
    results = [
        pltpu.make_async_copy(
            middle_ref.at[pl.ds(skipped, middle_out.shape[0])], middle_out, arrived.at[7]
        )
    ] + [
        pltpu.make_async_copy(
            ref, attended_out.at[:, pl.ds(index * half, half)], arrived.at[8 + index]
        )
        for index, ref in enumerate((low_ref, high_ref))
    ]
    mix_attend(
        keep_ref, broken_ref, doc_col_ref, doc_row_ref, x_ref, pole_ref, zero_ref, middle_ref,
        (low_ref, high_ref), signal, mixed, queries, keys, with_halo,
        results[0].start, lambda part: results[1 + part].start(),
    )
    for copy in results:
        copy.wait()


def section_step(place, sources, weights=(), mixing=(), with_halo=True):
    width = sources[0].shape[1]
    smem, vmem, anywhere = (
        pl.BlockSpec(memory_space=space) for space in (pltpu.SMEM, pltpu.VMEM, pltpu.HBM)
    )
    rows = sources[0].shape[0] if weights else 2 * sources[0].shape[0]
    folds = width // lanes
    wholes_count = sum(weight.shape[0] == width for weight in weights)
    halves_count = len(weights) - wholes_count
    scratch = [pltpu.SemaphoreType.DMA((12,))]
    if mixing:
        kept = rows if with_halo else rows // 2
        wide = pltpu.VMEM((rows * folds, lanes), jnp.float32)
        narrow = pltpu.VMEM((rows, width), jnp.bfloat16)
        half = pltpu.VMEM((kept, width // 2), jnp.bfloat16)
        table = pltpu.VMEM(mixing[-1].shape[1:], jnp.float32)
        scratch += [narrow, table, table, narrow, half, half, wide, wide, narrow, narrow]
        out_shape = [jax.ShapeDtypeStruct((kept, width), jnp.bfloat16)] * 2
        out_specs = [anywhere, anywhere]
    else:
        kept = rows
        out_shape = jax.ShapeDtypeStruct((rows, width), jnp.bfloat16)
        out_specs = vmem
    if weights:
        held = pltpu.VMEM((rows, width), jnp.bfloat16)
        scratch += [
            held, held,
            pltpu.VMEM((wholes_count,) + weights[0].shape, jnp.bfloat16),
        ]
        if halves_count:
            scratch.append(pltpu.VMEM((halves_count,) + weights[-1].shape, jnp.bfloat16))
    return pl.pallas_call(
        functools.partial(section_kernel, wholes_count, halves_count, bool(mixing), with_halo),
        out_shape=out_shape,
        in_specs=[smem]
        + ([smem, smem, vmem, vmem, anywhere] if mixing else [])
        + [anywhere] * (len(sources) + len(weights)),
        out_specs=out_specs,
        scratch_shapes=scratch,
        compiler_params=pltpu.CompilerParams(vmem_limit_bytes=60 << 20),
        cost_estimate=pl.CostEstimate(
            flops=2 * rows * width * width, bytes_accessed=2 * width * width, transcendentals=0
        ),
        name="section_step",
    )(place, *mixing, *sources, *weights)


def half_copy_kernel(place_ref, value_ref, out_ref, held, arrived, left):
    half = out_ref.shape[0]
    part = half // 4
    parts = [pl.ds(index * part, part) for index in range(4)]
    starts = [place_ref[1] * half + index * part for index in range(4)]
    sources = [value_ref.at[pl.ds(first, part)] for first in starts]
    coming = fetch(sources, [held.at[where] for where in parts], arrived)
    going = []
    for index, where in enumerate(parts):
        coming[index].wait()
        going.append(pltpu.make_async_copy(held.at[where], out_ref.at[where], left.at[index]))
        going[-1].start()
    for copy in going:
        copy.wait()


def core_half(value, place):
    hbm = pl.BlockSpec(memory_space=pltpu.HBM)
    shape = (value.shape[0] // 2,) + value.shape[1:]
    return pl.pallas_call(
        half_copy_kernel,
        out_shape=jax.ShapeDtypeStruct(shape, value.dtype),
        in_specs=[pl.BlockSpec(memory_space=pltpu.SMEM), hbm],
        out_specs=hbm,
        scratch_shapes=[pltpu.VMEM(shape, value.dtype)] + [pltpu.SemaphoreType.DMA((4,))] * 2,
        compiler_params=pltpu.CompilerParams(vmem_limit_bytes=60 << 20),
        name="core_half",
    )(place, value)


def document_flags(docs):
    goes_on = jnp.concatenate([jnp.zeros((1,), bool), docs[1:] == docs[:-1]])
    broken = jnp.any(jnp.logical_not(goes_on).reshape(-1, chunk_rows), axis=1)
    needed = docs == docs[docs.shape[0] // 2]
    first_chunk = jnp.argmax(needed) // chunk_rows
    flags = jnp.concatenate([broken.astype(jnp.int32), first_chunk.astype(jnp.int32)[None]])
    return goes_on.astype(jnp.float32), flags


def across(value, hops):
    count = lax.axis_size("pipe")
    return lax.ppermute(value, "pipe", [(i, i ^ hops) for i in range(count)])


def swapped(value):
    count = lax.axis_size("seq")
    return lax.ppermute(value, "seq", [(i, i ^ 1) for i in range(count)])


def spread_quarters(shard, offset, first):
    section_count = lax.axis_size("pipe")
    pipe_index = lax.axis_index("pipe")
    quarter = shard.shape[1] // section_count

    def columns(hops):
        return lax.dynamic_slice_in_dim(shard, (pipe_index ^ hops ^ offset) * quarter, quarter, 1)

    held = [columns(0)]
    for hops in range(1, section_count):
        pairs = [(i, i ^ hops) for i in range(first, section_count)]
        held.append(lax.ppermute(columns(hops), "pipe", pairs))
    held = jnp.stack(held)
    return {
        section: lax.dynamic_index_in_dim(held, pipe_index ^ section, 0, False)
        for section in range(first, section_count)
    }


def own_half(halves):
    return lax.dynamic_index_in_dim(halves, lax.axis_index("seq") % 2, 0, False)


def joined_tables(halves, fetched):
    fetched = jnp.stack(fetched)
    other = swapped(fetched)
    own = jnp.where(lax.axis_index("seq") % 2 == 0, halves, halves[::-1])
    return jnp.concatenate([own, jnp.stack([fetched, other], axis=1).reshape((-1,) + own.shape[1:])])


def sent_by_core(value, hops_by_core):
    pipe_count, seq_count = lax.axis_size("pipe"), lax.axis_size("seq")
    pairs = [
        (pipe * seq_count + seq, (pipe ^ hops_by_core[seq % 2]) * seq_count + seq)
        for pipe in range(pipe_count)
        for seq in range(seq_count)
    ]
    return lax.ppermute(value, ("pipe", "seq"), pairs)


def passed_on(fetched, place):
    return sent_by_core(core_half(fetched, place), (2, 1))


def permuted_rows(value, order):
    count = lax.axis_size("pipe")
    choices = list(itertools.permutations(range(count)))
    match = jnp.all(jnp.asarray(np.array(choices, np.int32)) == order[None, :], axis=1)
    which = jnp.argmax(match).astype(jnp.int32)

    def mover(choice):
        pairs = [(source, target) for target, source in enumerate(choice)]
        return lambda held: lax.ppermute(held, "pipe", pairs)

    return lax.switch(which, [mover(choice) for choice in choices], value)


def local(inputs, lengths, order, norm_gain, rate, angle, coef, skip, score_gains, out_proj):
    section_count = lax.axis_size("pipe")
    seq_count = lax.axis_size("seq")
    pipe_index = lax.axis_index("pipe")
    seq_index = lax.axis_index("seq")
    row_count = inputs.shape[1]

    place = jnp.stack([pipe_index, seq_index % 2]).astype(jnp.int32)
    vectors = jnp.concatenate([norm_gain, score_gains[0], skip])
    halves = mixer_tables(rate[0], angle[0], coef[0], skip[0], vectors)

    tie = lax.optimization_barrier
    quarters = spread_quarters(out_proj[0], 0, 0)
    own = permuted_rows(inputs[0], order)
    held = (quarters, halves, own, out_proj[0])
    quarters, halves, own, shard = tie(held)

    def along_seq(quarters):
        return {
            section: lax.all_gather(quarter, "seq", axis=0, tiled=True)
            for section, quarter in quarters.items()
        }

    wholes = along_seq(quarters)
    fetched = [across(own_half(halves), hops) for hops in range(1, section_count)]
    last_quarters = spread_quarters(shard, 3, seq_far)
    before = lax.ppermute(own, "seq", [(i, i + 1) for i in range(seq_count - 1)])

    positions = (seq_index - 1) * row_count + jnp.arange(2 * row_count)
    chosen = lax.dynamic_index_in_dim(order, pipe_index, 0, False)
    doc_ends = jnp.cumsum(lax.dynamic_index_in_dim(lengths, chosen, 0, False))
    counted = jnp.sum((doc_ends[None, :] <= positions[:, None]).astype(jnp.int32), axis=1)
    docs = jnp.where(positions >= 0, counted, -1)
    keep, flags = document_flags(docs)

    def hop(section):
        return sent_by_core(wholes[section], (1, 2))

    def mixing(section):
        hops = 2 * (pipe_index ^ section)
        which = jnp.stack([hops + place[1], hops + 1 - place[1]])
        return jnp.concatenate([place, which]), (keep, flags, docs[:, None], docs[None, :], tables)

    near, far = {}, {}
    held = (fetched, before, last_quarters, wholes[0])
    fetched, before, last_quarters, wholes[0] = tie(held)
    near[0] = hop(0)
    tables = joined_tables(halves, fetched)
    where, mixer = mixing(0)
    middle, attended = section_step(where, (before, own), mixing=mixer)
    held = (near[0], middle, attended, wholes[1], last_quarters)
    near[0], middle, attended, wholes[1], last_quarters = tie(held)
    last_quarters = along_seq(last_quarters)
    far[0] = passed_on(near[0], place)
    near[1] = hop(1)
    for section in range(section_count):
        weights = [wholes[section], near[section], swapped(near[section])]
        if section < seq_far:
            far[section], middle, attended = tie((far[section], middle, attended))
            weights += [far[section], swapped(far[section])]
        else:
            weights += [last_quarters[section]]
        if section + 2 < section_count:
            wholes[section + 2], middle, attended = tie((wholes[section + 2], middle, attended))
            near[section + 2] = hop(section + 2)
        if section + 1 < section_count:
            near[section + 1], middle, attended = tie((near[section + 1], middle, attended))
            if section + 1 < seq_far:
                far[section + 1] = passed_on(near[section + 1], place)
            where, mixer = mixing(section + 1)
            with_halo = section + 2 < section_count
            middle, attended = section_step(where, (middle, attended), weights, mixer, with_halo)
    x = section_step(place, (middle, attended), weights)
    return x[None]


def solution(mesh):
    in_specs = (
        P("pipe", "seq", None),
        P(),
        P(),
        P("pipe", None),
        P("pipe", None, None),
        P("pipe", None, None),
        P("pipe", None, None, None),
        P("pipe", None),
        P("pipe", None, None),
        P("pipe", "seq", None),
    )
    out_specs = P("pipe", "seq", None)
    return jax.shard_map(local, mesh=mesh, in_specs=in_specs, out_specs=out_specs, check_vma=False)
```

profile of v0, /device:TPU:24, one launch (start us, length us, event | category | flops | bytes accessed | tf_op | source)
XLA Modules:
  0.0 230.3 jit_solution(11277615572821251449)
XLA Ops:
  6.6 1.4 constant_dynamic-slice_fusion.3
  8.0 1.6 collective-permute-start.24
  9.6 1.5 collective-permute-start.25
  11.1 3.9 %collective-permute-start.26 = (bf16[256,512]{1,0:T(8,128)(2,1)S(1)}, bf16[256,512]{1,0:T(8,128)(2,1)S(1)}, u32[]{:S(2)}, u32[]{:S(2)}) collective-permute-start(bf16[256,512]{1,0:T(8,128)(2,1)S(1)} %get-tuple-element.171), channel_id=1, source_target_pairs={{0,24},{8,16},{16,8},{24,0},{1,25},{9,17},{17,9},{25,1},{2,26},{10... | collective-permute-start | bytes 786440 | tf_op jit(solution)/shard_map/ppermute | solution.py:403
  15.1 0.5 multiply_bitcast_fusion.1
  15.9 0.7 iota_reduce_fusion
  17.2 1.5 conditional.1
  17.2 1.5 collective-permute-start.2
  18.7 5.3 %collective-permute-done.26 = bf16[256,512]{1,0:T(8,128)(2,1)S(1)} collective-permute-done((bf16[256,512]{1,0:T(8,128)(2,1)S(1)}, bf16[256,512]{1,0:T(8,128)(2,1)S(1)}, u32[]{:S(2)}, u32[]{:S(2)}) %collective-permute-start.26) | collective-permute-done | bytes 262176 | tf_op jit(solution)/shard_map/ppermute | solution.py:403
  24.2 1.0 dynamic-slice_bitcast_fusion.4
  25.3 0.7 all-gather.11.cloned.1.call-update
  26.0 0.7 all-gather.13.cloned.1.call-update
  26.8 0.5 all-gather.9.cloned.1.call-update
  27.4 0.6 dynamic_slice.63
  30.4 0.7 collective-permute-start.31
  31.1 1.3 collective-permute-start.32
  32.4 0.5 slice.20
  33.0 1.3 collective-permute-start.33
  34.2 1.9 collective-permute-start.30
  36.2 12.1 %collective-permute-start.27 = (f32[36,16,128]{2,1,0:T(8,128)S(1)}, f32[36,16,128]{2,1,0:T(8,128)S(1)}, u32[]{:S(2)}, u32[]{:S(2)}) collective-permute-start(f32[36,16,128]{2,1,0:T(8,128)S(1)} %dynamic-slice_bitcast_fusion), channel_id=1, source_target_pairs={{0,8},{8,0},{16,24},{24,16},{1,9},{9,1},{17,25},{25,17},{2,10},{10... | collective-permute-start | bytes 884744 | tf_op jit(solution)/shard_map/ppermute | solution.py:384
  48.3 5.3 %collective-permute-start.28 = (f32[36,16,128]{2,1,0:T(8,128)S(1)}, f32[36,16,128]{2,1,0:T(8,128)S(1)}, u32[]{:S(2)}, u32[]{:S(2)}) collective-permute-start(f32[36,16,128]{2,1,0:T(8,128)S(1)} %dynamic-slice_bitcast_fusion), channel_id=1, source_target_pairs={{0,16},{8,24},{16,0},{24,8},{1,17},{9,25},{17,1},{25,9},{2,18},{10... | collective-permute-start | bytes 884744 | tf_op jit(solution)/shard_map/ppermute | solution.py:384
  53.5 3.6 %collective-permute-done.32 = bf16[256,512]{1,0:T(8,128)(2,1)} collective-permute-done((bf16[256,512]{1,0:T(8,128)(2,1)S(1)}, bf16[256,512]{1,0:T(8,128)(2,1)}, u32[]{:S(2)}, u32[]{:S(2)}) %collective-permute-start.32) | collective-permute-done | bytes 262176 | tf_op jit(solution)/shard_map/ppermute | solution.py:403
  57.1 2.3 %collective-permute-start.29 = (f32[36,16,128]{2,1,0:T(8,128)S(1)}, f32[36,16,128]{2,1,0:T(8,128)S(1)}, u32[]{:S(2)}, u32[]{:S(2)}) collective-permute-start(f32[36,16,128]{2,1,0:T(8,128)S(1)} %dynamic-slice_bitcast_fusion), channel_id=1, source_target_pairs={{0,24},{8,16},{16,8},{24,0},{1,25},{9,17},{17,9},{25,1},{2,26},{10... | collective-permute-start | bytes 884744 | tf_op jit(solution)/shard_map/ppermute | solution.py:384
  59.4 1.4 compare_reduce_fusion.1
  63.4 1.2 pad_maximum_fusion.3
  64.6 0.8 dynamic-slice_bitcast_fusion.1
  65.4 4.6 %collective-permute-done.29 = f32[36,16,128]{2,1,0:T(8,128)S(1)} collective-permute-done((f32[36,16,128]{2,1,0:T(8,128)S(1)}, f32[36,16,128]{2,1,0:T(8,128)S(1)}, u32[]{:S(2)}, u32[]{:S(2)}) %collective-permute-start.29) | collective-permute-done | bytes 294944 | tf_op jit(solution)/shard_map/ppermute | solution.py:384
  70.0 0.7 copy-done.7
  70.7 1.7 collective-permute-start.35
  72.5 0.7 fusion.6
  73.4 0.1 copy.18
  73.6 0.7 pad_add_fusion.4.refs_2_
  74.2 0.6 pad_add_fusion.7
  74.8 1.1 fusion.8
  76.0 0.6 compare_select_fusion.refs_4_
  76.5 0.7 pad_add_fusion.6
  77.2 0.7 fusion.4.refs_3_
  77.9 0.5 collective-permute-done.34
  78.5 1.7 pad_maximum_fusion.refs_5_
  80.2 14.3 %section_step.5 = (bf16[256,2048]{1,0:T(8,128)(2,1)}, bf16[256,2048]{1,0:T(8,128)(2,1)}) custom-call(s32[4]{0:T(128)} %get-tuple-element.182.refs_0_, f32[256]{0:T(256)} %get-tuple-element.185.refs_1_, s32[17]{0:T(128)} %pad_add_fusion.4.refs_2_, s32[256,1]{1,0:T(8,128)} %fusion.4.refs_3_, s32[1,256]{1,0:T(1,128)} %compare_select_fusion.refs_4_, ...), custom_call_target="tpu_custom_call" | custom-call | flops 2147483648 | bytes 8388608 | tf_op jit(solution)/shard_map/section_step/pallas_call | solution.py:327
  94.4 2.7 %all-gather.11.cloned.1.call-done.refs_8_ = bf16[2048,512]{1,0:T(8,128)(2,1)} async-done(((bf16[256,512]{1,0:T(8,128)(2,1)}), bf16[2048,512]{1,0:T(8,128)(2,1)}) %all-gather.11.cloned.1.call-update) | async-done | bytes 2097168 | tf_op jit(solution)/shard_map/all_gather | solution.py:468
  97.1 2.5 %collective-permute-start.36 = (bf16[2048,512]{1,0:T(8,128)(2,1)}, bf16[2048,512]{1,0:T(8,128)(2,1)}, u32[]{:S(2)}, u32[]{:S(2)}) collective-permute-start(bf16[2048,512]{1,0:T(8,128)(2,1)} %all-gather.11.cloned.1.call-done.refs_8_), channel_id=1, source_target_pairs={{0,8},{1,17},{2,10},{3,19},{4,12},{5,21},{6,14},{7,23},{8,0},{9,25... | collective-permute-start | bytes 6291464 | tf_op jit(solution)/shard_map/ppermute | solution.py:429
  99.7 0.2 all-gather.17.cloned.1.call-start
  99.9 0.6 pad_add_fusion.1.place_ref.refs_0_
  100.5 2.7 %core_half.2 = bf16[1024,512]{1,0:T(8,128)(2,1)} custom-call(s32[2]{0:T(128)} %pad_add_fusion.1.place_ref.refs_0_, bf16[2048,512]{1,0:T(8,128)(2,1)} %copy-done.1), custom_call_target="tpu_custom_call" | custom-call | tf_op jit(solution)/shard_map/core_half/pallas_call | solution.py:362
  103.2 0.5 collective-permute-start.37
  103.6 26.0 %collective-permute-done.37.refs_11_ = bf16[1024,512]{1,0:T(8,128)(2,1)} collective-permute-done((bf16[1024,512]{1,0:T(8,128)(2,1)}, bf16[1024,512]{1,0:T(8,128)(2,1)}, u32[]{:S(2)}, u32[]{:S(2)}) %collective-permute-start.37) | collective-permute-done | bytes 1048608 | tf_op jit(solution)/shard_map/ppermute | solution.py:429
  129.7 5.6 %collective-permute-done.36.value_ref.refs_9_ = bf16[2048,512]{1,0:T(8,128)(2,1)} collective-permute-done((bf16[2048,512]{1,0:T(8,128)(2,1)}, bf16[2048,512]{1,0:T(8,128)(2,1)}, u32[]{:S(2)}, u32[]{:S(2)}) %collective-permute-start.36) | collective-permute-done | bytes 2097184 | tf_op jit(solution)/shard_map/ppermute | solution.py:429
  135.2 2.7 %core_half.3 = bf16[1024,512]{1,0:T(8,128)(2,1)} custom-call(s32[2]{0:T(128)} %pad_add_fusion.1.place_ref.refs_0_, bf16[2048,512]{1,0:T(8,128)(2,1)} %collective-permute-done.36.value_ref.refs_9_), custom_call_target="tpu_custom_call" | custom-call | tf_op jit(solution)/shard_map/core_half/pallas_call | solution.py:362
  137.9 1.0 collective-permute-start.38
  138.9 1.5 collective-permute-start.42
  140.4 1.3 copy-done.4
  141.7 18.3 %section_step.6 = (bf16[256,2048]{1,0:T(8,128)(2,1)}, bf16[256,2048]{1,0:T(8,128)(2,1)}) custom-call(s32[4]{0:T(128)} %get-tuple-element.181.refs_0_, f32[256]{0:T(256)} %get-tuple-element.185.refs_1_, s32[17]{0:T(128)} %pad_add_fusion.4.refs_2_, s32[256,1]{1,0:T(8,128)} %fusion.4.refs_3_, s32[1,256]{1,0:T(1,128)} %compare_select_fusion.refs_4_, ...), custom_call_target="tpu_custom_call" | custom-call | flops 2147483648 | bytes 8388608 | tf_op jit(solution)/shard_map/section_step/pallas_call | solution.py:327
  160.1 4.1 %collective-permute-done.38.refs_11_ = bf16[1024,512]{1,0:T(8,128)(2,1)S(1)} collective-permute-done((bf16[1024,512]{1,0:T(8,128)(2,1)}, bf16[1024,512]{1,0:T(8,128)(2,1)S(1)}, u32[]{:S(2)}, u32[]{:S(2)}) %collective-permute-start.38) | collective-permute-done | bytes 1048608 | tf_op jit(solution)/shard_map/ppermute | solution.py:429
  164.2 2.1 collective-permute-start.41
  166.4 7.1 %collective-permute-done.42.refs_9_ = bf16[2048,512]{1,0:T(8,128)(2,1)} collective-permute-done((bf16[2048,512]{1,0:T(8,128)(2,1)}, bf16[2048,512]{1,0:T(8,128)(2,1)}, u32[]{:S(2)}, u32[]{:S(2)}) %collective-permute-start.42) | collective-permute-done | bytes 2097184 | tf_op jit(solution)/shard_map/ppermute | solution.py:429
  173.5 1.3 collective-permute-start.45
  174.7 1.1 copy-done.6
  175.8 18.5 %section_step.7 = (bf16[256,2048]{1,0:T(8,128)(2,1)}, bf16[256,2048]{1,0:T(8,128)(2,1)}) custom-call(s32[4]{0:T(128)} %get-tuple-element.156.refs_0_, f32[256]{0:T(256)} %get-tuple-element.185.refs_1_, s32[17]{0:T(128)} %pad_add_fusion.4.refs_2_, s32[256,1]{1,0:T(8,128)} %fusion.4.refs_3_, s32[1,256]{1,0:T(1,128)} %compare_select_fusion.refs_4_, ...), custom_call_target="tpu_custom_call" | custom-call | flops 2147483648 | bytes 8388608 | tf_op jit(solution)/shard_map/section_step/pallas_call | solution.py:327
  194.3 1.5 collective-permute-done.41.refs_4_
  195.8 1.0 collective-permute-start.46
  196.8 17.5 %section_step.8 = (bf16[128,2048]{1,0:T(8,128)(2,1)}, bf16[128,2048]{1,0:T(8,128)(2,1)}) custom-call(s32[4]{0:T(128)} %get-tuple-element.183.refs_0_, f32[256]{0:T(256)} %get-tuple-element.185.refs_1_, s32[17]{0:T(128)} %pad_add_fusion.4.refs_2_, s32[256,1]{1,0:T(8,128)} %fusion.4.refs_3_, s32[1,256]{1,0:T(1,128)} %compare_select_fusion.refs_4_, ...), custom_call_target="tpu_custom_call" | custom-call | flops 2147483648 | bytes 8388608 | tf_op jit(solution)/shard_map/section_step/pallas_call | solution.py:327
  214.3 3.3 %all-gather.17.cloned.1.call-done.refs_6_ = bf16[2048,512]{1,0:T(8,128)(2,1)} async-done(((bf16[256,512]{1,0:T(8,128)(2,1)}), bf16[2048,512]{1,0:T(8,128)(2,1)}) %all-gather.17.cloned.1.call-update) | async-done | bytes 2097168 | tf_op jit(solution)/shard_map/all_gather | solution.py:468
  217.6 5.8 %section_step.9 = bf16[128,2048]{1,0:T(8,128)(2,1)} custom-call(s32[2]{0:T(128)} %pad_add_fusion.1.place_ref.refs_0_, bf16[128,2048]{1,0:T(8,128)(2,1)} %get-tuple-element.152.refs_1_, bf16[128,2048]{1,0:T(8,128)(2,1)} %get-tuple-element.153.refs_2_, bf16[2048,512]{1,0:T(8,128)(2,1)} %all-gather.9.cloned.1.call-done.refs_3_, bf16[2048,512]{1,0:T(8,128)(2,1)} %copy-done.3, ...), custom_call_target="tpu_custom_call" | custom-call | flops 1073741824 | bytes 8388608 | tf_op jit(solution)/shard_map/section_step/pallas_call | solution.py:327
  (93 shorter events, 1.9 us)
Async XLA Ops:
  6.5 23.4 %copy-start = (s32[4,32]{1,0:T(4,128)S(1)}, s32[4,32]{1,0:T(4,128)}, u32[]{:S(2)}) copy-start(s32[4,32]{1,0:T(4,128)} %param.36) | copy-start | bytes 1540
  6.5 8.5 %copy-start.8 = (f32[1,2,16,2048]{3,2,1,0:T(8,128)S(1)}, f32[1,2,16,2048]{3,2,1,0:T(8,128)}, u32[]{:S(2)}) copy-start(f32[1,2,16,2048]{3,2,1,0:T(8,128)} %param.41) | copy-start | bytes 786436
  6.5 8.5 %copy-start.10 = (f32[1,16,2048]{2,1,0:T(8,128)S(1)}, f32[1,16,2048]{2,1,0:T(8,128)}, u32[]{:S(2)}) copy-start(f32[1,16,2048]{2,1,0:T(8,128)} %param.39) | copy-start | bytes 393220
  6.5 8.5 %copy-start.9 = (f32[1,16,2048]{2,1,0:T(8,128)S(1)}, f32[1,16,2048]{2,1,0:T(8,128)}, u32[]{:S(2)}) copy-start(f32[1,16,2048]{2,1,0:T(8,128)} %param.40) | copy-start | bytes 393220
  6.5 63.5 %all-gather.7.cloned.1.call-start = ((), (), s32[]{:S(2)}) async-start(), calls=%async_computation | async-start | bytes 2359296 | tf_op jit(solution)/shard_map/all_gather | solution.py:468
  8.0 7.8 %copy-start.13 = (f32[1,2048]{1,0:T(1,128)S(1)}, f32[1,2048]{1,0:T(1,128)}, u32[]{:S(2)}) copy-start(f32[1,2048]{1,0:T(1,128)} %param.38) | copy-start | bytes 24580
  8.0 7.8 %copy-start.12 = (f32[1,2,2048]{2,1,0:T(2,128)S(1)}, f32[1,2,2048]{2,1,0:T(2,128)}, u32[]{:S(2)}) copy-start(f32[1,2,2048]{2,1,0:T(2,128)} %param.43) | copy-start | bytes 49156
  8.0 7.8 %copy-start.14 = (s32[24,4]{0,1:T(4,128)S(1)}, s32[24,4]{0,1:T(4,128)}, u32[]{:S(2)}) copy-start(s32[24,4]{0,1:T(4,128)} %constant.115.clone) | copy-start | bytes 1156
  8.0 7.8 %copy-start.15 = (s32[4]{0:T(128)S(1)}, s32[4]{0:T(128)}, u32[]{:S(2)}) copy-start(s32[4]{0:T(128)} %param.37) | copy-start | bytes 52
  8.0 9.1 %copy-start.16 = (bf16[1,128,2048]{2,1,0:T(8,128)(2,1)S(1)}, bf16[1,128,2048]{2,1,0:T(8,128)(2,1)}, u32[]{:S(2)}) copy-start(bf16[1,128,2048]{2,1,0:T(8,128)(2,1)} %param.35) | copy-start | bytes 1572868
  8.0 10.6 %copy-start.11 = (f32[1,2048]{1,0:T(1,128)S(1)}, f32[1,2048]{1,0:T(1,128)}, u32[]{:S(2)}) copy-start(f32[1,2048]{1,0:T(1,128)} %param.42) | copy-start | bytes 24580
  8.0 10.7 %collective-permute-start.24 = (bf16[256,512]{1,0:T(8,128)(2,1)S(1)}, bf16[256,512]{1,0:T(8,128)(2,1)S(1)}, u32[]{:S(2)}, u32[]{:S(2)}) collective-permute-start(bf16[256,512]{1,0:T(8,128)(2,1)S(1)} %get-tuple-element.170), channel_id=1, source_target_pairs={{0,8},{8,0},{16,24},{24,16},{1,9},{9,1},{17,25},{25,17},{2,10},{10... | collective-permute-start | bytes 786440 | tf_op jit(solution)/shard_map/ppermute | solution.py:403
  9.6 9.1 %collective-permute-start.25 = (bf16[256,512]{1,0:T(8,128)(2,1)S(1)}, bf16[256,512]{1,0:T(8,128)(2,1)S(1)}, u32[]{:S(2)}, u32[]{:S(2)}) collective-permute-start(bf16[256,512]{1,0:T(8,128)(2,1)S(1)} %get-tuple-element.169), channel_id=1, source_target_pairs={{0,16},{8,24},{16,0},{24,8},{1,17},{9,25},{17,1},{25,9},{2,18},{10... | collective-permute-start | bytes 786440 | tf_op jit(solution)/shard_map/ppermute | solution.py:403
  11.1 12.9 %collective-permute-start.26 = (bf16[256,512]{1,0:T(8,128)(2,1)S(1)}, bf16[256,512]{1,0:T(8,128)(2,1)S(1)}, u32[]{:S(2)}, u32[]{:S(2)}) collective-permute-start(bf16[256,512]{1,0:T(8,128)(2,1)S(1)} %get-tuple-element.171), channel_id=1, source_target_pairs={{0,24},{8,16},{16,8},{24,0},{1,25},{9,17},{17,9},{25,1},{2,26},{10... | collective-permute-start | bytes 786440 | tf_op jit(solution)/shard_map/ppermute | solution.py:403
  17.2 1.5 collective-permute-start.2
  24.2 6.2 %copy-start.2 = (bf16[1,256,2048]{2,1,0:T(8,128)(2,1)S(1)}, bf16[1,256,2048]{2,1,0:T(8,128)(2,1)}, u32[]{:S(2)}) copy-start(bf16[1,256,2048]{2,1,0:T(8,128)(2,1)} %param.44) | copy-start | bytes 3145732
  25.2 71.9 %all-gather.11.cloned.1.call-start = ((), (), s32[]{:S(2)}) async-start(), calls=%async_computation.2 | async-start | bytes 2359296 | tf_op jit(solution)/shard_map/all_gather | solution.py:468
  26.0 103.7 %all-gather.13.cloned.1.call-start = ((), (), s32[]{:S(2)}) async-start(), calls=%async_computation.3 | async-start | bytes 2359296 | tf_op jit(solution)/shard_map/all_gather | solution.py:468
  26.7 137.5 %all-gather.9.cloned.1.call-start = ((), (), s32[]{:S(2)}) async-start(), calls=%async_computation.1 | async-start | bytes 2359296 | tf_op jit(solution)/shard_map/all_gather | solution.py:468
  27.3 169.5 %all-gather.15.cloned.1.call-start = ((), (), s32[]{:S(2)}) async-start(), calls=%async_computation.4 | async-start | bytes 2359296 | tf_op jit(solution)/shard_map/all_gather | solution.py:468
  30.4 17.8 %collective-permute-start.31 = (bf16[256,512]{1,0:T(8,128)(2,1)S(1)}, bf16[256,512]{1,0:T(8,128)(2,1)S(1)}, u32[]{:S(2)}, u32[]{:S(2)}) collective-permute-start(bf16[256,512]{1,0:T(8,128)(2,1)S(1)} %get-tuple-element.163), channel_id=1, source_target_pairs={{16,24},{24,16},{17,25},{25,17},{18,26},{26,18},{19,27},{27,19},{2... | collective-permute-start | bytes 786440 | tf_op jit(solution)/shard_map/ppermute | solution.py:403
  31.1 26.0 %collective-permute-start.32 = (bf16[256,512]{1,0:T(8,128)(2,1)S(1)}, bf16[256,512]{1,0:T(8,128)(2,1)}, u32[]{:S(2)}, u32[]{:S(2)}) collective-permute-start(bf16[256,512]{1,0:T(8,128)(2,1)S(1)} %get-tuple-element.162), channel_id=1, source_target_pairs={{16,0},{24,8},{17,1},{25,9},{18,2},{26,10},{19,3},{27,11},{20,4},{... | collective-permute-start | bytes 786440 | tf_op jit(solution)/shard_map/ppermute | solution.py:403
  33.0 30.4 %collective-permute-start.33 = (bf16[256,512]{1,0:T(8,128)(2,1)S(1)}, bf16[256,512]{1,0:T(8,128)(2,1)}, u32[]{:S(2)}, u32[]{:S(2)}) collective-permute-start(bf16[256,512]{1,0:T(8,128)(2,1)S(1)} %get-tuple-element.161), channel_id=1, source_target_pairs={{16,8},{24,0},{17,9},{25,1},{18,10},{26,2},{19,11},{27,3},{20,12},... | collective-permute-start | bytes 786440 | tf_op jit(solution)/shard_map/ppermute | solution.py:403
  34.2 35.8 %collective-permute-start.30 = (bf16[128,2048]{1,0:T(8,128)(2,1)}, bf16[128,2048]{1,0:T(8,128)(2,1)}, u32[]{:S(2)}, u32[]{:S(2)}) collective-permute-start(bf16[128,2048]{1,0:T(8,128)(2,1)} %get-tuple-element.186.refs_7_), channel_id=1, source_target_pairs={{0,1},{1,2},{2,3},{3,4},{4,5},{5,6},{6,7},{8,9},{9,10},{10,11},{11... | collective-permute-start | bytes 1572872 | tf_op jit(solution)/shard_map/ppermute | solution.py:475
  36.2 29.2 %collective-permute-start.27 = (f32[36,16,128]{2,1,0:T(8,128)S(1)}, f32[36,16,128]{2,1,0:T(8,128)S(1)}, u32[]{:S(2)}, u32[]{:S(2)}) collective-permute-start(f32[36,16,128]{2,1,0:T(8,128)S(1)} %dynamic-slice_bitcast_fusion), channel_id=1, source_target_pairs={{0,8},{8,0},{16,24},{24,16},{1,9},{9,1},{17,25},{25,17},{2,10},{10... | collective-permute-start | bytes 884744 | tf_op jit(solution)/shard_map/ppermute | solution.py:384
  48.3 17.1 %collective-permute-start.28 = (f32[36,16,128]{2,1,0:T(8,128)S(1)}, f32[36,16,128]{2,1,0:T(8,128)S(1)}, u32[]{:S(2)}, u32[]{:S(2)}) collective-permute-start(f32[36,16,128]{2,1,0:T(8,128)S(1)} %dynamic-slice_bitcast_fusion), channel_id=1, source_target_pairs={{0,16},{8,24},{16,0},{24,8},{1,17},{9,25},{17,1},{25,9},{2,18},{10... | collective-permute-start | bytes 884744 | tf_op jit(solution)/shard_map/ppermute | solution.py:384
  57.1 12.9 %collective-permute-start.29 = (f32[36,16,128]{2,1,0:T(8,128)S(1)}, f32[36,16,128]{2,1,0:T(8,128)S(1)}, u32[]{:S(2)}, u32[]{:S(2)}) collective-permute-start(f32[36,16,128]{2,1,0:T(8,128)S(1)} %dynamic-slice_bitcast_fusion), channel_id=1, source_target_pairs={{0,24},{8,16},{16,8},{24,0},{1,25},{9,17},{17,9},{25,1},{2,26},{10... | collective-permute-start | bytes 884744 | tf_op jit(solution)/shard_map/ppermute | solution.py:384
  70.0 0.7 copy-start.7
  70.7 26.4 %collective-permute-start.35 = (bf16[2048,512]{1,0:T(8,128)(2,1)}, bf16[2048,512]{1,0:T(8,128)(2,1)S(1)}, u32[]{:S(2)}, u32[]{:S(2)}) collective-permute-start(bf16[2048,512]{1,0:T(8,128)(2,1)} %all-gather.7.cloned.1.call-done.refs_8_), channel_id=1, source_target_pairs={{0,8},{1,17},{2,10},{3,19},{4,12},{5,21},{6,14},{7,23},{8,0},{9,25... | collective-permute-start | bytes 6291464 | tf_op jit(solution)/shard_map/ppermute | solution.py:429
  75.9 2.5 %collective-permute-start.34 = (f32[3,36,16,128]{3,2,1,0:T(8,128)S(1)}, f32[3,36,16,128]{3,2,1,0:T(8,128)S(1)}, u32[]{:S(2)}, u32[]{:S(2)}) collective-permute-start(f32[3,36,16,128]{3,2,1,0:T(8,128)S(1)} %get-tuple-element.173), channel_id=1, source_target_pairs={{0,1},{1,0},{2,3},{3,2},{4,5},{5,4},{6,7},{7,6},{8,9},{9,8},{10,11... | collective-permute-start | bytes 2654216 | tf_op jit(solution)/shard_map/ppermute | solution.py:389
  97.1 3.4 %copy-start.1 = (bf16[2048,512]{1,0:T(8,128)(2,1)}, bf16[2048,512]{1,0:T(8,128)(2,1)S(1)}, u32[]{:S(2)}) copy-start(bf16[2048,512]{1,0:T(8,128)(2,1)S(1)} %collective-permute-done.35.value_ref.refs_9_) | copy-start | bytes 6291460
  97.1 38.1 %collective-permute-start.36 = (bf16[2048,512]{1,0:T(8,128)(2,1)}, bf16[2048,512]{1,0:T(8,128)(2,1)}, u32[]{:S(2)}, u32[]{:S(2)}) collective-permute-start(bf16[2048,512]{1,0:T(8,128)(2,1)} %all-gather.11.cloned.1.call-done.refs_8_), channel_id=1, source_target_pairs={{0,8},{1,17},{2,10},{3,19},{4,12},{5,21},{6,14},{7,23},{8,0},{9,25... | collective-permute-start | bytes 6291464 | tf_op jit(solution)/shard_map/ppermute | solution.py:429
  99.7 117.9 %all-gather.17.cloned.1.call-start = ((), (), s32[]{:S(2)}) async-start(), calls=%async_computation.5 | async-start | bytes 2359296 | tf_op jit(solution)/shard_map/all_gather | solution.py:468
  103.2 26.5 %collective-permute-start.37 = (bf16[1024,512]{1,0:T(8,128)(2,1)}, bf16[1024,512]{1,0:T(8,128)(2,1)}, u32[]{:S(2)}, u32[]{:S(2)}) collective-permute-start(bf16[1024,512]{1,0:T(8,128)(2,1)} %core_half.2), channel_id=1, source_target_pairs={{0,16},{1,9},{2,18},{3,11},{4,20},{5,13},{6,22},{7,15},{8,24},{9,1... | collective-permute-start | bytes 3145736 | tf_op jit(solution)/shard_map/ppermute | solution.py:429
  103.6 36.7 %collective-permute-start.39 = (bf16[2048,512]{1,0:T(8,128)(2,1)}, bf16[2048,512]{1,0:T(8,128)(2,1)S(1)}, u32[]{:S(2)}, u32[]{:S(2)}) collective-permute-start(bf16[2048,512]{1,0:T(8,128)(2,1)} %copy-done.1), channel_id=1, source_target_pairs={{0,1},{1,0},{2,3},{3,2},{4,5},{5,4},{6,7},{7,6},{8,9},{9,8},{10,11... | collective-permute-start | bytes 6291464 | tf_op jit(solution)/shard_map/ppermute | solution.py:389
  129.6 10.7 %collective-permute-start.40 = (bf16[1024,512]{1,0:T(8,128)(2,1)}, bf16[1024,512]{1,0:T(8,128)(2,1)}, u32[]{:S(2)}, u32[]{:S(2)}) collective-permute-start(bf16[1024,512]{1,0:T(8,128)(2,1)} %collective-permute-done.37.refs_11_), channel_id=1, source_target_pairs={{0,1},{1,0},{2,3},{3,2},{4,5},{5,4},{6,7},{7,6},{8,9},{9,8},{10,11... | collective-permute-start | bytes 3145736 | tf_op jit(solution)/shard_map/ppermute | solution.py:389
  137.9 26.3 %collective-permute-start.38 = (bf16[1024,512]{1,0:T(8,128)(2,1)}, bf16[1024,512]{1,0:T(8,128)(2,1)S(1)}, u32[]{:S(2)}, u32[]{:S(2)}) collective-permute-start(bf16[1024,512]{1,0:T(8,128)(2,1)} %core_half.3), channel_id=1, source_target_pairs={{0,16},{1,9},{2,18},{3,11},{4,20},{5,13},{6,22},{7,15},{8,24},{9,1... | collective-permute-start | bytes 3145736 | tf_op jit(solution)/shard_map/ppermute | solution.py:429
  138.9 34.6 %collective-permute-start.42 = (bf16[2048,512]{1,0:T(8,128)(2,1)}, bf16[2048,512]{1,0:T(8,128)(2,1)}, u32[]{:S(2)}, u32[]{:S(2)}) collective-permute-start(bf16[2048,512]{1,0:T(8,128)(2,1)} %all-gather.13.cloned.1.call-done.refs_8_), channel_id=1, source_target_pairs={{0,8},{1,17},{2,10},{3,19},{4,12},{5,21},{6,14},{7,23},{8,0},{9,25... | collective-permute-start | bytes 6291464 | tf_op jit(solution)/shard_map/ppermute | solution.py:429
  140.4 35.4 %collective-permute-start.43 = (bf16[2048,512]{1,0:T(8,128)(2,1)}, bf16[2048,512]{1,0:T(8,128)(2,1)}, u32[]{:S(2)}, u32[]{:S(2)}) collective-permute-start(bf16[2048,512]{1,0:T(8,128)(2,1)} %collective-permute-done.36.value_ref.refs_9_), channel_id=1, source_target_pairs={{0,1},{1,0},{2,3},{3,2},{4,5},{5,4},{6,7},{7,6},{8,9},{9,8},{10,11... | collective-permute-start | bytes 6291464 | tf_op jit(solution)/shard_map/ppermute | solution.py:389
  140.4 1.4 copy-start.4
  164.2 11.6 %copy-start.5 = (bf16[1024,512]{1,0:T(8,128)(2,1)}, bf16[1024,512]{1,0:T(8,128)(2,1)S(1)}, u32[]{:S(2)}) copy-start(bf16[1024,512]{1,0:T(8,128)(2,1)S(1)} %collective-permute-done.38.refs_11_) | copy-start | bytes 3145732
  164.2 31.7 %collective-permute-start.41 = (bf16[2048,512]{1,0:T(8,128)(2,1)}, bf16[2048,512]{1,0:T(8,128)(2,1)S(1)}, u32[]{:S(2)}, u32[]{:S(2)}) collective-permute-start(bf16[2048,512]{1,0:T(8,128)(2,1)} %all-gather.9.cloned.1.call-done.refs_3_), channel_id=1, source_target_pairs={{0,8},{1,17},{2,10},{3,19},{4,12},{5,21},{6,14},{7,23},{8,0},{9,25... | collective-permute-start | bytes 6291464 | tf_op jit(solution)/shard_map/ppermute | solution.py:429
  166.3 8.4 %collective-permute-start.44 = (bf16[1024,512]{1,0:T(8,128)(2,1)S(1)}, bf16[1024,512]{1,0:T(8,128)(2,1)S(1)}, u32[]{:S(2)}, u32[]{:S(2)}) collective-permute-start(bf16[1024,512]{1,0:T(8,128)(2,1)S(1)} %collective-permute-done.38.refs_11_), channel_id=1, source_target_pairs={{0,1},{1,0},{2,3},{3,2},{4,5},{5,4},{6,7},{7,6},{8,9},{9,8},{10,11... | collective-permute-start | bytes 3145736 | tf_op jit(solution)/shard_map/ppermute | solution.py:389
  173.5 23.3 %collective-permute-start.45 = (bf16[2048,512]{1,0:T(8,128)(2,1)}, bf16[2048,512]{1,0:T(8,128)(2,1)}, u32[]{:S(2)}, u32[]{:S(2)}) collective-permute-start(bf16[2048,512]{1,0:T(8,128)(2,1)} %collective-permute-done.42.refs_9_), channel_id=1, source_target_pairs={{0,1},{1,0},{2,3},{3,2},{4,5},{5,4},{6,7},{7,6},{8,9},{9,8},{10,11... | collective-permute-start | bytes 6291464 | tf_op jit(solution)/shard_map/ppermute | solution.py:389
  174.7 1.1 copy-start.6
  195.8 18.5 %copy-start.3 = (bf16[2048,512]{1,0:T(8,128)(2,1)}, bf16[2048,512]{1,0:T(8,128)(2,1)S(1)}, u32[]{:S(2)}) copy-start(bf16[2048,512]{1,0:T(8,128)(2,1)S(1)} %collective-permute-done.41.refs_4_) | copy-start | bytes 6291460
  195.8 21.8 %collective-permute-start.46 = (bf16[2048,512]{1,0:T(8,128)(2,1)S(1)}, bf16[2048,512]{1,0:T(8,128)(2,1)}, u32[]{:S(2)}, u32[]{:S(2)}) collective-permute-start(bf16[2048,512]{1,0:T(8,128)(2,1)S(1)} %collective-permute-done.41.refs_4_), channel_id=1, source_target_pairs={{0,1},{1,0},{2,3},{3,2},{4,5},{5,4},{6,7},{7,6},{8,9},{9,8},{10,11... | collective-permute-start | bytes 6291464 | tf_op jit(solution)/shard_map/ppermute | solution.py:389
Sparse Core Ops, SparseCore 0:
  25.4 38.2 all-gather.6
  65.2 31.8 all-gather.10
  98.7 28.5 all-gather.12
  128.8 28.5 all-gather.8
  158.9 28.5 all-gather.14
  189.0 28.5 all-gather.16
where the time goes:
time: 235 us; the launch traced here: 230 us
  Pallas kernels  79.8 us (34%)
  waiting for transfers between devices  66.1 us (28%)
  starting transfers between devices  45.3 us (19%)
  between operations  19.2 us (8%)
  other arithmetic  11.8 us (5%)
  local copies, waits for them, and re-layouts  8.15 us (3%)
    pallas_call x5, Pallas kernels, section_step(): pl.pallas_call(functools.partial(section_kernel, wholes_count, halves_cou...  74.4 us
    ppermute x6, waiting for transfers between devices, sent_by_core(): return lax.ppermute(value, ('pipe', 'seq'), pairs)  44.3 us
    ppermute x3, starting transfers between devices, across(): return lax.ppermute(value, 'pipe', [(i, i ^ hops) for i in range(count)])  19.7 us
    ppermute x6, starting transfers between devices, spread_quarters(): held.append(lax.ppermute(columns(hops), 'pipe', pairs))  10.2 us
    ppermute x6, starting transfers between devices, sent_by_core(): return lax.ppermute(value, ('pipe', 'seq'), pairs)  9.29 us
    ppermute x6, waiting for transfers between devices, spread_quarters(): held.append(lax.ppermute(columns(hops), 'pipe', pairs))  8.85 us
    all_gather x6, waiting for transfers between devices, along_seq(): lax.all_gather(quarter, 'seq', axis=0, tiled=True)  5.95 us
    pallas_call x2, Pallas kernels, core_half(): pl.pallas_call(half_copy_kernel, out_shape=jax.ShapeDtypeStruct(shape, va...  5.34 us
  transfers between devices with their start and end apart: 30, of which 11 were waited for; matrix products, arithmetic and copies ran while one was open for 6% of the time, Pallas kernels for 32%

commit v1 on v0

--- a/solution.py
+++ b/solution.py
@@ -459,9 +459,8 @@
 
     tie = lax.optimization_barrier
     quarters = spread_quarters(out_proj[0], 0, 0)
-    own = permuted_rows(inputs[0], order)
-    held = (quarters, halves, own, out_proj[0])
-    quarters, halves, own, shard = tie(held)
+    held = (quarters, halves, inputs[0], out_proj[0])
+    quarters, halves, entering, shard = tie(held)
 
     def along_seq(quarters):
         return {
@@ -470,6 +469,7 @@
         }
 
     wholes = along_seq(quarters)
+    own, halves, shard = tie((permuted_rows(entering, order), halves, shard))
     fetched = [across(own_half(halves), hops) for hops in range(1, section_count)]
     last_quarters = spread_quarters(shard, 3, seq_far)
     before = lax.ppermute(own, "seq", [(i, i + 1) for i in range(seq_count - 1)])
@@ -490,17 +490,18 @@
         return jnp.concatenate([place, which]), (keep, flags, docs[:, None], docs[None, :], tables)
 
     near, far = {}, {}
-    held = (fetched, before, last_quarters, wholes[0])
-    fetched, before, last_quarters, wholes[0] = tie(held)
+    fetched, wholes[0] = tie((fetched, wholes[0]))
     near[0] = hop(0)
+    held = (near[0], wholes[1], own, before, fetched, last_quarters)
+    near[0], wholes[1], own, before, fetched, last_quarters = tie(held)
+    half = core_half(near[0], place)
+    half, own, before, fetched, halves = tie((half, own, before, fetched, halves))
+    far[0] = sent_by_core(half, (2, 1))
+    near[1] = hop(1)
+    last_quarters = along_seq(last_quarters)
     tables = joined_tables(halves, fetched)
     where, mixer = mixing(0)
     middle, attended = section_step(where, (before, own), mixing=mixer)
-    held = (near[0], middle, attended, wholes[1], last_quarters)
-    near[0], middle, attended, wholes[1], last_quarters = tie(held)
-    last_quarters = along_seq(last_quarters)
-    far[0] = passed_on(near[0], place)
-    near[1] = hop(1)
     for section in range(section_count):
         weights = [wholes[section], near[section], swapped(near[section])]
         if section < seq_far:

time: 235 us -> 228 us (0.970); the launches traced: 230 us -> 229 us
  starting transfers between devices: 45.3 us -> 22.1 us
  Pallas kernels: 79.8 us -> 94.9 us
  waiting for transfers between devices: 66.1 us -> 71.2 us
    ppermute x6, waiting for transfers between devices: 44.3 us -> 12.7 us  [sent_by_core(): return lax.ppermute(value, ('pipe', 'seq'), pairs)]
    ppermute x6, waiting for transfers between devices: 8.85 us -> 32.8 us  [spread_quarters(): held.append(lax.ppermute(columns(hops), 'pipe', pairs))]
    ppermute x3, starting transfers between devices: 19.7 us -> 3.55 us  [across(): return lax.ppermute(value, 'pipe', [(i, i ^ hops) for i in range(count)])]
    pallas_call x5, Pallas kernels: 74.4 us -> 89.6 us  [section_step(): pl.pallas_call(functools.partial(section_kernel, wholes_count, halves_cou...]
    ppermute x1, waiting for transfers between devices: 0.01 us -> 12.3 us  [mover(): return lambda held: lax.ppermute(held, 'pipe', pairs)]
    ppermute x3, waiting for transfers between devices: 4.6 us -> 11.4 us  [across(): return lax.ppermute(value, 'pipe', [(i, i ^ hops) for i in range(count)])]
    ppermute x6, starting transfers between devices: 9.29 us -> 2.7 us  [sent_by_core(): return lax.ppermute(value, ('pipe', 'seq'), pairs)]
    all_gather x6, waiting for transfers between devices: 5.95 us -> 0.03 us  [along_seq(): lax.all_gather(quarter, 'seq', axis=0, tiled=True)]
  transfers between devices with their start and end apart: 30 -> 30, of which waited for: 11 -> 10; matrix products, arithmetic and copies ran while one was open for 6% -> 8% of each run, Pallas kernels for 32% -> 39%
where the time goes in v1:
time: 228 us; the launch traced here: 229 us
  Pallas kernels  94.9 us (42%)
  waiting for transfers between devices  71.2 us (31%)
  starting transfers between devices  22.1 us (10%)
  between operations  19 us (8%)
  other arithmetic  13.8 us (6%)
  local copies, waits for them, and re-layouts  7.72 us (3%)
    pallas_call x5, Pallas kernels, section_step(): pl.pallas_call(functools.partial(section_kernel, wholes_count, halves_cou...  89.6 us
    ppermute x6, waiting for transfers between devices, spread_quarters(): held.append(lax.ppermute(columns(hops), 'pipe', pairs))  32.8 us
    ppermute x6, waiting for transfers between devices, sent_by_core(): return lax.ppermute(value, ('pipe', 'seq'), pairs)  12.7 us
    ppermute x1, waiting for transfers between devices, mover(): return lambda held: lax.ppermute(held, 'pipe', pairs)  12.3 us
    ppermute x3, waiting for transfers between devices, across(): return lax.ppermute(value, 'pipe', [(i, i ^ hops) for i in range(count)])  11.4 us
    ppermute x6, starting transfers between devices, spread_quarters(): held.append(lax.ppermute(columns(hops), 'pipe', pairs))  6.8 us
    pallas_call x2, Pallas kernels, core_half(): pl.pallas_call(half_copy_kernel, out_shape=jax.ShapeDtypeStruct(shape, va...  5.36 us
    ppermute x7, starting transfers between devices, swapped(): return lax.ppermute(value, 'seq', [(i, i ^ 1) for i in range(count)])  5.32 us
  transfers between devices with their start and end apart: 30, of which 10 were waited for; matrix products, arithmetic and copies ran while one was open for 8% of the time, Pallas kernels for 39%

profile of v1, /device:TPU:24, one launch (start us, length us, event | category | flops | bytes accessed | tf_op | source)
XLA Modules:
  0.0 228.8 jit_solution(12944404274016291241)
XLA Ops:
  6.6 1.4 constant_dynamic-slice_fusion.3
  8.0 1.6 collective-permute-start.24
  9.6 1.5 collective-permute-start.25
  11.1 0.5 collective-permute-start.26
  11.7 0.5 multiply_bitcast_fusion.1
  12.5 4.8 %collective-permute-done.24 = bf16[256,512]{1,0:T(8,128)(2,1)S(1)} collective-permute-done((bf16[256,512]{1,0:T(8,128)(2,1)S(1)}, bf16[256,512]{1,0:T(8,128)(2,1)S(1)}, u32[]{:S(2)}, u32[]{:S(2)}) %collective-permute-start.24) | collective-permute-done | bytes 262176 | tf_op jit(solution)/shard_map/ppermute | solution.py:403
  17.3 5.7 %collective-permute-done.25 = bf16[256,512]{1,0:T(8,128)(2,1)S(1)} collective-permute-done((bf16[256,512]{1,0:T(8,128)(2,1)S(1)}, bf16[256,512]{1,0:T(8,128)(2,1)S(1)}, u32[]{:S(2)}, u32[]{:S(2)}) %collective-permute-start.25) | collective-permute-done | bytes 262176 | tf_op jit(solution)/shard_map/ppermute | solution.py:403
  23.0 0.1 pad_maximum_fusion.2
  23.1 1.0 dynamic-slice_bitcast_fusion.4
  24.2 0.7 all-gather.9.cloned.1.call-update
  25.0 0.7 all-gather.13.cloned.1.call-update
  25.7 0.5 all-gather.11.cloned.1.call-update
  26.4 0.7 iota_reduce_fusion
  27.7 13.9 %conditional.1 = (bf16[128,2048]{1,0:T(8,128)(2,1)}) conditional(s32[]{:T(128)} %clamp.3, bf16[128,2048]{1,0:T(8,128)(2,1)S(1)} %bitcast.143, bf16[128,2048]{1,0:T(8,128)(2,1)S(1)} %bitcast.133, bf16[128,2048]{1,0:T(8,128)(2,1)S(1)} %bitcast.134, bf16[128,2048]{1,0:T(8,128)(2,1)S(1)} %bitcast.135, ...), branch_computations={%region_6.7_spmd, %region_7.8_spmd, %region_8.9_spmd, %region_9.10... | conditional | bytes 2097200 | solution.py:446
  27.8 1.6 collective-permute-start.22
  29.3 12.3 %collective-permute-done.22 = bf16[128,2048]{1,0:T(8,128)(2,1)} collective-permute-done((bf16[128,2048]{1,0:T(8,128)(2,1)S(1)}, bf16[128,2048]{1,0:T(8,128)(2,1)}, u32[]{:S(2)}, u32[]{:S(2)}) %collective-permute-start.22) | collective-permute-done | bytes 524320 | tf_op jit(solution)/shard_map/cond/branch_22_fun/ppermute | solution.py:444
  41.7 1.5 collective-permute-start.27
  43.2 2.0 collective-permute-start.29
  45.2 6.2 %collective-permute-done.27 = f32[36,16,128]{2,1,0:T(8,128)S(1)} collective-permute-done((f32[36,16,128]{2,1,0:T(8,128)S(1)}, f32[36,16,128]{2,1,0:T(8,128)S(1)}, u32[]{:S(2)}, u32[]{:S(2)}) %collective-permute-start.27) | collective-permute-done | bytes 294944 | tf_op jit(solution)/shard_map/ppermute | solution.py:384
  51.4 5.2 %collective-permute-done.28 = f32[36,16,128]{2,1,0:T(8,128)S(1)} collective-permute-done((f32[36,16,128]{2,1,0:T(8,128)S(1)}, f32[36,16,128]{2,1,0:T(8,128)S(1)}, u32[]{:S(2)}, u32[]{:S(2)}) %collective-permute-start.28) | collective-permute-done | bytes 294944 | tf_op jit(solution)/shard_map/ppermute | solution.py:384
  56.7 0.7 copy-done.11
  57.4 0.7 dynamic_slice.63
  60.1 0.1 reduce.36
  60.3 0.6 slice.20
  60.9 1.3 compare_reduce_fusion.1
  64.5 1.0 dynamic-slice_bitcast_fusion.3
  65.5 0.7 collective-permute-start.32
  66.1 1.3 collective-permute-start.33
  67.4 1.3 collective-permute-start.34
  68.7 1.9 collective-permute-start.31
  70.7 0.7 fusion.6
  71.5 0.1 reduce_or.9
  71.6 8.8 %collective-permute-done.33 = bf16[256,512]{1,0:T(8,128)(2,1)S(1)} collective-permute-done((bf16[256,512]{1,0:T(8,128)(2,1)}, bf16[256,512]{1,0:T(8,128)(2,1)S(1)}, u32[]{:S(2)}, u32[]{:S(2)}) %collective-permute-start.33) | collective-permute-done | bytes 262176 | tf_op jit(solution)/shard_map/ppermute | solution.py:403
  80.5 13.5 %collective-permute-done.34 = bf16[256,512]{1,0:T(8,128)(2,1)S(1)} collective-permute-done((bf16[256,512]{1,0:T(8,128)(2,1)}, bf16[256,512]{1,0:T(8,128)(2,1)S(1)}, u32[]{:S(2)}, u32[]{:S(2)}) %collective-permute-start.34) | collective-permute-done | bytes 262176 | tf_op jit(solution)/shard_map/ppermute | solution.py:403
  94.0 0.1 pad_maximum_fusion.3
  94.1 0.9 dynamic-slice_bitcast_fusion.1
  95.0 0.9 collective-permute-start.36
  96.0 0.7 pad_add_fusion.1.place_ref.refs_0_
  96.6 0.5 compare_select_fusion.refs_4_
  97.2 2.7 %core_half.2 = bf16[1024,512]{1,0:T(8,128)(2,1)} custom-call(s32[2]{0:T(128)} %pad_add_fusion.1.place_ref.refs_0_, bf16[2048,512]{1,0:T(8,128)(2,1)} %copy-done.1), custom_call_target="tpu_custom_call" | custom-call | tf_op jit(solution)/shard_map/core_half/pallas_call | solution.py:362
  99.9 2.6 %fusion.8 = (f32[3,1,36,16,128]{4,3,2,1,0:T(8,128)}, f32[3,36,16,128]{3,2,1,0:T(8,128)}) fusion(f32[1,36,16,128]{3,2,1,0:T(8,128)} %bitcast.34, f32[1,36,16,128]{3,2,1,0:T(8,128)} %bitcast.119, f32[1,36,16,128]{3,2,1,0:T(8,128)S(1)} %bitcast.118), kind=kLoop, calls=%fused_computation.61 | loop fusion | flops 442368 | bytes 2654208 | tf_op jit(solution)/shard_map/stack | solution.py:419
  102.5 0.6 pad_add_fusion.7
  103.1 0.7 pad_add_fusion.6
  103.8 0.5 collective-permute-start.39
  104.3 0.7 pad_add_fusion.4.refs_2_
  105.0 0.1 copy.18
  105.1 0.7 fusion.4.refs_3_
  105.9 1.7 pad_maximum_fusion.1
  107.6 1.7 pad_maximum_fusion.refs_5_
  109.2 18.2 %section_step.5 = (bf16[256,2048]{1,0:T(8,128)(2,1)}, bf16[256,2048]{1,0:T(8,128)(2,1)}) custom-call(s32[4]{0:T(128)} %get-tuple-element.202.refs_0_, f32[256]{0:T(256)} %get-tuple-element.205.refs_1_, s32[17]{0:T(128)} %pad_add_fusion.4.refs_2_, s32[256,1]{1,0:T(8,128)} %fusion.4.refs_3_, s32[1,256]{1,0:T(1,128)} %compare_select_fusion.refs_4_, ...), custom_call_target="tpu_custom_call" | custom-call | flops 2147483648 | bytes 8388608 | tf_op jit(solution)/shard_map/section_step/pallas_call | solution.py:327
  127.5 2.4 %collective-permute-start.40 = (bf16[1024,512]{1,0:T(8,128)(2,1)}, bf16[1024,512]{1,0:T(8,128)(2,1)}, u32[]{:S(2)}, u32[]{:S(2)}) collective-permute-start(bf16[1024,512]{1,0:T(8,128)(2,1)} %collective-permute-done.37.refs_11_), channel_id=1, source_target_pairs={{0,1},{1,0},{2,3},{3,2},{4,5},{5,4},{6,7},{7,6},{8,9},{9,8},{10,11... | collective-permute-start | bytes 3145736 | tf_op jit(solution)/shard_map/ppermute | solution.py:389
  129.9 2.8 %collective-permute-done.36.value_ref.refs_9_ = bf16[2048,512]{1,0:T(8,128)(2,1)} collective-permute-done((bf16[2048,512]{1,0:T(8,128)(2,1)}, bf16[2048,512]{1,0:T(8,128)(2,1)}, u32[]{:S(2)}, u32[]{:S(2)}) %collective-permute-start.36) | collective-permute-done | bytes 2097184 | tf_op jit(solution)/shard_map/ppermute | solution.py:429
  132.7 2.7 %core_half.3 = bf16[1024,512]{1,0:T(8,128)(2,1)} custom-call(s32[2]{0:T(128)} %pad_add_fusion.1.place_ref.refs_0_, bf16[2048,512]{1,0:T(8,128)(2,1)} %collective-permute-done.36.value_ref.refs_9_), custom_call_target="tpu_custom_call" | custom-call | tf_op jit(solution)/shard_map/core_half/pallas_call | solution.py:362
  135.4 0.9 collective-permute-start.42
  136.3 22.1 %section_step.6 = (bf16[256,2048]{1,0:T(8,128)(2,1)}, bf16[256,2048]{1,0:T(8,128)(2,1)}) custom-call(s32[4]{0:T(128)} %get-tuple-element.201.refs_0_, f32[256]{0:T(256)} %get-tuple-element.205.refs_1_, s32[17]{0:T(128)} %pad_add_fusion.4.refs_2_, s32[256,1]{1,0:T(8,128)} %fusion.4.refs_3_, s32[1,256]{1,0:T(1,128)} %compare_select_fusion.refs_4_, ...), custom_call_target="tpu_custom_call" | custom-call | flops 2147483648 | bytes 8388608 | tf_op jit(solution)/shard_map/section_step/pallas_call | solution.py:327
  158.4 3.3 %collective-permute-done.38.refs_11_ = bf16[1024,512]{1,0:T(8,128)(2,1)S(1)} collective-permute-done((bf16[1024,512]{1,0:T(8,128)(2,1)}, bf16[1024,512]{1,0:T(8,128)(2,1)S(1)}, u32[]{:S(2)}, u32[]{:S(2)}) %collective-permute-start.38) | collective-permute-done | bytes 1048608 | tf_op jit(solution)/shard_map/ppermute | solution.py:429
  161.7 0.8 collective-permute-start.41
  162.6 6.6 %collective-permute-done.42.refs_9_ = bf16[2048,512]{1,0:T(8,128)(2,1)} collective-permute-done((bf16[2048,512]{1,0:T(8,128)(2,1)}, bf16[2048,512]{1,0:T(8,128)(2,1)}, u32[]{:S(2)}, u32[]{:S(2)}) %collective-permute-start.42) | collective-permute-done | bytes 2097184 | tf_op jit(solution)/shard_map/ppermute | solution.py:429
  169.2 1.0 collective-permute-start.45
  170.3 1.0 copy-done.8
  171.3 22.3 %section_step.7 = (bf16[256,2048]{1,0:T(8,128)(2,1)}, bf16[256,2048]{1,0:T(8,128)(2,1)}) custom-call(s32[4]{0:T(128)} %get-tuple-element.176.refs_0_, f32[256]{0:T(256)} %get-tuple-element.205.refs_1_, s32[17]{0:T(128)} %pad_add_fusion.4.refs_2_, s32[256,1]{1,0:T(8,128)} %fusion.4.refs_3_, s32[1,256]{1,0:T(1,128)} %compare_select_fusion.refs_4_, ...), custom_call_target="tpu_custom_call" | custom-call | flops 2147483648 | bytes 8388608 | tf_op jit(solution)/shard_map/section_step/pallas_call | solution.py:327
  193.6 1.3 collective-permute-start.46
  194.9 21.2 %section_step.8 = (bf16[128,2048]{1,0:T(8,128)(2,1)}, bf16[128,2048]{1,0:T(8,128)(2,1)}) custom-call(s32[4]{0:T(128)} %get-tuple-element.203.refs_0_, f32[256]{0:T(256)} %get-tuple-element.205.refs_1_, s32[17]{0:T(128)} %pad_add_fusion.4.refs_2_, s32[256,1]{1,0:T(8,128)} %fusion.4.refs_3_, s32[1,256]{1,0:T(1,128)} %compare_select_fusion.refs_4_, ...), custom_call_target="tpu_custom_call" | custom-call | flops 2147483648 | bytes 8388608 | tf_op jit(solution)/shard_map/section_step/pallas_call | solution.py:327
  216.1 5.8 %section_step.9 = bf16[128,2048]{1,0:T(8,128)(2,1)} custom-call(s32[2]{0:T(128)} %pad_add_fusion.1.place_ref.refs_0_, bf16[128,2048]{1,0:T(8,128)(2,1)} %get-tuple-element.172.refs_1_, bf16[128,2048]{1,0:T(8,128)(2,1)} %get-tuple-element.173.refs_2_, bf16[2048,512]{1,0:T(8,128)(2,1)} %all-gather.11.cloned.1.call-done.refs_3_, bf16[2048,512]{1,0:T(8,128)(2,1)} %copy-done.6, ...), custom_call_target="tpu_custom_call" | custom-call | flops 1073741824 | bytes 8388608 | tf_op jit(solution)/shard_map/section_step/pallas_call | solution.py:327
  (101 shorter events, 1.4 us)
Async XLA Ops:
  6.5 53.4 %copy-start = (s32[4,32]{1,0:T(4,128)S(1)}, s32[4,32]{1,0:T(4,128)}, u32[]{:S(2)}) copy-start(s32[4,32]{1,0:T(4,128)} %param.36) | copy-start | bytes 1540
  6.5 5.0 %copy-start.12 = (f32[1,2,16,2048]{3,2,1,0:T(8,128)S(1)}, f32[1,2,16,2048]{3,2,1,0:T(8,128)}, u32[]{:S(2)}) copy-start(f32[1,2,16,2048]{3,2,1,0:T(8,128)} %param.41) | copy-start | bytes 786436
  6.5 5.1 %copy-start.14 = (f32[1,16,2048]{2,1,0:T(8,128)S(1)}, f32[1,16,2048]{2,1,0:T(8,128)}, u32[]{:S(2)}) copy-start(f32[1,16,2048]{2,1,0:T(8,128)} %param.39) | copy-start | bytes 393220
  6.5 5.1 %copy-start.13 = (f32[1,16,2048]{2,1,0:T(8,128)S(1)}, f32[1,16,2048]{2,1,0:T(8,128)}, u32[]{:S(2)}) copy-start(f32[1,16,2048]{2,1,0:T(8,128)} %param.40) | copy-start | bytes 393220
  6.5 50.8 %all-gather.7.cloned.1.call-start = ((), (), s32[]{:S(2)}) async-start(), calls=%async_computation | async-start | bytes 2359296 | tf_op jit(solution)/shard_map/all_gather | solution.py:467
  8.0 4.3 %copy-start.17 = (f32[1,2048]{1,0:T(1,128)S(1)}, f32[1,2048]{1,0:T(1,128)}, u32[]{:S(2)}) copy-start(f32[1,2048]{1,0:T(1,128)} %param.38) | copy-start | bytes 24580
  8.0 4.3 %copy-start.16 = (f32[1,2,2048]{2,1,0:T(2,128)S(1)}, f32[1,2,2048]{2,1,0:T(2,128)}, u32[]{:S(2)}) copy-start(f32[1,2,2048]{2,1,0:T(2,128)} %param.43) | copy-start | bytes 49156
  8.0 4.4 %copy-start.15 = (f32[1,2048]{1,0:T(1,128)S(1)}, f32[1,2048]{1,0:T(1,128)}, u32[]{:S(2)}) copy-start(f32[1,2048]{1,0:T(1,128)} %param.42) | copy-start | bytes 24580
  8.0 9.3 %collective-permute-start.24 = (bf16[256,512]{1,0:T(8,128)(2,1)S(1)}, bf16[256,512]{1,0:T(8,128)(2,1)S(1)}, u32[]{:S(2)}, u32[]{:S(2)}) collective-permute-start(bf16[256,512]{1,0:T(8,128)(2,1)S(1)} %get-tuple-element.190), channel_id=1, source_target_pairs={{0,8},{8,0},{16,24},{24,16},{1,9},{9,1},{17,25},{25,17},{2,10},{10... | collective-permute-start | bytes 786440 | tf_op jit(solution)/shard_map/ppermute | solution.py:403
  9.6 13.4 %collective-permute-start.25 = (bf16[256,512]{1,0:T(8,128)(2,1)S(1)}, bf16[256,512]{1,0:T(8,128)(2,1)S(1)}, u32[]{:S(2)}, u32[]{:S(2)}) collective-permute-start(bf16[256,512]{1,0:T(8,128)(2,1)S(1)} %get-tuple-element.189), channel_id=1, source_target_pairs={{0,16},{8,24},{16,0},{24,8},{1,17},{9,25},{17,1},{25,9},{2,18},{10... | collective-permute-start | bytes 786440 | tf_op jit(solution)/shard_map/ppermute | solution.py:403
  11.1 11.9 %collective-permute-start.26 = (bf16[256,512]{1,0:T(8,128)(2,1)S(1)}, bf16[256,512]{1,0:T(8,128)(2,1)S(1)}, u32[]{:S(2)}, u32[]{:S(2)}) collective-permute-start(bf16[256,512]{1,0:T(8,128)(2,1)S(1)} %get-tuple-element.191), channel_id=1, source_target_pairs={{0,24},{8,16},{16,8},{24,0},{1,25},{9,17},{17,9},{25,1},{2,26},{10... | collective-permute-start | bytes 786440 | tf_op jit(solution)/shard_map/ppermute | solution.py:403
  12.5 29.2 %copy-start.4 = (f32[2,36,16,128]{3,2,1,0:T(8,128)}, f32[2,36,16,128]{3,2,1,0:T(8,128)S(1)}, u32[]{:S(2)}) copy-start(f32[2,36,16,128]{3,2,1,0:T(8,128)S(1)} %pad_maximum_fusion.5) | copy-start | bytes 1769476
  23.1 3.2 %copy-start.18 = (s32[24,4]{0,1:T(4,128)S(1)}, s32[24,4]{0,1:T(4,128)}, u32[]{:S(2)}) copy-start(s32[24,4]{0,1:T(4,128)} %constant.115.clone) | copy-start | bytes 1156
  23.1 3.2 %copy-start.19 = (s32[4]{0:T(128)S(1)}, s32[4]{0:T(128)}, u32[]{:S(2)}) copy-start(s32[4]{0:T(128)} %param.37) | copy-start | bytes 52
  23.1 4.6 %copy-start.20 = (bf16[1,128,2048]{2,1,0:T(8,128)(2,1)S(1)}, bf16[1,128,2048]{2,1,0:T(8,128)(2,1)}, u32[]{:S(2)}) copy-start(bf16[1,128,2048]{2,1,0:T(8,128)(2,1)} %param.35) | copy-start | bytes 1572868
  23.1 41.4 %copy-start.3 = (bf16[1,256,2048]{2,1,0:T(8,128)(2,1)S(1)}, bf16[1,256,2048]{2,1,0:T(8,128)(2,1)}, u32[]{:S(2)}) copy-start(bf16[1,256,2048]{2,1,0:T(8,128)(2,1)} %param.44) | copy-start | bytes 3145732
  24.2 70.8 %all-gather.9.cloned.1.call-start = ((), (), s32[]{:S(2)}) async-start(), calls=%async_computation.1 | async-start | bytes 2359296 | tf_op jit(solution)/shard_map/all_gather | solution.py:467
  25.0 104.9 %all-gather.13.cloned.1.call-start = ((), (), s32[]{:S(2)}) async-start(), calls=%async_computation.3 | async-start | bytes 2359296 | tf_op jit(solution)/shard_map/all_gather | solution.py:467
  25.7 136.0 %all-gather.11.cloned.1.call-start = ((), (), s32[]{:S(2)}) async-start(), calls=%async_computation.2 | async-start | bytes 2359296 | tf_op jit(solution)/shard_map/all_gather | solution.py:467
  26.3 168.6 %all-gather.15.cloned.1.call-start = ((), (), s32[]{:S(2)}) async-start(), calls=%async_computation.4 | async-start | bytes 2359296 | tf_op jit(solution)/shard_map/all_gather | solution.py:467
  27.8 13.9 %collective-permute-start.22 = (bf16[128,2048]{1,0:T(8,128)(2,1)S(1)}, bf16[128,2048]{1,0:T(8,128)(2,1)}, u32[]{:S(2)}, u32[]{:S(2)}) collective-permute-start(bf16[128,2048]{1,0:T(8,128)(2,1)S(1)} %param.22), channel_id=1, source_target_pairs={{24,0},{16,8},{0,16},{8,24},{25,1},{17,9},{1,17},{9,25},{26,2},{18... | collective-permute-start | bytes 1572872 | tf_op jit(solution)/shard_map/cond/branch_22_fun/ppermute | solution.py:444
  41.7 9.7 %collective-permute-start.27 = (f32[36,16,128]{2,1,0:T(8,128)S(1)}, f32[36,16,128]{2,1,0:T(8,128)S(1)}, u32[]{:S(2)}, u32[]{:S(2)}) collective-permute-start(f32[36,16,128]{2,1,0:T(8,128)S(1)} %dynamic-slice_bitcast_fusion), channel_id=1, source_target_pairs={{0,8},{8,0},{16,24},{24,16},{1,9},{9,1},{17,25},{25,17},{2,10},{10... | collective-permute-start | bytes 884744 | tf_op jit(solution)/shard_map/ppermute | solution.py:384
  43.2 13.4 %collective-permute-start.28 = (f32[36,16,128]{2,1,0:T(8,128)S(1)}, f32[36,16,128]{2,1,0:T(8,128)S(1)}, u32[]{:S(2)}, u32[]{:S(2)}) collective-permute-start(f32[36,16,128]{2,1,0:T(8,128)S(1)} %dynamic-slice_bitcast_fusion), channel_id=1, source_target_pairs={{0,16},{8,24},{16,0},{24,8},{1,17},{9,25},{17,1},{25,9},{2,18},{10... | collective-permute-start | bytes 884744 | tf_op jit(solution)/shard_map/ppermute | solution.py:384
  43.2 14.1 %collective-permute-start.29 = (f32[36,16,128]{2,1,0:T(8,128)S(1)}, f32[36,16,128]{2,1,0:T(8,128)}, u32[]{:S(2)}, u32[]{:S(2)}) collective-permute-start(f32[36,16,128]{2,1,0:T(8,128)S(1)} %dynamic-slice_bitcast_fusion), channel_id=1, source_target_pairs={{0,24},{8,16},{16,8},{24,0},{1,25},{9,17},{17,9},{25,1},{2,26},{10... | collective-permute-start | bytes 884744 | tf_op jit(solution)/shard_map/ppermute | solution.py:384
  51.4 5.2 %copy-start.9 = (f32[36,16,128]{2,1,0:T(8,128)}, f32[36,16,128]{2,1,0:T(8,128)S(1)}, u32[]{:S(2)}) copy-start(f32[36,16,128]{2,1,0:T(8,128)S(1)} %collective-permute-done.27) | copy-start | bytes 884740
  56.7 0.7 copy-start.11
  57.4 37.6 %collective-permute-start.30 = (bf16[2048,512]{1,0:T(8,128)(2,1)}, bf16[2048,512]{1,0:T(8,128)(2,1)S(1)}, u32[]{:S(2)}, u32[]{:S(2)}) collective-permute-start(bf16[2048,512]{1,0:T(8,128)(2,1)} %all-gather.7.cloned.1.call-done.refs_8_), channel_id=1, source_target_pairs={{0,8},{1,17},{2,10},{3,19},{4,12},{5,21},{6,14},{7,23},{8,0},{9,25... | collective-permute-start | bytes 6291464 | tf_op jit(solution)/shard_map/ppermute | solution.py:429
  65.5 6.2 %collective-permute-start.32 = (bf16[256,512]{1,0:T(8,128)(2,1)}, bf16[256,512]{1,0:T(8,128)(2,1)S(1)}, u32[]{:S(2)}, u32[]{:S(2)}) collective-permute-start(bf16[256,512]{1,0:T(8,128)(2,1)} %get-tuple-element.183), channel_id=1, source_target_pairs={{16,24},{24,16},{17,25},{25,17},{18,26},{26,18},{19,27},{27,19},{2... | collective-permute-start | bytes 786440 | tf_op jit(solution)/shard_map/ppermute | solution.py:403
  66.1 14.3 %collective-permute-start.33 = (bf16[256,512]{1,0:T(8,128)(2,1)}, bf16[256,512]{1,0:T(8,128)(2,1)S(1)}, u32[]{:S(2)}, u32[]{:S(2)}) collective-permute-start(bf16[256,512]{1,0:T(8,128)(2,1)} %get-tuple-element.182), channel_id=1, source_target_pairs={{16,0},{24,8},{17,1},{25,9},{18,2},{26,10},{19,3},{27,11},{20,4},{... | collective-permute-start | bytes 786440 | tf_op jit(solution)/shard_map/ppermute | solution.py:403
  67.4 26.5 %collective-permute-start.34 = (bf16[256,512]{1,0:T(8,128)(2,1)}, bf16[256,512]{1,0:T(8,128)(2,1)S(1)}, u32[]{:S(2)}, u32[]{:S(2)}) collective-permute-start(bf16[256,512]{1,0:T(8,128)(2,1)} %get-tuple-element.181), channel_id=1, source_target_pairs={{16,8},{24,0},{17,9},{25,1},{18,10},{26,2},{19,11},{27,3},{20,12},... | collective-permute-start | bytes 786440 | tf_op jit(solution)/shard_map/ppermute | solution.py:403
  68.7 26.3 %collective-permute-start.31 = (bf16[128,2048]{1,0:T(8,128)(2,1)}, bf16[128,2048]{1,0:T(8,128)(2,1)}, u32[]{:S(2)}, u32[]{:S(2)}) collective-permute-start(bf16[128,2048]{1,0:T(8,128)(2,1)} %get-tuple-element.206.refs_7_), channel_id=1, source_target_pairs={{0,1},{1,2},{2,3},{3,4},{4,5},{5,6},{6,7},{8,9},{9,10},{10,11},{11... | collective-permute-start | bytes 1572872 | tf_op jit(solution)/shard_map/ppermute | solution.py:475
  94.1 5.8 %copy-start.10 = (f32[36,16,128]{2,1,0:T(8,128)S(1)}, f32[36,16,128]{2,1,0:T(8,128)}, u32[]{:S(2)}) copy-start(f32[36,16,128]{2,1,0:T(8,128)} %copy-done.9) | copy-start | bytes 884740
  95.0 2.2 copy-start.1
  95.0 37.7 %collective-permute-start.36 = (bf16[2048,512]{1,0:T(8,128)(2,1)}, bf16[2048,512]{1,0:T(8,128)(2,1)}, u32[]{:S(2)}, u32[]{:S(2)}) collective-permute-start(bf16[2048,512]{1,0:T(8,128)(2,1)} %all-gather.9.cloned.1.call-done.refs_8_), channel_id=1, source_target_pairs={{0,8},{1,17},{2,10},{3,19},{4,12},{5,21},{6,14},{7,23},{8,0},{9,25... | collective-permute-start | bytes 6291464 | tf_op jit(solution)/shard_map/ppermute | solution.py:429
  95.9 120.2 %all-gather.17.cloned.1.call-start = ((), (), s32[]{:S(2)}) async-start(), calls=%async_computation.5 | async-start | bytes 2359296 | tf_op jit(solution)/shard_map/all_gather | solution.py:467
  99.9 4.0 %copy-start.2 = (bf16[2048,512]{1,0:T(8,128)(2,1)S(1)}, bf16[2048,512]{1,0:T(8,128)(2,1)}, u32[]{:S(2)}) copy-start(bf16[2048,512]{1,0:T(8,128)(2,1)} %copy-done.1) | copy-start | bytes 6291460
  99.9 5.9 %copy-start.5 = (f32[2,36,16,128]{3,2,1,0:T(8,128)S(1)}, f32[2,36,16,128]{3,2,1,0:T(8,128)}, u32[]{:S(2)}) copy-start(f32[2,36,16,128]{3,2,1,0:T(8,128)} %copy-done.4) | copy-start | bytes 1769476
  102.5 3.4 %collective-permute-start.35 = (f32[3,36,16,128]{3,2,1,0:T(8,128)}, f32[3,36,16,128]{3,2,1,0:T(8,128)}, u32[]{:S(2)}, u32[]{:S(2)}) collective-permute-start(f32[3,36,16,128]{3,2,1,0:T(8,128)} %get-tuple-element.193), channel_id=1, source_target_pairs={{0,1},{1,0},{2,3},{3,2},{4,5},{5,4},{6,7},{7,6},{8,9},{9,8},{10,11... | collective-permute-start | bytes 2654216 | tf_op jit(solution)/shard_map/ppermute | solution.py:389
  103.8 32.5 %collective-permute-start.39 = (bf16[2048,512]{1,0:T(8,128)(2,1)S(1)}, bf16[2048,512]{1,0:T(8,128)(2,1)}, u32[]{:S(2)}, u32[]{:S(2)}) collective-permute-start(bf16[2048,512]{1,0:T(8,128)(2,1)S(1)} %copy-done.2), channel_id=1, source_target_pairs={{0,1},{1,0},{2,3},{3,2},{4,5},{5,4},{6,7},{7,6},{8,9},{9,8},{10,11... | collective-permute-start | bytes 6291464 | tf_op jit(solution)/shard_map/ppermute | solution.py:389
  104.3 23.2 %collective-permute-start.37 = (bf16[1024,512]{1,0:T(8,128)(2,1)}, bf16[1024,512]{1,0:T(8,128)(2,1)}, u32[]{:S(2)}, u32[]{:S(2)}) collective-permute-start(bf16[1024,512]{1,0:T(8,128)(2,1)} %core_half.2), channel_id=1, source_target_pairs={{0,16},{1,9},{2,18},{3,11},{4,20},{5,13},{6,22},{7,15},{8,24},{9,1... | collective-permute-start | bytes 3145736 | tf_op jit(solution)/shard_map/ppermute | solution.py:429
  127.5 8.8 %collective-permute-start.40 = (bf16[1024,512]{1,0:T(8,128)(2,1)}, bf16[1024,512]{1,0:T(8,128)(2,1)}, u32[]{:S(2)}, u32[]{:S(2)}) collective-permute-start(bf16[1024,512]{1,0:T(8,128)(2,1)} %collective-permute-done.37.refs_11_), channel_id=1, source_target_pairs={{0,1},{1,0},{2,3},{3,2},{4,5},{5,4},{6,7},{7,6},{8,9},{9,8},{10,11... | collective-permute-start | bytes 3145736 | tf_op jit(solution)/shard_map/ppermute | solution.py:389
  135.3 26.4 %collective-permute-start.38 = (bf16[1024,512]{1,0:T(8,128)(2,1)}, bf16[1024,512]{1,0:T(8,128)(2,1)S(1)}, u32[]{:S(2)}, u32[]{:S(2)}) collective-permute-start(bf16[1024,512]{1,0:T(8,128)(2,1)} %core_half.3), channel_id=1, source_target_pairs={{0,16},{1,9},{2,18},{3,11},{4,20},{5,13},{6,22},{7,15},{8,24},{9,1... | collective-permute-start | bytes 3145736 | tf_op jit(solution)/shard_map/ppermute | solution.py:429
  135.4 33.8 %collective-permute-start.42 = (bf16[2048,512]{1,0:T(8,128)(2,1)}, bf16[2048,512]{1,0:T(8,128)(2,1)}, u32[]{:S(2)}, u32[]{:S(2)}) collective-permute-start(bf16[2048,512]{1,0:T(8,128)(2,1)} %all-gather.13.cloned.1.call-done.refs_8_), channel_id=1, source_target_pairs={{0,8},{1,17},{2,10},{3,19},{4,12},{5,21},{6,14},{7,23},{8,0},{9,25... | collective-permute-start | bytes 6291464 | tf_op jit(solution)/shard_map/ppermute | solution.py:429
  136.3 35.0 %collective-permute-start.43 = (bf16[2048,512]{1,0:T(8,128)(2,1)}, bf16[2048,512]{1,0:T(8,128)(2,1)}, u32[]{:S(2)}, u32[]{:S(2)}) collective-permute-start(bf16[2048,512]{1,0:T(8,128)(2,1)} %collective-permute-done.36.value_ref.refs_9_), channel_id=1, source_target_pairs={{0,1},{1,0},{2,3},{3,2},{4,5},{5,4},{6,7},{7,6},{8,9},{9,8},{10,11... | collective-permute-start | bytes 6291464 | tf_op jit(solution)/shard_map/ppermute | solution.py:389
  161.7 9.6 %copy-start.7 = (bf16[1024,512]{1,0:T(8,128)(2,1)}, bf16[1024,512]{1,0:T(8,128)(2,1)S(1)}, u32[]{:S(2)}) copy-start(bf16[1024,512]{1,0:T(8,128)(2,1)S(1)} %collective-permute-done.38.refs_11_) | copy-start | bytes 3145732
  161.7 31.8 %collective-permute-start.41 = (bf16[2048,512]{1,0:T(8,128)(2,1)}, bf16[2048,512]{1,0:T(8,128)(2,1)S(1)}, u32[]{:S(2)}, u32[]{:S(2)}) collective-permute-start(bf16[2048,512]{1,0:T(8,128)(2,1)} %all-gather.11.cloned.1.call-done.refs_3_), channel_id=1, source_target_pairs={{0,8},{1,17},{2,10},{3,19},{4,12},{5,21},{6,14},{7,23},{8,0},{9,25... | collective-permute-start | bytes 6291464 | tf_op jit(solution)/shard_map/ppermute | solution.py:429
  162.6 7.7 %collective-permute-start.44 = (bf16[1024,512]{1,0:T(8,128)(2,1)S(1)}, bf16[1024,512]{1,0:T(8,128)(2,1)S(1)}, u32[]{:S(2)}, u32[]{:S(2)}) collective-permute-start(bf16[1024,512]{1,0:T(8,128)(2,1)S(1)} %collective-permute-done.38.refs_11_), channel_id=1, source_target_pairs={{0,1},{1,0},{2,3},{3,2},{4,5},{5,4},{6,7},{7,6},{8,9},{9,8},{10,11... | collective-permute-start | bytes 3145736 | tf_op jit(solution)/shard_map/ppermute | solution.py:389
  169.2 25.6 %collective-permute-start.45 = (bf16[2048,512]{1,0:T(8,128)(2,1)}, bf16[2048,512]{1,0:T(8,128)(2,1)}, u32[]{:S(2)}, u32[]{:S(2)}) collective-permute-start(bf16[2048,512]{1,0:T(8,128)(2,1)} %collective-permute-done.42.refs_9_), channel_id=1, source_target_pairs={{0,1},{1,0},{2,3},{3,2},{4,5},{5,4},{6,7},{7,6},{8,9},{9,8},{10,11... | collective-permute-start | bytes 6291464 | tf_op jit(solution)/shard_map/ppermute | solution.py:389
  170.3 1.0 copy-start.8
  193.5 22.5 %copy-start.6 = (bf16[2048,512]{1,0:T(8,128)(2,1)}, bf16[2048,512]{1,0:T(8,128)(2,1)S(1)}, u32[]{:S(2)}) copy-start(bf16[2048,512]{1,0:T(8,128)(2,1)S(1)} %collective-permute-done.41.refs_4_) | copy-start | bytes 6291460
  193.6 22.6 %collective-permute-start.46 = (bf16[2048,512]{1,0:T(8,128)(2,1)S(1)}, bf16[2048,512]{1,0:T(8,128)(2,1)}, u32[]{:S(2)}, u32[]{:S(2)}) collective-permute-start(bf16[2048,512]{1,0:T(8,128)(2,1)S(1)} %collective-permute-done.41.refs_4_), channel_id=1, source_target_pairs={{0,1},{1,0},{2,3},{3,2},{4,5},{5,4},{6,7},{7,6},{8,9},{9,8},{10,11... | collective-permute-start | bytes 6291464 | tf_op jit(solution)/shard_map/ppermute | solution.py:389
Sparse Core Ops, SparseCore 0:
  24.3 27.7 all-gather.6
  53.7 30.4 all-gather.8
  85.8 28.1 all-gather.12
  115.5 28.5 all-gather.10
  145.5 29.0 all-gather.14
  176.0 28.1 all-gather.16

commit v2 on v1

--- a/solution.py
+++ b/solution.py
@@ -15,11 +15,11 @@
 masked_score = -1e30
 lanes = 128
 mode_group = 8
-chunk_rows = 16
 seq_far = 2
 head_batch = 8
 vector_rows = 4
 row_tile = 16
+chunk_rows = row_tile
 
 
 def mixer_tables(rate_now, angle_now, coef_now, skip_now, vectors):
@@ -89,7 +89,12 @@
     heads = width // HEAD_DIM
     tiles = rows // row_tile
     first_chunk = broken_ref[rows // chunk_rows]
-    first_tile = first_chunk // (2 * row_tile // chunk_rows) * 2
+    first_tile = first_chunk // 2 * 2
+
+    @pl.when(first_chunk > first_tile)
+    def _():
+        blank = pl.ds(pl.multiple_of(first_tile * row_tile * folds, row_tile * folds), row_tile * folds)
+        mixed[blank, :] = jnp.zeros((row_tile * folds, lanes), jnp.float32)
 
     def gain(row, fold):
         return zero_ref[2 * modes + row, fold : fold + 1, :]

time: 228 us -> 231 us (1.013)
  the two profiles are of different devices: /device:TPU:24 before, /device:TPU:23 now
where the time goes in v2:
time: 231 us; the launch traced here: 230 us
  Pallas kernels  100 us (43%)
  waiting for transfers between devices  47.7 us (21%)
  starting transfers between devices  41.2 us (18%)
  between operations  19 us (8%)
  other arithmetic  13.9 us (6%)
  local copies, waits for them, and re-layouts  8.35 us (4%)
    pallas_call x5, Pallas kernels, section_step(): pl.pallas_call(functools.partial(section_kernel, wholes_count, halves_cou...  94.7 us
    ppermute x6, waiting for transfers between devices, spread_quarters(): held.append(lax.ppermute(columns(hops), 'pipe', pairs))  18.6 us
    ppermute x7, starting transfers between devices, swapped(): return lax.ppermute(value, 'seq', [(i, i ^ 1) for i in range(count)])  12.2 us
    ppermute x1, waiting for transfers between devices, mover(): return lambda held: lax.ppermute(held, 'pipe', pairs)  11.4 us
    ppermute x3, waiting for transfers between devices, across(): return lax.ppermute(value, 'pipe', [(i, i ^ hops) for i in range(count)])  8.73 us
    ppermute x1, starting transfers between devices, local(): lax.ppermute(own, 'seq', [(i, i + 1) for i in range(seq_count - 1)])  8.31 us
    ppermute x6, starting transfers between devices, spread_quarters(): held.append(lax.ppermute(columns(hops), 'pipe', pairs))  7.8 us
    ppermute x6, starting transfers between devices, sent_by_core(): return lax.ppermute(value, ('pipe', 'seq'), pairs)  6.85 us
  transfers between devices with their start and end apart: 30, of which 9 were waited for; matrix products, arithmetic and copies ran while one was open for 7% of the time, Pallas kernels for 41%

profile of v2, /device:TPU:23, one launch (start us, length us, event | category | flops | bytes accessed | tf_op | source)
XLA Modules:
  0.0 230.2 jit_solution(7483366647132279429)
XLA Ops:
  6.6 1.4 constant_dynamic-slice_fusion.3
  8.0 0.3 collective-permute-start.24
  8.3 0.2 collective-permute-start.25
  8.6 2.2 collective-permute-start.26
  10.8 0.5 multiply_bitcast_fusion.1
  11.7 3.6 %collective-permute-done.24 = bf16[256,512]{1,0:T(8,128)(2,1)S(1)} collective-permute-done((bf16[256,512]{1,0:T(8,128)(2,1)S(1)}, bf16[256,512]{1,0:T(8,128)(2,1)S(1)}, u32[]{:S(2)}, u32[]{:S(2)}) %collective-permute-start.24) | collective-permute-done | bytes 262176 | tf_op jit(solution)/shard_map/ppermute | solution.py:408
  15.2 5.6 %collective-permute-done.26 = bf16[256,512]{1,0:T(8,128)(2,1)S(1)} collective-permute-done((bf16[256,512]{1,0:T(8,128)(2,1)S(1)}, bf16[256,512]{1,0:T(8,128)(2,1)S(1)}, u32[]{:S(2)}, u32[]{:S(2)}) %collective-permute-start.26) | collective-permute-done | bytes 262176 | tf_op jit(solution)/shard_map/ppermute | solution.py:408
  20.9 0.1 pad_maximum_fusion.2
  21.0 1.0 dynamic-slice_bitcast_fusion.4
  22.2 0.7 all-gather.9.cloned.1.call-update
  22.9 0.7 all-gather.13.cloned.1.call-update
  23.6 0.5 all-gather.11.cloned.1.call-update
  24.3 0.7 iota_reduce_fusion
  25.6 14.5 %conditional.1 = (bf16[128,2048]{1,0:T(8,128)(2,1)}) conditional(s32[]{:T(128)} %clamp.3, bf16[128,2048]{1,0:T(8,128)(2,1)S(1)} %bitcast.143, bf16[128,2048]{1,0:T(8,128)(2,1)S(1)} %bitcast.133, bf16[128,2048]{1,0:T(8,128)(2,1)S(1)} %bitcast.134, bf16[128,2048]{1,0:T(8,128)(2,1)S(1)} %bitcast.135, ...), branch_computations={%region_6.7_spmd, %region_7.8_spmd, %region_8.9_spmd, %region_9.10... | conditional | bytes 2097200 | solution.py:451
  25.7 3.1 %collective-permute-start.11 = (bf16[128,2048]{1,0:T(8,128)(2,1)S(1)}, bf16[128,2048]{1,0:T(8,128)(2,1)}, u32[]{:S(2)}, u32[]{:S(2)}) collective-permute-start(bf16[128,2048]{1,0:T(8,128)(2,1)S(1)} %param.11), channel_id=1, source_target_pairs={{8,0},{24,8},{16,16},{0,24},{9,1},{25,9},{17,17},{1,25},{10,2},{26... | collective-permute-start | bytes 1572872 | tf_op jit(solution)/shard_map/cond/branch_11_fun/ppermute | solution.py:449
  28.8 11.4 %collective-permute-done.11 = bf16[128,2048]{1,0:T(8,128)(2,1)} collective-permute-done((bf16[128,2048]{1,0:T(8,128)(2,1)S(1)}, bf16[128,2048]{1,0:T(8,128)(2,1)}, u32[]{:S(2)}, u32[]{:S(2)}) %collective-permute-start.11) | collective-permute-done | bytes 524320 | tf_op jit(solution)/shard_map/cond/branch_11_fun/ppermute | solution.py:449
  40.3 0.6 collective-permute-start.28
  40.9 2.0 collective-permute-start.29
  42.9 3.3 %collective-permute-done.27 = f32[36,16,128]{2,1,0:T(8,128)S(1)} collective-permute-done((f32[36,16,128]{2,1,0:T(8,128)S(1)}, f32[36,16,128]{2,1,0:T(8,128)S(1)}, u32[]{:S(2)}, u32[]{:S(2)}) %collective-permute-start.27) | collective-permute-done | bytes 294944 | tf_op jit(solution)/shard_map/ppermute | solution.py:389
  46.3 0.6 copy-done.9
  47.0 0.7 copy-done.11
  47.7 5.3 %collective-permute-done.29 = f32[36,16,128]{2,1,0:T(8,128)} collective-permute-done((f32[36,16,128]{2,1,0:T(8,128)S(1)}, f32[36,16,128]{2,1,0:T(8,128)}, u32[]{:S(2)}, u32[]{:S(2)}) %collective-permute-start.29) | collective-permute-done | bytes 294944 | tf_op jit(solution)/shard_map/ppermute | solution.py:389
  53.0 0.4 all-gather.7.cloned.1.call-done.refs_8_
  53.4 0.3 collective-permute-start.30
  53.7 0.6 dynamic_slice.63
  56.4 0.1 reduce.36
  56.6 0.6 slice.20
  57.2 1.3 compare_reduce_fusion.1
  60.8 1.0 dynamic-slice_bitcast_fusion.3
  61.8 2.2 collective-permute-start.32
  63.9 1.6 collective-permute-start.33
  65.5 1.3 collective-permute-start.34
  66.9 8.3 %collective-permute-start.31 = (bf16[128,2048]{1,0:T(8,128)(2,1)}, bf16[128,2048]{1,0:T(8,128)(2,1)}, u32[]{:S(2)}, u32[]{:S(2)}) collective-permute-start(bf16[128,2048]{1,0:T(8,128)(2,1)} %get-tuple-element.206.refs_7_), channel_id=1, source_target_pairs={{0,1},{1,2},{2,3},{3,4},{4,5},{5,6},{6,7},{8,9},{9,10},{10,11},{11... | collective-permute-start | bytes 1572872 | tf_op jit(solution)/shard_map/ppermute | solution.py:480
  75.3 0.7 fusion.6
  76.0 0.1 reduce_or.9
  76.2 9.4 %collective-permute-done.33 = bf16[256,512]{1,0:T(8,128)(2,1)S(1)} collective-permute-done((bf16[256,512]{1,0:T(8,128)(2,1)}, bf16[256,512]{1,0:T(8,128)(2,1)S(1)}, u32[]{:S(2)}, u32[]{:S(2)}) %collective-permute-start.33) | collective-permute-done | bytes 262176 | tf_op jit(solution)/shard_map/ppermute | solution.py:408
  85.6 0.1 pad_maximum_fusion.3
  85.8 0.9 dynamic-slice_bitcast_fusion.1
  86.6 1.9 collective-permute-start.36
  88.6 0.7 pad_add_fusion.1.place_ref.refs_0_
  89.2 0.5 compare_select_fusion.refs_4_
  89.7 2.7 %core_half.2 = bf16[1024,512]{1,0:T(8,128)(2,1)} custom-call(s32[2]{0:T(128)} %pad_add_fusion.1.place_ref.refs_0_, bf16[2048,512]{1,0:T(8,128)(2,1)} %copy-done.1), custom_call_target="tpu_custom_call" | custom-call | tf_op jit(solution)/shard_map/core_half/pallas_call | solution.py:367
  92.5 2.6 %fusion.8 = (f32[3,1,36,16,128]{4,3,2,1,0:T(8,128)}, f32[3,36,16,128]{3,2,1,0:T(8,128)}) fusion(f32[1,36,16,128]{3,2,1,0:T(8,128)} %bitcast.34, f32[1,36,16,128]{3,2,1,0:T(8,128)} %bitcast.119, f32[1,36,16,128]{3,2,1,0:T(8,128)S(1)} %bitcast.118), kind=kLoop, calls=%fused_computation.61 | loop fusion | flops 442368 | bytes 2654208 | tf_op jit(solution)/shard_map/stack | solution.py:424
  95.1 6.8 %collective-permute-start.35 = (f32[3,36,16,128]{3,2,1,0:T(8,128)}, f32[3,36,16,128]{3,2,1,0:T(8,128)}, u32[]{:S(2)}, u32[]{:S(2)}) collective-permute-start(f32[3,36,16,128]{3,2,1,0:T(8,128)} %get-tuple-element.193), channel_id=1, source_target_pairs={{0,1},{1,0},{2,3},{3,2},{4,5},{5,4},{6,7},{7,6},{8,9},{9,8},{10,11... | collective-permute-start | bytes 2654216 | tf_op jit(solution)/shard_map/ppermute | solution.py:394
  101.9 0.6 pad_add_fusion.7
  102.5 0.7 pad_add_fusion.6
  103.2 1.6 collective-permute-start.37
  104.8 0.7 pad_add_fusion.4.refs_2_
  105.4 0.1 copy.18
  105.6 0.7 fusion.4.refs_3_
  106.3 1.7 pad_maximum_fusion.1
  108.0 1.7 pad_maximum_fusion.refs_5_
  109.7 19.5 %section_step.5 = (bf16[256,2048]{1,0:T(8,128)(2,1)}, bf16[256,2048]{1,0:T(8,128)(2,1)}) custom-call(s32[4]{0:T(128)} %get-tuple-element.202.refs_0_, f32[256]{0:T(256)} %get-tuple-element.205.refs_1_, s32[17]{0:T(128)} %pad_add_fusion.4.refs_2_, s32[256,1]{1,0:T(8,128)} %fusion.4.refs_3_, s32[1,256]{1,0:T(1,128)} %compare_select_fusion.refs_4_, ...), custom_call_target="tpu_custom_call" | custom-call | flops 2147483648 | bytes 8388608 | tf_op jit(solution)/shard_map/section_step/pallas_call | solution.py:332
  129.3 2.6 %core_half.3 = bf16[1024,512]{1,0:T(8,128)(2,1)} custom-call(s32[2]{0:T(128)} %pad_add_fusion.1.place_ref.refs_0_, bf16[2048,512]{1,0:T(8,128)(2,1)} %collective-permute-done.36.value_ref.refs_9_), custom_call_target="tpu_custom_call" | custom-call | tf_op jit(solution)/shard_map/core_half/pallas_call | solution.py:367
  131.9 1.1 collective-permute-start.38
  133.0 2.0 collective-permute-start.42
  135.0 4.3 %collective-permute-start.43 = (bf16[2048,512]{1,0:T(8,128)(2,1)}, bf16[2048,512]{1,0:T(8,128)(2,1)}, u32[]{:S(2)}, u32[]{:S(2)}) collective-permute-start(bf16[2048,512]{1,0:T(8,128)(2,1)} %collective-permute-done.36.value_ref.refs_9_), channel_id=1, source_target_pairs={{0,1},{1,0},{2,3},{3,2},{4,5},{5,4},{6,7},{7,6},{8,9},{9,8},{10,11... | collective-permute-start | bytes 6291464 | tf_op jit(solution)/shard_map/ppermute | solution.py:394
  139.3 23.3 %section_step.6 = (bf16[256,2048]{1,0:T(8,128)(2,1)}, bf16[256,2048]{1,0:T(8,128)(2,1)}) custom-call(s32[4]{0:T(128)} %get-tuple-element.201.refs_0_, f32[256]{0:T(256)} %get-tuple-element.205.refs_1_, s32[17]{0:T(128)} %pad_add_fusion.4.refs_2_, s32[256,1]{1,0:T(8,128)} %fusion.4.refs_3_, s32[1,256]{1,0:T(1,128)} %compare_select_fusion.refs_4_, ...), custom_call_target="tpu_custom_call" | custom-call | flops 2147483648 | bytes 8388608 | tf_op jit(solution)/shard_map/section_step/pallas_call | solution.py:332
  162.8 0.9 collective-permute-start.44
  163.7 6.4 %collective-permute-done.42.refs_9_ = bf16[2048,512]{1,0:T(8,128)(2,1)} collective-permute-done((bf16[2048,512]{1,0:T(8,128)(2,1)}, bf16[2048,512]{1,0:T(8,128)(2,1)}, u32[]{:S(2)}, u32[]{:S(2)}) %collective-permute-start.42) | collective-permute-done | bytes 2097184 | tf_op jit(solution)/shard_map/ppermute | solution.py:434
  170.2 1.0 copy-done.8
  171.2 23.5 %section_step.7 = (bf16[256,2048]{1,0:T(8,128)(2,1)}, bf16[256,2048]{1,0:T(8,128)(2,1)}) custom-call(s32[4]{0:T(128)} %get-tuple-element.176.refs_0_, f32[256]{0:T(256)} %get-tuple-element.205.refs_1_, s32[17]{0:T(128)} %pad_add_fusion.4.refs_2_, s32[256,1]{1,0:T(8,128)} %fusion.4.refs_3_, s32[1,256]{1,0:T(1,128)} %compare_select_fusion.refs_4_, ...), custom_call_target="tpu_custom_call" | custom-call | flops 2147483648 | bytes 8388608 | tf_op jit(solution)/shard_map/section_step/pallas_call | solution.py:332
  194.8 22.6 %section_step.8 = (bf16[128,2048]{1,0:T(8,128)(2,1)}, bf16[128,2048]{1,0:T(8,128)(2,1)}) custom-call(s32[4]{0:T(128)} %get-tuple-element.203.refs_0_, f32[256]{0:T(256)} %get-tuple-element.205.refs_1_, s32[17]{0:T(128)} %pad_add_fusion.4.refs_2_, s32[256,1]{1,0:T(8,128)} %fusion.4.refs_3_, s32[1,256]{1,0:T(1,128)} %compare_select_fusion.refs_4_, ...), custom_call_target="tpu_custom_call" | custom-call | flops 2147483648 | bytes 8388608 | tf_op jit(solution)/shard_map/section_step/pallas_call | solution.py:332
  217.5 5.8 %section_step.9 = bf16[128,2048]{1,0:T(8,128)(2,1)} custom-call(s32[2]{0:T(128)} %pad_add_fusion.1.place_ref.refs_0_, bf16[128,2048]{1,0:T(8,128)(2,1)} %get-tuple-element.172.refs_1_, bf16[128,2048]{1,0:T(8,128)(2,1)} %get-tuple-element.173.refs_2_, bf16[2048,512]{1,0:T(8,128)(2,1)} %all-gather.11.cloned.1.call-done.refs_3_, bf16[2048,512]{1,0:T(8,128)(2,1)} %copy-done.6, ...), custom_call_target="tpu_custom_call" | custom-call | flops 1073741824 | bytes 8388608 | tf_op jit(solution)/shard_map/section_step/pallas_call | solution.py:332
  (101 shorter events, 1.7 us)
Async XLA Ops:
  6.5 49.7 %copy-start = (s32[4,32]{1,0:T(4,128)S(1)}, s32[4,32]{1,0:T(4,128)}, u32[]{:S(2)}) copy-start(s32[4,32]{1,0:T(4,128)} %param.36) | copy-start | bytes 1540
  6.5 4.2 %copy-start.12 = (f32[1,2,16,2048]{3,2,1,0:T(8,128)S(1)}, f32[1,2,16,2048]{3,2,1,0:T(8,128)}, u32[]{:S(2)}) copy-start(f32[1,2,16,2048]{3,2,1,0:T(8,128)} %param.41) | copy-start | bytes 786436
  6.5 4.3 %copy-start.14 = (f32[1,16,2048]{2,1,0:T(8,128)S(1)}, f32[1,16,2048]{2,1,0:T(8,128)}, u32[]{:S(2)}) copy-start(f32[1,16,2048]{2,1,0:T(8,128)} %param.39) | copy-start | bytes 393220
  6.5 4.3 %copy-start.13 = (f32[1,16,2048]{2,1,0:T(8,128)S(1)}, f32[1,16,2048]{2,1,0:T(8,128)}, u32[]{:S(2)}) copy-start(f32[1,16,2048]{2,1,0:T(8,128)} %param.40) | copy-start | bytes 393220
  6.5 46.9 %all-gather.7.cloned.1.call-start = ((), (), s32[]{:S(2)}) async-start(), calls=%async_computation | async-start | bytes 2359296 | tf_op jit(solution)/shard_map/all_gather | solution.py:472
  8.0 3.5 %copy-start.17 = (f32[1,2048]{1,0:T(1,128)S(1)}, f32[1,2048]{1,0:T(1,128)}, u32[]{:S(2)}) copy-start(f32[1,2048]{1,0:T(1,128)} %param.38) | copy-start | bytes 24580
  8.0 3.5 %copy-start.16 = (f32[1,2,2048]{2,1,0:T(2,128)S(1)}, f32[1,2,2048]{2,1,0:T(2,128)}, u32[]{:S(2)}) copy-start(f32[1,2,2048]{2,1,0:T(2,128)} %param.43) | copy-start | bytes 49156
  8.0 3.6 %copy-start.15 = (f32[1,2048]{1,0:T(1,128)S(1)}, f32[1,2048]{1,0:T(1,128)}, u32[]{:S(2)}) copy-start(f32[1,2048]{1,0:T(1,128)} %param.42) | copy-start | bytes 24580
  8.0 7.2 %collective-permute-start.24 = (bf16[256,512]{1,0:T(8,128)(2,1)S(1)}, bf16[256,512]{1,0:T(8,128)(2,1)S(1)}, u32[]{:S(2)}, u32[]{:S(2)}) collective-permute-start(bf16[256,512]{1,0:T(8,128)(2,1)S(1)} %get-tuple-element.190), channel_id=1, source_target_pairs={{0,8},{8,0},{16,24},{24,16},{1,9},{9,1},{17,25},{25,17},{2,10},{10... | collective-permute-start | bytes 786440 | tf_op jit(solution)/shard_map/ppermute | solution.py:408
  8.3 6.9 %collective-permute-start.25 = (bf16[256,512]{1,0:T(8,128)(2,1)S(1)}, bf16[256,512]{1,0:T(8,128)(2,1)S(1)}, u32[]{:S(2)}, u32[]{:S(2)}) collective-permute-start(bf16[256,512]{1,0:T(8,128)(2,1)S(1)} %get-tuple-element.189), channel_id=1, source_target_pairs={{0,16},{8,24},{16,0},{24,8},{1,17},{9,25},{17,1},{25,9},{2,18},{10... | collective-permute-start | bytes 786440 | tf_op jit(solution)/shard_map/ppermute | solution.py:408
  8.6 12.3 %collective-permute-start.26 = (bf16[256,512]{1,0:T(8,128)(2,1)S(1)}, bf16[256,512]{1,0:T(8,128)(2,1)S(1)}, u32[]{:S(2)}, u32[]{:S(2)}) collective-permute-start(bf16[256,512]{1,0:T(8,128)(2,1)S(1)} %get-tuple-element.191), channel_id=1, source_target_pairs={{0,24},{8,16},{16,8},{24,0},{1,25},{9,17},{17,9},{25,1},{2,26},{10... | collective-permute-start | bytes 786440 | tf_op jit(solution)/shard_map/ppermute | solution.py:408
  11.7 28.5 %copy-start.4 = (f32[2,36,16,128]{3,2,1,0:T(8,128)}, f32[2,36,16,128]{3,2,1,0:T(8,128)S(1)}, u32[]{:S(2)}) copy-start(f32[2,36,16,128]{3,2,1,0:T(8,128)S(1)} %pad_maximum_fusion.5) | copy-start | bytes 1769476
  21.0 3.2 %copy-start.18 = (s32[24,4]{0,1:T(4,128)S(1)}, s32[24,4]{0,1:T(4,128)}, u32[]{:S(2)}) copy-start(s32[24,4]{0,1:T(4,128)} %constant.115.clone) | copy-start | bytes 1156
  21.0 3.2 %copy-start.19 = (s32[4]{0:T(128)S(1)}, s32[4]{0:T(128)}, u32[]{:S(2)}) copy-start(s32[4]{0:T(128)} %param.37) | copy-start | bytes 52
  21.0 4.6 %copy-start.20 = (bf16[1,128,2048]{2,1,0:T(8,128)(2,1)S(1)}, bf16[1,128,2048]{2,1,0:T(8,128)(2,1)}, u32[]{:S(2)}) copy-start(bf16[1,128,2048]{2,1,0:T(8,128)(2,1)} %param.35) | copy-start | bytes 1572868
  21.0 39.8 %copy-start.3 = (bf16[1,256,2048]{2,1,0:T(8,128)(2,1)S(1)}, bf16[1,256,2048]{2,1,0:T(8,128)(2,1)}, u32[]{:S(2)}) copy-start(bf16[1,256,2048]{2,1,0:T(8,128)(2,1)} %param.44) | copy-start | bytes 3145732
  22.1 64.5 %all-gather.9.cloned.1.call-start = ((), (), s32[]{:S(2)}) async-start(), calls=%async_computation.1 | async-start | bytes 2359296 | tf_op jit(solution)/shard_map/all_gather | solution.py:472
  22.9 106.4 %all-gather.13.cloned.1.call-start = ((), (), s32[]{:S(2)}) async-start(), calls=%async_computation.3 | async-start | bytes 2359296 | tf_op jit(solution)/shard_map/all_gather | solution.py:472
  23.6 139.1 %all-gather.11.cloned.1.call-start = ((), (), s32[]{:S(2)}) async-start(), calls=%async_computation.2 | async-start | bytes 2359296 | tf_op jit(solution)/shard_map/all_gather | solution.py:472
  24.2 170.6 %all-gather.15.cloned.1.call-start = ((), (), s32[]{:S(2)}) async-start(), calls=%async_computation.4 | async-start | bytes 2359296 | tf_op jit(solution)/shard_map/all_gather | solution.py:472
  25.7 14.5 %collective-permute-start.11 = (bf16[128,2048]{1,0:T(8,128)(2,1)S(1)}, bf16[128,2048]{1,0:T(8,128)(2,1)}, u32[]{:S(2)}, u32[]{:S(2)}) collective-permute-start(bf16[128,2048]{1,0:T(8,128)(2,1)S(1)} %param.11), channel_id=1, source_target_pairs={{8,0},{24,8},{16,16},{0,24},{9,1},{25,9},{17,17},{1,25},{10,2},{26... | collective-permute-start | bytes 1572872 | tf_op jit(solution)/shard_map/cond/branch_11_fun/ppermute | solution.py:449
  40.2 6.0 %collective-permute-start.27 = (f32[36,16,128]{2,1,0:T(8,128)S(1)}, f32[36,16,128]{2,1,0:T(8,128)S(1)}, u32[]{:S(2)}, u32[]{:S(2)}) collective-permute-start(f32[36,16,128]{2,1,0:T(8,128)S(1)} %dynamic-slice_bitcast_fusion), channel_id=1, source_target_pairs={{0,8},{8,0},{16,24},{24,16},{1,9},{9,1},{17,25},{25,17},{2,10},{10... | collective-permute-start | bytes 884744 | tf_op jit(solution)/shard_map/ppermute | solution.py:389
  40.3 6.0 %collective-permute-start.28 = (f32[36,16,128]{2,1,0:T(8,128)S(1)}, f32[36,16,128]{2,1,0:T(8,128)S(1)}, u32[]{:S(2)}, u32[]{:S(2)}) collective-permute-start(f32[36,16,128]{2,1,0:T(8,128)S(1)} %dynamic-slice_bitcast_fusion), channel_id=1, source_target_pairs={{0,16},{8,24},{16,0},{24,8},{1,17},{9,25},{17,1},{25,9},{2,18},{10... | collective-permute-start | bytes 884744 | tf_op jit(solution)/shard_map/ppermute | solution.py:389
  40.9 12.1 %collective-permute-start.29 = (f32[36,16,128]{2,1,0:T(8,128)S(1)}, f32[36,16,128]{2,1,0:T(8,128)}, u32[]{:S(2)}, u32[]{:S(2)}) collective-permute-start(f32[36,16,128]{2,1,0:T(8,128)S(1)} %dynamic-slice_bitcast_fusion), channel_id=1, source_target_pairs={{0,24},{8,16},{16,8},{24,0},{1,25},{9,17},{17,9},{25,1},{2,26},{10... | collective-permute-start | bytes 884744 | tf_op jit(solution)/shard_map/ppermute | solution.py:389
  46.2 0.7 copy-start.9
  47.0 0.7 copy-start.11
  53.4 33.2 %collective-permute-start.30 = (bf16[2048,512]{1,0:T(8,128)(2,1)}, bf16[2048,512]{1,0:T(8,128)(2,1)S(1)}, u32[]{:S(2)}, u32[]{:S(2)}) collective-permute-start(bf16[2048,512]{1,0:T(8,128)(2,1)} %all-gather.7.cloned.1.call-done.refs_8_), channel_id=1, source_target_pairs={{0,8},{1,17},{2,10},{3,19},{4,12},{5,21},{6,14},{7,23},{8,0},{9,25... | collective-permute-start | bytes 6291464 | tf_op jit(solution)/shard_map/ppermute | solution.py:434
  61.8 14.4 %collective-permute-start.32 = (bf16[256,512]{1,0:T(8,128)(2,1)}, bf16[256,512]{1,0:T(8,128)(2,1)S(1)}, u32[]{:S(2)}, u32[]{:S(2)}) collective-permute-start(bf16[256,512]{1,0:T(8,128)(2,1)} %get-tuple-element.183), channel_id=1, source_target_pairs={{16,24},{24,16},{17,25},{25,17},{18,26},{26,18},{19,27},{27,19},{2... | collective-permute-start | bytes 786440 | tf_op jit(solution)/shard_map/ppermute | solution.py:408
  63.9 21.7 %collective-permute-start.33 = (bf16[256,512]{1,0:T(8,128)(2,1)}, bf16[256,512]{1,0:T(8,128)(2,1)S(1)}, u32[]{:S(2)}, u32[]{:S(2)}) collective-permute-start(bf16[256,512]{1,0:T(8,128)(2,1)} %get-tuple-element.182), channel_id=1, source_target_pairs={{16,0},{24,8},{17,1},{25,9},{18,2},{26,10},{19,3},{27,11},{20,4},{... | collective-permute-start | bytes 786440 | tf_op jit(solution)/shard_map/ppermute | solution.py:408
  65.5 20.1 %collective-permute-start.34 = (bf16[256,512]{1,0:T(8,128)(2,1)}, bf16[256,512]{1,0:T(8,128)(2,1)S(1)}, u32[]{:S(2)}, u32[]{:S(2)}) collective-permute-start(bf16[256,512]{1,0:T(8,128)(2,1)} %get-tuple-element.181), channel_id=1, source_target_pairs={{16,8},{24,0},{17,9},{25,1},{18,10},{26,2},{19,11},{27,3},{20,12},... | collective-permute-start | bytes 786440 | tf_op jit(solution)/shard_map/ppermute | solution.py:408
  66.9 19.8 %collective-permute-start.31 = (bf16[128,2048]{1,0:T(8,128)(2,1)}, bf16[128,2048]{1,0:T(8,128)(2,1)}, u32[]{:S(2)}, u32[]{:S(2)}) collective-permute-start(bf16[128,2048]{1,0:T(8,128)(2,1)} %get-tuple-element.206.refs_7_), channel_id=1, source_target_pairs={{0,1},{1,2},{2,3},{3,4},{4,5},{5,6},{6,7},{8,9},{9,10},{10,11},{11... | collective-permute-start | bytes 1572872 | tf_op jit(solution)/shard_map/ppermute | solution.py:480
  85.7 6.7 %copy-start.10 = (f32[36,16,128]{2,1,0:T(8,128)S(1)}, f32[36,16,128]{2,1,0:T(8,128)}, u32[]{:S(2)}) copy-start(f32[36,16,128]{2,1,0:T(8,128)} %copy-done.9) | copy-start | bytes 884740
  86.6 3.1 %copy-start.1 = (bf16[2048,512]{1,0:T(8,128)(2,1)}, bf16[2048,512]{1,0:T(8,128)(2,1)S(1)}, u32[]{:S(2)}) copy-start(bf16[2048,512]{1,0:T(8,128)(2,1)S(1)} %collective-permute-done.30.value_ref.refs_9_) | copy-start | bytes 6291460
  86.6 42.6 %collective-permute-start.36 = (bf16[2048,512]{1,0:T(8,128)(2,1)}, bf16[2048,512]{1,0:T(8,128)(2,1)}, u32[]{:S(2)}, u32[]{:S(2)}) collective-permute-start(bf16[2048,512]{1,0:T(8,128)(2,1)} %all-gather.9.cloned.1.call-done.refs_8_), channel_id=1, source_target_pairs={{0,8},{1,17},{2,10},{3,19},{4,12},{5,21},{6,14},{7,23},{8,0},{9,25... | collective-permute-start | bytes 6291464 | tf_op jit(solution)/shard_map/ppermute | solution.py:434
  88.5 129.0 %all-gather.17.cloned.1.call-start = ((), (), s32[]{:S(2)}) async-start(), calls=%async_computation.5 | async-start | bytes 2359296 | tf_op jit(solution)/shard_map/all_gather | solution.py:472
  92.4 10.7 %copy-start.2 = (bf16[2048,512]{1,0:T(8,128)(2,1)S(1)}, bf16[2048,512]{1,0:T(8,128)(2,1)}, u32[]{:S(2)}) copy-start(bf16[2048,512]{1,0:T(8,128)(2,1)} %copy-done.1) | copy-start | bytes 6291460
  92.5 13.8 %copy-start.5 = (f32[2,36,16,128]{3,2,1,0:T(8,128)S(1)}, f32[2,36,16,128]{3,2,1,0:T(8,128)}, u32[]{:S(2)}) copy-start(f32[2,36,16,128]{3,2,1,0:T(8,128)} %copy-done.4) | copy-start | bytes 1769476
  95.1 11.2 %collective-permute-start.35 = (f32[3,36,16,128]{3,2,1,0:T(8,128)}, f32[3,36,16,128]{3,2,1,0:T(8,128)}, u32[]{:S(2)}, u32[]{:S(2)}) collective-permute-start(f32[3,36,16,128]{3,2,1,0:T(8,128)} %get-tuple-element.193), channel_id=1, source_target_pairs={{0,1},{1,0},{2,3},{3,2},{4,5},{5,4},{6,7},{7,6},{8,9},{9,8},{10,11... | collective-permute-start | bytes 2654216 | tf_op jit(solution)/shard_map/ppermute | solution.py:394
  103.2 36.2 %collective-permute-start.39 = (bf16[2048,512]{1,0:T(8,128)(2,1)S(1)}, bf16[2048,512]{1,0:T(8,128)(2,1)}, u32[]{:S(2)}, u32[]{:S(2)}) collective-permute-start(bf16[2048,512]{1,0:T(8,128)(2,1)S(1)} %copy-done.2), channel_id=1, source_target_pairs={{0,1},{1,0},{2,3},{3,2},{4,5},{5,4},{6,7},{7,6},{8,9},{9,8},{10,11... | collective-permute-start | bytes 6291464 | tf_op jit(solution)/shard_map/ppermute | solution.py:394
  103.2 25.9 %collective-permute-start.37 = (bf16[1024,512]{1,0:T(8,128)(2,1)}, bf16[1024,512]{1,0:T(8,128)(2,1)}, u32[]{:S(2)}, u32[]{:S(2)}) collective-permute-start(bf16[1024,512]{1,0:T(8,128)(2,1)} %core_half.2), channel_id=1, source_target_pairs={{0,16},{1,9},{2,18},{3,11},{4,20},{5,13},{6,22},{7,15},{8,24},{9,1... | collective-permute-start | bytes 3145736 | tf_op jit(solution)/shard_map/ppermute | solution.py:434
  129.1 10.2 %collective-permute-start.40 = (bf16[1024,512]{1,0:T(8,128)(2,1)}, bf16[1024,512]{1,0:T(8,128)(2,1)}, u32[]{:S(2)}, u32[]{:S(2)}) collective-permute-start(bf16[1024,512]{1,0:T(8,128)(2,1)} %collective-permute-done.37.refs_11_), channel_id=1, source_target_pairs={{0,1},{1,0},{2,3},{3,2},{4,5},{5,4},{6,7},{7,6},{8,9},{9,8},{10,11... | collective-permute-start | bytes 3145736 | tf_op jit(solution)/shard_map/ppermute | solution.py:394
  131.9 30.7 %collective-permute-start.38 = (bf16[1024,512]{1,0:T(8,128)(2,1)}, bf16[1024,512]{1,0:T(8,128)(2,1)S(1)}, u32[]{:S(2)}, u32[]{:S(2)}) collective-permute-start(bf16[1024,512]{1,0:T(8,128)(2,1)} %core_half.3), channel_id=1, source_target_pairs={{0,16},{1,9},{2,18},{3,11},{4,20},{5,13},{6,22},{7,15},{8,24},{9,1... | collective-permute-start | bytes 3145736 | tf_op jit(solution)/shard_map/ppermute | solution.py:434
  133.0 37.1 %collective-permute-start.42 = (bf16[2048,512]{1,0:T(8,128)(2,1)}, bf16[2048,512]{1,0:T(8,128)(2,1)}, u32[]{:S(2)}, u32[]{:S(2)}) collective-permute-start(bf16[2048,512]{1,0:T(8,128)(2,1)} %all-gather.13.cloned.1.call-done.refs_8_), channel_id=1, source_target_pairs={{0,8},{1,17},{2,10},{3,19},{4,12},{5,21},{6,14},{7,23},{8,0},{9,25... | collective-permute-start | bytes 6291464 | tf_op jit(solution)/shard_map/ppermute | solution.py:434
  135.0 36.2 %collective-permute-start.43 = (bf16[2048,512]{1,0:T(8,128)(2,1)}, bf16[2048,512]{1,0:T(8,128)(2,1)}, u32[]{:S(2)}, u32[]{:S(2)}) collective-permute-start(bf16[2048,512]{1,0:T(8,128)(2,1)} %collective-permute-done.36.value_ref.refs_9_), channel_id=1, source_target_pairs={{0,1},{1,0},{2,3},{3,2},{4,5},{5,4},{6,7},{7,6},{8,9},{9,8},{10,11... | collective-permute-start | bytes 6291464 | tf_op jit(solution)/shard_map/ppermute | solution.py:394
  162.7 8.5 %copy-start.7 = (bf16[1024,512]{1,0:T(8,128)(2,1)}, bf16[1024,512]{1,0:T(8,128)(2,1)S(1)}, u32[]{:S(2)}) copy-start(bf16[1024,512]{1,0:T(8,128)(2,1)S(1)} %collective-permute-done.38.refs_11_) | copy-start | bytes 3145732
  162.7 32.0 %collective-permute-start.41 = (bf16[2048,512]{1,0:T(8,128)(2,1)}, bf16[2048,512]{1,0:T(8,128)(2,1)S(1)}, u32[]{:S(2)}, u32[]{:S(2)}) collective-permute-start(bf16[2048,512]{1,0:T(8,128)(2,1)} %all-gather.11.cloned.1.call-done.refs_3_), channel_id=1, source_target_pairs={{0,8},{1,17},{2,10},{3,19},{4,12},{5,21},{6,14},{7,23},{8,0},{9,25... | collective-permute-start | bytes 6291464 | tf_op jit(solution)/shard_map/ppermute | solution.py:434
  162.8 7.4 %collective-permute-start.44 = (bf16[1024,512]{1,0:T(8,128)(2,1)S(1)}, bf16[1024,512]{1,0:T(8,128)(2,1)S(1)}, u32[]{:S(2)}, u32[]{:S(2)}) collective-permute-start(bf16[1024,512]{1,0:T(8,128)(2,1)S(1)} %collective-permute-done.38.refs_11_), channel_id=1, source_target_pairs={{0,1},{1,0},{2,3},{3,2},{4,5},{5,4},{6,7},{7,6},{8,9},{9,8},{10,11... | collective-permute-start | bytes 3145736 | tf_op jit(solution)/shard_map/ppermute | solution.py:394
  170.2 24.6 %collective-permute-start.45 = (bf16[2048,512]{1,0:T(8,128)(2,1)}, bf16[2048,512]{1,0:T(8,128)(2,1)}, u32[]{:S(2)}, u32[]{:S(2)}) collective-permute-start(bf16[2048,512]{1,0:T(8,128)(2,1)} %collective-permute-done.42.refs_9_), channel_id=1, source_target_pairs={{0,1},{1,0},{2,3},{3,2},{4,5},{5,4},{6,7},{7,6},{8,9},{9,8},{10,11... | collective-permute-start | bytes 6291464 | tf_op jit(solution)/shard_map/ppermute | solution.py:394
  170.2 1.0 copy-start.8
  194.7 22.8 %copy-start.6 = (bf16[2048,512]{1,0:T(8,128)(2,1)}, bf16[2048,512]{1,0:T(8,128)(2,1)S(1)}, u32[]{:S(2)}) copy-start(bf16[2048,512]{1,0:T(8,128)(2,1)S(1)} %collective-permute-done.41.refs_4_) | copy-start | bytes 6291460
  194.7 22.8 %collective-permute-start.46 = (bf16[2048,512]{1,0:T(8,128)(2,1)S(1)}, bf16[2048,512]{1,0:T(8,128)(2,1)}, u32[]{:S(2)}, u32[]{:S(2)}) collective-permute-start(bf16[2048,512]{1,0:T(8,128)(2,1)S(1)} %collective-permute-done.41.refs_4_), channel_id=1, source_target_pairs={{0,1},{1,0},{2,3},{3,2},{4,5},{5,4},{6,7},{7,6},{8,9},{9,8},{10,11... | collective-permute-start | bytes 6291464 | tf_op jit(solution)/shard_map/ppermute | solution.py:394
Sparse Core Ops, SparseCore 0:
  22.2 31.1 all-gather.6
  55.0 29.5 all-gather.8
  86.3 28.7 all-gather.12
  116.5 28.6 all-gather.10
  146.6 28.5 all-gather.14
  176.7 29.8 all-gather.16

commit v3 on v2

--- a/solution.py
+++ b/solution.py
@@ -473,8 +473,10 @@
             for section, quarter in quarters.items()
         }
 
-    wholes = along_seq(quarters)
-    own, halves, shard = tie((permuted_rows(entering, order), halves, shard))
+    wholes = along_seq({0: quarters.pop(0)})
+    held = (permuted_rows(entering, order), halves, shard, quarters)
+    own, halves, shard, quarters = tie(held)
+    wholes.update(along_seq(quarters))
     fetched = [across(own_half(halves), hops) for hops in range(1, section_count)]
     last_quarters = spread_quarters(shard, 3, seq_far)
     before = lax.ppermute(own, "seq", [(i, i + 1) for i in range(seq_count - 1)])

time: 231 us -> 228 us (0.987)
  the two profiles are of different devices: /device:TPU:23 before, /device:TPU:24 now
where the time goes in v3:
time: 228 us; the launch traced here: 224 us
  Pallas kernels  88.9 us (39%)
  waiting for transfers between devices  73.4 us (32%)
  starting transfers between devices  21.6 us (9%)
  between operations  18.9 us (8%)
  other arithmetic  13.8 us (6%)
  local copies, waits for them, and re-layouts  7.72 us (3%)
    pallas_call x5, Pallas kernels, section_step(): pl.pallas_call(functools.partial(section_kernel, wholes_count, halves_cou...  83.6 us
    ppermute x6, waiting for transfers between devices, spread_quarters(): held.append(lax.ppermute(columns(hops), 'pipe', pairs))  34.1 us
    ppermute x6, waiting for transfers between devices, sent_by_core(): return lax.ppermute(value, ('pipe', 'seq'), pairs)  15.9 us
    ppermute x1, waiting for transfers between devices, mover(): return lambda held: lax.ppermute(held, 'pipe', pairs)  11.2 us
    ppermute x3, waiting for transfers between devices, across(): return lax.ppermute(value, 'pipe', [(i, i ^ hops) for i in range(count)])  11 us
    ppermute x6, starting transfers between devices, spread_quarters(): held.append(lax.ppermute(columns(hops), 'pipe', pairs))  6.8 us
    pallas_call x2, Pallas kernels, core_half(): pl.pallas_call(half_copy_kernel, out_shape=jax.ShapeDtypeStruct(shape, va...  5.34 us
    ppermute x7, starting transfers between devices, swapped(): return lax.ppermute(value, 'seq', [(i, i ^ 1) for i in range(count)])  4.69 us
  transfers between devices with their start and end apart: 30, of which 11 were waited for; matrix products, arithmetic and copies ran while one was open for 8% of the time, Pallas kernels for 37%

profile of v3, /device:TPU:24, one launch (start us, length us, event | category | flops | bytes accessed | tf_op | source)
XLA Modules:
  0.0 224.5 jit_solution(6110227990345492821)
XLA Ops:
  6.6 1.4 constant_dynamic-slice_fusion.3
  8.0 1.6 collective-permute-start.24
  9.6 1.5 collective-permute-start.25
  11.1 0.5 collective-permute-start.26
  11.7 0.5 multiply_bitcast_fusion.1
  12.5 4.8 %collective-permute-done.24 = bf16[256,512]{1,0:T(8,128)(2,1)S(1)} collective-permute-done((bf16[256,512]{1,0:T(8,128)(2,1)S(1)}, bf16[256,512]{1,0:T(8,128)(2,1)S(1)}, u32[]{:S(2)}, u32[]{:S(2)}) %collective-permute-start.24) | collective-permute-done | bytes 262176 | tf_op jit(solution)/shard_map/ppermute | solution.py:408
  17.3 5.7 %collective-permute-done.25 = bf16[256,512]{1,0:T(8,128)(2,1)S(1)} collective-permute-done((bf16[256,512]{1,0:T(8,128)(2,1)S(1)}, bf16[256,512]{1,0:T(8,128)(2,1)S(1)}, u32[]{:S(2)}, u32[]{:S(2)}) %collective-permute-start.25) | collective-permute-done | bytes 262176 | tf_op jit(solution)/shard_map/ppermute | solution.py:408
  23.0 0.1 pad_maximum_fusion.2
  23.1 1.0 dynamic-slice_bitcast_fusion.4
  24.3 0.7 iota_reduce_fusion
  25.6 12.8 %conditional.1 = (bf16[128,2048]{1,0:T(8,128)(2,1)}) conditional(s32[]{:T(128)} %clamp.3, bf16[128,2048]{1,0:T(8,128)(2,1)S(1)} %bitcast.143, bf16[128,2048]{1,0:T(8,128)(2,1)S(1)} %bitcast.133, bf16[128,2048]{1,0:T(8,128)(2,1)S(1)} %bitcast.134, bf16[128,2048]{1,0:T(8,128)(2,1)S(1)} %bitcast.135, ...), branch_computations={%region_6.7_spmd, %region_7.8_spmd, %region_8.9_spmd, %region_9.10... | conditional | bytes 2097200 | solution.py:451
  25.7 1.5 collective-permute-start.17
  27.2 11.2 %collective-permute-done.17 = bf16[128,2048]{1,0:T(8,128)(2,1)} collective-permute-done((bf16[128,2048]{1,0:T(8,128)(2,1)S(1)}, bf16[128,2048]{1,0:T(8,128)(2,1)}, u32[]{:S(2)}, u32[]{:S(2)}) %collective-permute-start.17) | collective-permute-done | bytes 524320 | tf_op jit(solution)/shard_map/cond/branch_17_fun/ppermute | solution.py:449
  38.5 0.7 all-gather.13.cloned.1.call-update
  39.2 0.5 all-gather.11.cloned.1.call-update
  39.8 1.5 collective-permute-start.27
  41.4 1.5 collective-permute-start.28
  42.8 0.6 collective-permute-start.29
  43.4 6.4 %collective-permute-done.27 = f32[36,16,128]{2,1,0:T(8,128)S(1)} collective-permute-done((f32[36,16,128]{2,1,0:T(8,128)S(1)}, f32[36,16,128]{2,1,0:T(8,128)S(1)}, u32[]{:S(2)}, u32[]{:S(2)}) %collective-permute-start.27) | collective-permute-done | bytes 294944 | tf_op jit(solution)/shard_map/ppermute | solution.py:389
  49.8 4.5 %collective-permute-done.28 = f32[36,16,128]{2,1,0:T(8,128)S(1)} collective-permute-done((f32[36,16,128]{2,1,0:T(8,128)S(1)}, f32[36,16,128]{2,1,0:T(8,128)S(1)}, u32[]{:S(2)}, u32[]{:S(2)}) %collective-permute-start.28) | collective-permute-done | bytes 294944 | tf_op jit(solution)/shard_map/ppermute | solution.py:389
  54.4 0.7 copy-done.11
  55.1 0.3 collective-permute-start.30
  55.3 0.6 dynamic_slice.63
  58.3 0.6 slice.20
  58.8 1.3 compare_reduce_fusion.1
  62.4 1.0 dynamic-slice_bitcast_fusion.3
  63.4 0.7 collective-permute-start.32
  64.1 1.3 collective-permute-start.33
  65.4 1.3 collective-permute-start.34
  66.7 1.9 collective-permute-start.31
  68.7 0.7 fusion.6
  69.6 10.2 %collective-permute-done.33 = bf16[256,512]{1,0:T(8,128)(2,1)S(1)} collective-permute-done((bf16[256,512]{1,0:T(8,128)(2,1)}, bf16[256,512]{1,0:T(8,128)(2,1)S(1)}, u32[]{:S(2)}, u32[]{:S(2)}) %collective-permute-start.33) | collective-permute-done | bytes 262176 | tf_op jit(solution)/shard_map/ppermute | solution.py:408
  79.7 13.5 %collective-permute-done.34 = bf16[256,512]{1,0:T(8,128)(2,1)S(1)} collective-permute-done((bf16[256,512]{1,0:T(8,128)(2,1)}, bf16[256,512]{1,0:T(8,128)(2,1)S(1)}, u32[]{:S(2)}, u32[]{:S(2)}) %collective-permute-start.34) | collective-permute-done | bytes 262176 | tf_op jit(solution)/shard_map/ppermute | solution.py:408
  93.3 0.1 pad_maximum_fusion.3
  93.4 0.9 dynamic-slice_bitcast_fusion.1
  94.3 0.9 collective-permute-start.36
  95.2 0.7 pad_add_fusion.1.place_ref.refs_0_
  95.9 0.5 compare_select_fusion.refs_4_
  96.4 2.7 %core_half.2 = bf16[1024,512]{1,0:T(8,128)(2,1)} custom-call(s32[2]{0:T(128)} %pad_add_fusion.1.place_ref.refs_0_, bf16[2048,512]{1,0:T(8,128)(2,1)} %copy-done.1), custom_call_target="tpu_custom_call" | custom-call | tf_op jit(solution)/shard_map/core_half/pallas_call | solution.py:367
  99.1 2.6 %fusion.8 = (f32[3,1,36,16,128]{4,3,2,1,0:T(8,128)}, f32[3,36,16,128]{3,2,1,0:T(8,128)}) fusion(f32[1,36,16,128]{3,2,1,0:T(8,128)} %bitcast.34, f32[1,36,16,128]{3,2,1,0:T(8,128)} %bitcast.119, f32[1,36,16,128]{3,2,1,0:T(8,128)S(1)} %bitcast.118), kind=kLoop, calls=%fused_computation.61 | loop fusion | flops 442368 | bytes 2654208 | tf_op jit(solution)/shard_map/stack | solution.py:424
  101.7 0.6 pad_add_fusion.7
  102.4 0.7 pad_add_fusion.6
  103.1 0.5 collective-permute-start.39
  103.6 0.7 pad_add_fusion.4.refs_2_
  104.2 0.1 copy.18
  104.4 0.7 fusion.4.refs_3_
  105.1 1.7 pad_maximum_fusion.1
  106.8 1.7 pad_maximum_fusion.refs_5_
  108.5 16.7 %section_step.5 = (bf16[256,2048]{1,0:T(8,128)(2,1)}, bf16[256,2048]{1,0:T(8,128)(2,1)}) custom-call(s32[4]{0:T(128)} %get-tuple-element.208.refs_0_, f32[256]{0:T(256)} %get-tuple-element.211.refs_1_, s32[17]{0:T(128)} %pad_add_fusion.4.refs_2_, s32[256,1]{1,0:T(8,128)} %fusion.4.refs_3_, s32[1,256]{1,0:T(1,128)} %compare_select_fusion.refs_4_, ...), custom_call_target="tpu_custom_call" | custom-call | flops 2147483648 | bytes 8388608 | tf_op jit(solution)/shard_map/section_step/pallas_call | solution.py:332
  125.2 1.6 collective-permute-done.37.refs_11_
  126.8 2.3 %collective-permute-start.40 = (bf16[1024,512]{1,0:T(8,128)(2,1)}, bf16[1024,512]{1,0:T(8,128)(2,1)}, u32[]{:S(2)}, u32[]{:S(2)}) collective-permute-start(bf16[1024,512]{1,0:T(8,128)(2,1)} %collective-permute-done.37.refs_11_), channel_id=1, source_target_pairs={{0,1},{1,0},{2,3},{3,2},{4,5},{5,4},{6,7},{7,6},{8,9},{9,8},{10,11... | collective-permute-start | bytes 3145736 | tf_op jit(solution)/shard_map/ppermute | solution.py:394
  129.1 2.8 %collective-permute-done.36.value_ref.refs_9_ = bf16[2048,512]{1,0:T(8,128)(2,1)} collective-permute-done((bf16[2048,512]{1,0:T(8,128)(2,1)}, bf16[2048,512]{1,0:T(8,128)(2,1)}, u32[]{:S(2)}, u32[]{:S(2)}) %collective-permute-start.36) | collective-permute-done | bytes 2097184 | tf_op jit(solution)/shard_map/ppermute | solution.py:434
  131.9 2.6 %core_half.3 = bf16[1024,512]{1,0:T(8,128)(2,1)} custom-call(s32[2]{0:T(128)} %pad_add_fusion.1.place_ref.refs_0_, bf16[2048,512]{1,0:T(8,128)(2,1)} %collective-permute-done.36.value_ref.refs_9_), custom_call_target="tpu_custom_call" | custom-call | tf_op jit(solution)/shard_map/core_half/pallas_call | solution.py:367
  134.7 0.9 collective-permute-start.42
  135.5 20.6 %section_step.6 = (bf16[256,2048]{1,0:T(8,128)(2,1)}, bf16[256,2048]{1,0:T(8,128)(2,1)}) custom-call(s32[4]{0:T(128)} %get-tuple-element.207.refs_0_, f32[256]{0:T(256)} %get-tuple-element.211.refs_1_, s32[17]{0:T(128)} %pad_add_fusion.4.refs_2_, s32[256,1]{1,0:T(8,128)} %fusion.4.refs_3_, s32[1,256]{1,0:T(1,128)} %compare_select_fusion.refs_4_, ...), custom_call_target="tpu_custom_call" | custom-call | flops 2147483648 | bytes 8388608 | tf_op jit(solution)/shard_map/section_step/pallas_call | solution.py:332
  156.1 4.9 %collective-permute-done.38.refs_11_ = bf16[1024,512]{1,0:T(8,128)(2,1)S(1)} collective-permute-done((bf16[1024,512]{1,0:T(8,128)(2,1)}, bf16[1024,512]{1,0:T(8,128)(2,1)S(1)}, u32[]{:S(2)}, u32[]{:S(2)}) %collective-permute-start.38) | collective-permute-done | bytes 1048608 | tf_op jit(solution)/shard_map/ppermute | solution.py:434
  161.0 0.8 collective-permute-start.41
  161.9 6.6 %collective-permute-done.42.refs_9_ = bf16[2048,512]{1,0:T(8,128)(2,1)} collective-permute-done((bf16[2048,512]{1,0:T(8,128)(2,1)}, bf16[2048,512]{1,0:T(8,128)(2,1)}, u32[]{:S(2)}, u32[]{:S(2)}) %collective-permute-start.42) | collective-permute-done | bytes 2097184 | tf_op jit(solution)/shard_map/ppermute | solution.py:434
  168.5 1.1 collective-permute-start.45
  169.5 1.0 copy-done.8
  170.5 20.8 %section_step.7 = (bf16[256,2048]{1,0:T(8,128)(2,1)}, bf16[256,2048]{1,0:T(8,128)(2,1)}) custom-call(s32[4]{0:T(128)} %get-tuple-element.182.refs_0_, f32[256]{0:T(256)} %get-tuple-element.211.refs_1_, s32[17]{0:T(128)} %pad_add_fusion.4.refs_2_, s32[256,1]{1,0:T(8,128)} %fusion.4.refs_3_, s32[1,256]{1,0:T(1,128)} %compare_select_fusion.refs_4_, ...), custom_call_target="tpu_custom_call" | custom-call | flops 2147483648 | bytes 8388608 | tf_op jit(solution)/shard_map/section_step/pallas_call | solution.py:332
  191.3 0.7 collective-permute-start.46
  192.0 19.7 %section_step.8 = (bf16[128,2048]{1,0:T(8,128)(2,1)}, bf16[128,2048]{1,0:T(8,128)(2,1)}) custom-call(s32[4]{0:T(128)} %get-tuple-element.209.refs_0_, f32[256]{0:T(256)} %get-tuple-element.211.refs_1_, s32[17]{0:T(128)} %pad_add_fusion.4.refs_2_, s32[256,1]{1,0:T(8,128)} %fusion.4.refs_3_, s32[1,256]{1,0:T(1,128)} %compare_select_fusion.refs_4_, ...), custom_call_target="tpu_custom_call" | custom-call | flops 2147483648 | bytes 8388608 | tf_op jit(solution)/shard_map/section_step/pallas_call | solution.py:332
  211.8 5.8 %section_step.9 = bf16[128,2048]{1,0:T(8,128)(2,1)} custom-call(s32[2]{0:T(128)} %pad_add_fusion.1.place_ref.refs_0_, bf16[128,2048]{1,0:T(8,128)(2,1)} %get-tuple-element.178.refs_1_, bf16[128,2048]{1,0:T(8,128)(2,1)} %get-tuple-element.179.refs_2_, bf16[2048,512]{1,0:T(8,128)(2,1)} %all-gather.11.cloned.1.call-done.refs_3_, bf16[2048,512]{1,0:T(8,128)(2,1)} %copy-done.6, ...), custom_call_target="tpu_custom_call" | custom-call | flops 1073741824 | bytes 8388608 | tf_op jit(solution)/shard_map/section_step/pallas_call | solution.py:332
  (101 shorter events, 1.7 us)
Async XLA Ops:
  6.5 51.3 %copy-start = (s32[4,32]{1,0:T(4,128)S(1)}, s32[4,32]{1,0:T(4,128)}, u32[]{:S(2)}) copy-start(s32[4,32]{1,0:T(4,128)} %param.36) | copy-start | bytes 1540
  6.5 5.0 %copy-start.12 = (f32[1,2,16,2048]{3,2,1,0:T(8,128)S(1)}, f32[1,2,16,2048]{3,2,1,0:T(8,128)}, u32[]{:S(2)}) copy-start(f32[1,2,16,2048]{3,2,1,0:T(8,128)} %param.41) | copy-start | bytes 786436
  6.5 5.1 %copy-start.14 = (f32[1,16,2048]{2,1,0:T(8,128)S(1)}, f32[1,16,2048]{2,1,0:T(8,128)}, u32[]{:S(2)}) copy-start(f32[1,16,2048]{2,1,0:T(8,128)} %param.39) | copy-start | bytes 393220
  6.5 5.1 %copy-start.13 = (f32[1,16,2048]{2,1,0:T(8,128)S(1)}, f32[1,16,2048]{2,1,0:T(8,128)}, u32[]{:S(2)}) copy-start(f32[1,16,2048]{2,1,0:T(8,128)} %param.40) | copy-start | bytes 393220
  6.5 48.5 %all-gather.7.cloned.1.call-start = ((), (), s32[]{:S(2)}) async-start(), calls=%async_computation | async-start | bytes 2359296 | tf_op jit(solution)/shard_map/all_gather | solution.py:472
  8.0 4.3 %copy-start.17 = (f32[1,2048]{1,0:T(1,128)S(1)}, f32[1,2048]{1,0:T(1,128)}, u32[]{:S(2)}) copy-start(f32[1,2048]{1,0:T(1,128)} %param.38) | copy-start | bytes 24580
  8.0 4.3 %copy-start.16 = (f32[1,2,2048]{2,1,0:T(2,128)S(1)}, f32[1,2,2048]{2,1,0:T(2,128)}, u32[]{:S(2)}) copy-start(f32[1,2,2048]{2,1,0:T(2,128)} %param.43) | copy-start | bytes 49156
  8.0 4.4 %copy-start.15 = (f32[1,2048]{1,0:T(1,128)S(1)}, f32[1,2048]{1,0:T(1,128)}, u32[]{:S(2)}) copy-start(f32[1,2048]{1,0:T(1,128)} %param.42) | copy-start | bytes 24580
  8.0 9.3 %collective-permute-start.24 = (bf16[256,512]{1,0:T(8,128)(2,1)S(1)}, bf16[256,512]{1,0:T(8,128)(2,1)S(1)}, u32[]{:S(2)}, u32[]{:S(2)}) collective-permute-start(bf16[256,512]{1,0:T(8,128)(2,1)S(1)} %get-tuple-element.196), channel_id=1, source_target_pairs={{0,8},{8,0},{16,24},{24,16},{1,9},{9,1},{17,25},{25,17},{2,10},{10... | collective-permute-start | bytes 786440 | tf_op jit(solution)/shard_map/ppermute | solution.py:408
  9.6 13.4 %collective-permute-start.25 = (bf16[256,512]{1,0:T(8,128)(2,1)S(1)}, bf16[256,512]{1,0:T(8,128)(2,1)S(1)}, u32[]{:S(2)}, u32[]{:S(2)}) collective-permute-start(bf16[256,512]{1,0:T(8,128)(2,1)S(1)} %get-tuple-element.195), channel_id=1, source_target_pairs={{0,16},{8,24},{16,0},{24,8},{1,17},{9,25},{17,1},{25,9},{2,18},{10... | collective-permute-start | bytes 786440 | tf_op jit(solution)/shard_map/ppermute | solution.py:408
  11.1 11.9 %collective-permute-start.26 = (bf16[256,512]{1,0:T(8,128)(2,1)S(1)}, bf16[256,512]{1,0:T(8,128)(2,1)S(1)}, u32[]{:S(2)}, u32[]{:S(2)}) collective-permute-start(bf16[256,512]{1,0:T(8,128)(2,1)S(1)} %get-tuple-element.197), channel_id=1, source_target_pairs={{0,24},{8,16},{16,8},{24,0},{1,25},{9,17},{17,9},{25,1},{2,26},{10... | collective-permute-start | bytes 786440 | tf_op jit(solution)/shard_map/ppermute | solution.py:408
  12.5 27.3 %copy-start.4 = (f32[2,36,16,128]{3,2,1,0:T(8,128)}, f32[2,36,16,128]{3,2,1,0:T(8,128)S(1)}, u32[]{:S(2)}) copy-start(f32[2,36,16,128]{3,2,1,0:T(8,128)S(1)} %pad_maximum_fusion.5) | copy-start | bytes 1769476
  23.0 1.3 copy-start.18
  23.0 1.3 copy-start.19
  23.0 2.1 copy-start.20
  23.1 39.3 %copy-start.3 = (bf16[1,256,2048]{2,1,0:T(8,128)(2,1)S(1)}, bf16[1,256,2048]{2,1,0:T(8,128)(2,1)}, u32[]{:S(2)}) copy-start(bf16[1,256,2048]{2,1,0:T(8,128)(2,1)} %param.44) | copy-start | bytes 3145732
  24.2 70.1 %all-gather.9.cloned.1.call-start = ((), (), s32[]{:S(2)}) async-start(), calls=%async_computation.1 | async-start | bytes 2359296 | tf_op jit(solution)/shard_map/all_gather | solution.py:472
  25.7 12.7 %collective-permute-start.17 = (bf16[128,2048]{1,0:T(8,128)(2,1)S(1)}, bf16[128,2048]{1,0:T(8,128)(2,1)}, u32[]{:S(2)}, u32[]{:S(2)}) collective-permute-start(bf16[128,2048]{1,0:T(8,128)(2,1)S(1)} %param.17), channel_id=1, source_target_pairs={{16,0},{24,8},{8,16},{0,24},{17,1},{25,9},{9,17},{1,25},{18,2},{26... | collective-permute-start | bytes 1572872 | tf_op jit(solution)/shard_map/cond/branch_17_fun/ppermute | solution.py:449
  38.4 90.7 %all-gather.13.cloned.1.call-start = ((), (), s32[]{:S(2)}) async-start(), calls=%async_computation.3 | async-start | bytes 2359296 | tf_op jit(solution)/shard_map/all_gather | solution.py:472
  39.2 121.8 %all-gather.11.cloned.1.call-start = ((), (), s32[]{:S(2)}) async-start(), calls=%async_computation.2 | async-start | bytes 2359296 | tf_op jit(solution)/shard_map/all_gather | solution.py:472
  39.7 152.3 %all-gather.15.cloned.1.call-start = ((), (), s32[]{:S(2)}) async-start(), calls=%async_computation.4 | async-start | bytes 2359296 | tf_op jit(solution)/shard_map/all_gather | solution.py:472
  39.8 10.0 %collective-permute-start.27 = (f32[36,16,128]{2,1,0:T(8,128)S(1)}, f32[36,16,128]{2,1,0:T(8,128)S(1)}, u32[]{:S(2)}, u32[]{:S(2)}) collective-permute-start(f32[36,16,128]{2,1,0:T(8,128)S(1)} %dynamic-slice_bitcast_fusion), channel_id=1, source_target_pairs={{0,8},{8,0},{16,24},{24,16},{1,9},{9,1},{17,25},{25,17},{2,10},{10... | collective-permute-start | bytes 884744 | tf_op jit(solution)/shard_map/ppermute | solution.py:389
  41.4 13.0 %collective-permute-start.28 = (f32[36,16,128]{2,1,0:T(8,128)S(1)}, f32[36,16,128]{2,1,0:T(8,128)S(1)}, u32[]{:S(2)}, u32[]{:S(2)}) collective-permute-start(f32[36,16,128]{2,1,0:T(8,128)S(1)} %dynamic-slice_bitcast_fusion), channel_id=1, source_target_pairs={{0,16},{8,24},{16,0},{24,8},{1,17},{9,25},{17,1},{25,9},{2,18},{10... | collective-permute-start | bytes 884744 | tf_op jit(solution)/shard_map/ppermute | solution.py:389
  42.8 12.3 %collective-permute-start.29 = (f32[36,16,128]{2,1,0:T(8,128)S(1)}, f32[36,16,128]{2,1,0:T(8,128)}, u32[]{:S(2)}, u32[]{:S(2)}) collective-permute-start(f32[36,16,128]{2,1,0:T(8,128)S(1)} %dynamic-slice_bitcast_fusion), channel_id=1, source_target_pairs={{0,24},{8,16},{16,8},{24,0},{1,25},{9,17},{17,9},{25,1},{2,26},{10... | collective-permute-start | bytes 884744 | tf_op jit(solution)/shard_map/ppermute | solution.py:389
  49.8 4.6 %copy-start.9 = (f32[36,16,128]{2,1,0:T(8,128)}, f32[36,16,128]{2,1,0:T(8,128)S(1)}, u32[]{:S(2)}) copy-start(f32[36,16,128]{2,1,0:T(8,128)S(1)} %collective-permute-done.27) | copy-start | bytes 884740
  54.4 0.7 copy-start.11
  55.1 39.2 %collective-permute-start.30 = (bf16[2048,512]{1,0:T(8,128)(2,1)}, bf16[2048,512]{1,0:T(8,128)(2,1)S(1)}, u32[]{:S(2)}, u32[]{:S(2)}) collective-permute-start(bf16[2048,512]{1,0:T(8,128)(2,1)} %all-gather.7.cloned.1.call-done.refs_8_), channel_id=1, source_target_pairs={{0,8},{1,17},{2,10},{3,19},{4,12},{5,21},{6,14},{7,23},{8,0},{9,25... | collective-permute-start | bytes 6291464 | tf_op jit(solution)/shard_map/ppermute | solution.py:434
  63.4 6.2 %collective-permute-start.32 = (bf16[256,512]{1,0:T(8,128)(2,1)}, bf16[256,512]{1,0:T(8,128)(2,1)S(1)}, u32[]{:S(2)}, u32[]{:S(2)}) collective-permute-start(bf16[256,512]{1,0:T(8,128)(2,1)} %get-tuple-element.189), channel_id=1, source_target_pairs={{16,24},{24,16},{17,25},{25,17},{18,26},{26,18},{19,27},{27,19},{2... | collective-permute-start | bytes 786440 | tf_op jit(solution)/shard_map/ppermute | solution.py:408
  64.1 15.7 %collective-permute-start.33 = (bf16[256,512]{1,0:T(8,128)(2,1)}, bf16[256,512]{1,0:T(8,128)(2,1)S(1)}, u32[]{:S(2)}, u32[]{:S(2)}) collective-permute-start(bf16[256,512]{1,0:T(8,128)(2,1)} %get-tuple-element.188), channel_id=1, source_target_pairs={{16,0},{24,8},{17,1},{25,9},{18,2},{26,10},{19,3},{27,11},{20,4},{... | collective-permute-start | bytes 786440 | tf_op jit(solution)/shard_map/ppermute | solution.py:408
  65.4 27.9 %collective-permute-start.34 = (bf16[256,512]{1,0:T(8,128)(2,1)}, bf16[256,512]{1,0:T(8,128)(2,1)S(1)}, u32[]{:S(2)}, u32[]{:S(2)}) collective-permute-start(bf16[256,512]{1,0:T(8,128)(2,1)} %get-tuple-element.187), channel_id=1, source_target_pairs={{16,8},{24,0},{17,9},{25,1},{18,10},{26,2},{19,11},{27,3},{20,12},... | collective-permute-start | bytes 786440 | tf_op jit(solution)/shard_map/ppermute | solution.py:408
  66.7 27.6 %collective-permute-start.31 = (bf16[128,2048]{1,0:T(8,128)(2,1)}, bf16[128,2048]{1,0:T(8,128)(2,1)}, u32[]{:S(2)}, u32[]{:S(2)}) collective-permute-start(bf16[128,2048]{1,0:T(8,128)(2,1)} %get-tuple-element.212.refs_7_), channel_id=1, source_target_pairs={{0,1},{1,2},{2,3},{3,4},{4,5},{5,6},{6,7},{8,9},{9,10},{10,11},{11... | collective-permute-start | bytes 1572872 | tf_op jit(solution)/shard_map/ppermute | solution.py:482
  93.4 5.7 %copy-start.10 = (f32[36,16,128]{2,1,0:T(8,128)S(1)}, f32[36,16,128]{2,1,0:T(8,128)}, u32[]{:S(2)}) copy-start(f32[36,16,128]{2,1,0:T(8,128)} %copy-done.9) | copy-start | bytes 884740
  94.3 2.1 copy-start.1
  94.3 37.7 %collective-permute-start.36 = (bf16[2048,512]{1,0:T(8,128)(2,1)}, bf16[2048,512]{1,0:T(8,128)(2,1)}, u32[]{:S(2)}, u32[]{:S(2)}) collective-permute-start(bf16[2048,512]{1,0:T(8,128)(2,1)} %all-gather.9.cloned.1.call-done.refs_8_), channel_id=1, source_target_pairs={{0,8},{1,17},{2,10},{3,19},{4,12},{5,21},{6,14},{7,23},{8,0},{9,25... | collective-permute-start | bytes 6291464 | tf_op jit(solution)/shard_map/ppermute | solution.py:434
  95.2 116.6 %all-gather.17.cloned.1.call-start = ((), (), s32[]{:S(2)}) async-start(), calls=%async_computation.5 | async-start | bytes 2359296 | tf_op jit(solution)/shard_map/all_gather | solution.py:472
  99.1 4.0 %copy-start.2 = (bf16[2048,512]{1,0:T(8,128)(2,1)S(1)}, bf16[2048,512]{1,0:T(8,128)(2,1)}, u32[]{:S(2)}) copy-start(bf16[2048,512]{1,0:T(8,128)(2,1)} %copy-done.1) | copy-start | bytes 6291460
  99.1 5.9 %copy-start.5 = (f32[2,36,16,128]{3,2,1,0:T(8,128)S(1)}, f32[2,36,16,128]{3,2,1,0:T(8,128)}, u32[]{:S(2)}) copy-start(f32[2,36,16,128]{3,2,1,0:T(8,128)} %copy-done.4) | copy-start | bytes 1769476
  101.7 3.4 %collective-permute-start.35 = (f32[3,36,16,128]{3,2,1,0:T(8,128)}, f32[3,36,16,128]{3,2,1,0:T(8,128)}, u32[]{:S(2)}, u32[]{:S(2)}) collective-permute-start(f32[3,36,16,128]{3,2,1,0:T(8,128)} %get-tuple-element.199), channel_id=1, source_target_pairs={{0,1},{1,0},{2,3},{3,2},{4,5},{5,4},{6,7},{7,6},{8,9},{9,8},{10,11... | collective-permute-start | bytes 2654216 | tf_op jit(solution)/shard_map/ppermute | solution.py:394
  103.1 32.5 %collective-permute-start.39 = (bf16[2048,512]{1,0:T(8,128)(2,1)S(1)}, bf16[2048,512]{1,0:T(8,128)(2,1)}, u32[]{:S(2)}, u32[]{:S(2)}) collective-permute-start(bf16[2048,512]{1,0:T(8,128)(2,1)S(1)} %copy-done.2), channel_id=1, source_target_pairs={{0,1},{1,0},{2,3},{3,2},{4,5},{5,4},{6,7},{7,6},{8,9},{9,8},{10,11... | collective-permute-start | bytes 6291464 | tf_op jit(solution)/shard_map/ppermute | solution.py:394
  103.6 23.2 %collective-permute-start.37 = (bf16[1024,512]{1,0:T(8,128)(2,1)}, bf16[1024,512]{1,0:T(8,128)(2,1)}, u32[]{:S(2)}, u32[]{:S(2)}) collective-permute-start(bf16[1024,512]{1,0:T(8,128)(2,1)} %core_half.2), channel_id=1, source_target_pairs={{0,16},{1,9},{2,18},{3,11},{4,20},{5,13},{6,22},{7,15},{8,24},{9,1... | collective-permute-start | bytes 3145736 | tf_op jit(solution)/shard_map/ppermute | solution.py:434
  126.8 8.8 %collective-permute-start.40 = (bf16[1024,512]{1,0:T(8,128)(2,1)}, bf16[1024,512]{1,0:T(8,128)(2,1)}, u32[]{:S(2)}, u32[]{:S(2)}) collective-permute-start(bf16[1024,512]{1,0:T(8,128)(2,1)} %collective-permute-done.37.refs_11_), channel_id=1, source_target_pairs={{0,1},{1,0},{2,3},{3,2},{4,5},{5,4},{6,7},{7,6},{8,9},{9,8},{10,11... | collective-permute-start | bytes 3145736 | tf_op jit(solution)/shard_map/ppermute | solution.py:394
  134.6 26.4 %collective-permute-start.38 = (bf16[1024,512]{1,0:T(8,128)(2,1)}, bf16[1024,512]{1,0:T(8,128)(2,1)S(1)}, u32[]{:S(2)}, u32[]{:S(2)}) collective-permute-start(bf16[1024,512]{1,0:T(8,128)(2,1)} %core_half.3), channel_id=1, source_target_pairs={{0,16},{1,9},{2,18},{3,11},{4,20},{5,13},{6,22},{7,15},{8,24},{9,1... | collective-permute-start | bytes 3145736 | tf_op jit(solution)/shard_map/ppermute | solution.py:434
  134.7 33.8 %collective-permute-start.42 = (bf16[2048,512]{1,0:T(8,128)(2,1)}, bf16[2048,512]{1,0:T(8,128)(2,1)}, u32[]{:S(2)}, u32[]{:S(2)}) collective-permute-start(bf16[2048,512]{1,0:T(8,128)(2,1)} %all-gather.13.cloned.1.call-done.refs_8_), channel_id=1, source_target_pairs={{0,8},{1,17},{2,10},{3,19},{4,12},{5,21},{6,14},{7,23},{8,0},{9,25... | collective-permute-start | bytes 6291464 | tf_op jit(solution)/shard_map/ppermute | solution.py:434
  135.5 35.0 %collective-permute-start.43 = (bf16[2048,512]{1,0:T(8,128)(2,1)}, bf16[2048,512]{1,0:T(8,128)(2,1)}, u32[]{:S(2)}, u32[]{:S(2)}) collective-permute-start(bf16[2048,512]{1,0:T(8,128)(2,1)} %collective-permute-done.36.value_ref.refs_9_), channel_id=1, source_target_pairs={{0,1},{1,0},{2,3},{3,2},{4,5},{5,4},{6,7},{7,6},{8,9},{9,8},{10,11... | collective-permute-start | bytes 6291464 | tf_op jit(solution)/shard_map/ppermute | solution.py:394
  161.0 9.6 %copy-start.7 = (bf16[1024,512]{1,0:T(8,128)(2,1)}, bf16[1024,512]{1,0:T(8,128)(2,1)S(1)}, u32[]{:S(2)}) copy-start(bf16[1024,512]{1,0:T(8,128)(2,1)S(1)} %collective-permute-done.38.refs_11_) | copy-start | bytes 3145732
  161.0 30.3 %collective-permute-start.41 = (bf16[2048,512]{1,0:T(8,128)(2,1)}, bf16[2048,512]{1,0:T(8,128)(2,1)S(1)}, u32[]{:S(2)}, u32[]{:S(2)}) collective-permute-start(bf16[2048,512]{1,0:T(8,128)(2,1)} %all-gather.11.cloned.1.call-done.refs_3_), channel_id=1, source_target_pairs={{0,8},{1,17},{2,10},{3,19},{4,12},{5,21},{6,14},{7,23},{8,0},{9,25... | collective-permute-start | bytes 6291464 | tf_op jit(solution)/shard_map/ppermute | solution.py:434
  161.8 7.8 %collective-permute-start.44 = (bf16[1024,512]{1,0:T(8,128)(2,1)S(1)}, bf16[1024,512]{1,0:T(8,128)(2,1)S(1)}, u32[]{:S(2)}, u32[]{:S(2)}) collective-permute-start(bf16[1024,512]{1,0:T(8,128)(2,1)S(1)} %collective-permute-done.38.refs_11_), channel_id=1, source_target_pairs={{0,1},{1,0},{2,3},{3,2},{4,5},{5,4},{6,7},{7,6},{8,9},{9,8},{10,11... | collective-permute-start | bytes 3145736 | tf_op jit(solution)/shard_map/ppermute | solution.py:394
  168.5 23.6 %collective-permute-start.45 = (bf16[2048,512]{1,0:T(8,128)(2,1)}, bf16[2048,512]{1,0:T(8,128)(2,1)}, u32[]{:S(2)}, u32[]{:S(2)}) collective-permute-start(bf16[2048,512]{1,0:T(8,128)(2,1)} %collective-permute-done.42.refs_9_), channel_id=1, source_target_pairs={{0,1},{1,0},{2,3},{3,2},{4,5},{5,4},{6,7},{7,6},{8,9},{9,8},{10,11... | collective-permute-start | bytes 6291464 | tf_op jit(solution)/shard_map/ppermute | solution.py:394
  169.5 1.0 copy-start.8
  191.3 20.4 %copy-start.6 = (bf16[2048,512]{1,0:T(8,128)(2,1)}, bf16[2048,512]{1,0:T(8,128)(2,1)S(1)}, u32[]{:S(2)}) copy-start(bf16[2048,512]{1,0:T(8,128)(2,1)S(1)} %collective-permute-done.41.refs_4_) | copy-start | bytes 6291460
  191.3 20.5 %collective-permute-start.46 = (bf16[2048,512]{1,0:T(8,128)(2,1)S(1)}, bf16[2048,512]{1,0:T(8,128)(2,1)}, u32[]{:S(2)}, u32[]{:S(2)}) collective-permute-start(bf16[2048,512]{1,0:T(8,128)(2,1)S(1)} %collective-permute-done.41.refs_4_), channel_id=1, source_target_pairs={{0,1},{1,0},{2,3},{3,2},{4,5},{5,4},{6,7},{7,6},{8,9},{9,8},{10,11... | collective-permute-start | bytes 6291464 | tf_op jit(solution)/shard_map/ppermute | solution.py:394
Sparse Core Ops, SparseCore 0:
  24.3 27.7 all-gather.6
  53.7 30.8 all-gather.8
  86.2 28.1 all-gather.12
  115.9 28.5 all-gather.10
  146.0 28.6 all-gather.14
  176.1 28.5 all-gather.16

commit v4 on v3

--- a/solution.py
+++ b/solution.py
@@ -438,11 +438,14 @@
     return sent_by_core(core_half(fetched, place), (2, 1))
 
 
-def permuted_rows(value, order):
-    count = lax.axis_size("pipe")
-    choices = list(itertools.permutations(range(count)))
+def permutation_index(order):
+    choices = list(itertools.permutations(range(lax.axis_size("pipe"))))
     match = jnp.all(jnp.asarray(np.array(choices, np.int32)) == order[None, :], axis=1)
-    which = jnp.argmax(match).astype(jnp.int32)
+    return jnp.argmax(match).astype(jnp.int32)
+
+
+def permuted_rows(value, which):
+    choices = list(itertools.permutations(range(lax.axis_size("pipe"))))
 
     def mover(choice):
         pairs = [(source, target) for target, source in enumerate(choice)]
@@ -464,8 +467,8 @@
 
     tie = lax.optimization_barrier
     quarters = spread_quarters(out_proj[0], 0, 0)
-    held = (quarters, halves, inputs[0], out_proj[0])
-    quarters, halves, entering, shard = tie(held)
+    held = (quarters, halves, inputs[0], out_proj[0], permutation_index(order))
+    quarters, halves, entering, shard, which = tie(held)
 
     def along_seq(quarters):
         return {
@@ -474,7 +477,7 @@
         }
 
     wholes = along_seq({0: quarters.pop(0)})
-    held = (permuted_rows(entering, order), halves, shard, quarters)
+    held = (permuted_rows(entering, which), halves, shard, quarters)
     own, halves, shard, quarters = tie(held)
     wholes.update(along_seq(quarters))
     fetched = [across(own_half(halves), hops) for hops in range(1, section_count)]

time: 228 us -> 229 us (level)
  Pallas kernels: 88.9 us -> 93 us
  waiting for transfers between devices: 73.4 us -> 70 us
    pallas_call x5, Pallas kernels: 83.6 us -> 87.7 us  [section_step(): pl.pallas_call(functools.partial(section_kernel, wholes_count, halves_cou...]
  transfers between devices with their start and end apart: 30 -> 30, of which waited for: 11 -> 11; matrix products, arithmetic and copies ran while one was open for 8% -> 8% of each run, Pallas kernels for 37% -> 39%
where the time goes in v4:
time: 229 us; the launch traced here: 226 us
  Pallas kernels  93 us (41%)
  waiting for transfers between devices  70 us (31%)
  starting transfers between devices  22.7 us (10%)
  between operations  18.9 us (8%)
  other arithmetic  13.8 us (6%)
  local copies, waits for them, and re-layouts  7.72 us (3%)
    pallas_call x5, Pallas kernels, section_step(): pl.pallas_call(functools.partial(section_kernel, wholes_count, halves_cou...  87.7 us
    ppermute x6, waiting for transfers between devices, spread_quarters(): held.append(lax.ppermute(columns(hops), 'pipe', pairs))  32.3 us
    ppermute x6, waiting for transfers between devices, sent_by_core(): return lax.ppermute(value, ('pipe', 'seq'), pairs)  13.9 us
    ppermute x1, waiting for transfers between devices, mover(): return lambda held: lax.ppermute(held, 'pipe', pairs)  11.4 us
    ppermute x3, waiting for transfers between devices, across(): return lax.ppermute(value, 'pipe', [(i, i ^ hops) for i in range(count)])  11 us
    ppermute x6, starting transfers between devices, spread_quarters(): held.append(lax.ppermute(columns(hops), 'pipe', pairs))  6.8 us
    pallas_call x2, Pallas kernels, core_half(): pl.pallas_call(half_copy_kernel, out_shape=jax.ShapeDtypeStruct(shape, va...  5.33 us
  transfers between devices with their start and end apart: 30, of which 11 were waited for; matrix products, arithmetic and copies ran while one was open for 8% of the time, Pallas kernels for 39%

profile of v4, /device:TPU:24, one launch (start us, length us, event | category | flops | bytes accessed | tf_op | source)
XLA Modules:
  0.0 226.2 jit_solution(3485152214939667745)
XLA Ops:
  6.6 1.4 constant_dynamic-slice_fusion.3
  8.0 1.6 collective-permute-start.24
  9.6 1.5 collective-permute-start.25
  11.1 0.5 collective-permute-start.26
  11.7 0.5 multiply_bitcast_fusion.1
  12.6 0.7 iota_reduce_fusion
  13.3 4.0 %collective-permute-done.24 = bf16[256,512]{1,0:T(8,128)(2,1)S(1)} collective-permute-done((bf16[256,512]{1,0:T(8,128)(2,1)S(1)}, bf16[256,512]{1,0:T(8,128)(2,1)S(1)}, u32[]{:S(2)}, u32[]{:S(2)}) %collective-permute-start.24) | collective-permute-done | bytes 262176 | tf_op jit(solution)/shard_map/ppermute | solution.py:408
  17.3 5.7 %collective-permute-done.25 = bf16[256,512]{1,0:T(8,128)(2,1)S(1)} collective-permute-done((bf16[256,512]{1,0:T(8,128)(2,1)S(1)}, bf16[256,512]{1,0:T(8,128)(2,1)S(1)}, u32[]{:S(2)}, u32[]{:S(2)}) %collective-permute-start.25) | collective-permute-done | bytes 262176 | tf_op jit(solution)/shard_map/ppermute | solution.py:408
  23.0 0.1 pad_maximum_fusion.2
  23.1 1.0 dynamic-slice_bitcast_fusion.4
  24.8 14.6 %conditional.1 = (bf16[128,2048]{1,0:T(8,128)(2,1)}) conditional(s32[]{:T(128)} %clamp.3, bf16[128,2048]{1,0:T(8,128)(2,1)S(1)} %bitcast.143, bf16[128,2048]{1,0:T(8,128)(2,1)S(1)} %bitcast.133, bf16[128,2048]{1,0:T(8,128)(2,1)S(1)} %bitcast.134, bf16[128,2048]{1,0:T(8,128)(2,1)S(1)} %bitcast.135, ...), branch_computations={%region_6.7_spmd, %region_7.8_spmd, %region_8.9_spmd, %region_9.10... | conditional | bytes 2097200 | solution.py:454
  24.9 3.1 %collective-permute-start.6 = (bf16[128,2048]{1,0:T(8,128)(2,1)S(1)}, bf16[128,2048]{1,0:T(8,128)(2,1)}, u32[]{:S(2)}, u32[]{:S(2)}) collective-permute-start(bf16[128,2048]{1,0:T(8,128)(2,1)S(1)} %param.6), channel_id=1, source_target_pairs={{8,0},{0,8},{16,16},{24,24},{9,1},{1,9},{17,17},{25,25},{10,2},{2,... | collective-permute-start | bytes 1572872 | tf_op jit(solution)/shard_map/cond/branch_6_fun/ppermute | solution.py:452
  28.0 11.4 %collective-permute-done.6 = bf16[128,2048]{1,0:T(8,128)(2,1)} collective-permute-done((bf16[128,2048]{1,0:T(8,128)(2,1)S(1)}, bf16[128,2048]{1,0:T(8,128)(2,1)}, u32[]{:S(2)}, u32[]{:S(2)}) %collective-permute-start.6) | collective-permute-done | bytes 524320 | tf_op jit(solution)/shard_map/cond/branch_6_fun/ppermute | solution.py:452
  39.5 0.7 all-gather.13.cloned.1.call-update
  40.3 0.5 all-gather.11.cloned.1.call-update
  40.9 1.5 collective-permute-start.27
  42.4 2.0 collective-permute-start.29
  44.4 6.4 %collective-permute-done.27 = f32[36,16,128]{2,1,0:T(8,128)S(1)} collective-permute-done((f32[36,16,128]{2,1,0:T(8,128)S(1)}, f32[36,16,128]{2,1,0:T(8,128)S(1)}, u32[]{:S(2)}, u32[]{:S(2)}) %collective-permute-start.27) | collective-permute-done | bytes 294944 | tf_op jit(solution)/shard_map/ppermute | solution.py:389
  50.9 4.5 %collective-permute-done.28 = f32[36,16,128]{2,1,0:T(8,128)S(1)} collective-permute-done((f32[36,16,128]{2,1,0:T(8,128)S(1)}, f32[36,16,128]{2,1,0:T(8,128)S(1)}, u32[]{:S(2)}, u32[]{:S(2)}) %collective-permute-start.28) | collective-permute-done | bytes 294944 | tf_op jit(solution)/shard_map/ppermute | solution.py:389
  55.4 0.7 copy-done.11
  56.1 0.4 collective-permute-start.30
  56.5 0.6 dynamic_slice.63
  59.2 0.1 reduce.36
  59.4 0.6 slice.20
  60.0 1.3 compare_reduce_fusion.1
  63.6 1.0 dynamic-slice_bitcast_fusion.3
  64.5 0.7 collective-permute-start.32
  65.2 1.3 collective-permute-start.33
  66.5 1.3 collective-permute-start.34
  67.8 1.9 collective-permute-start.31
  69.8 0.7 fusion.6
  70.6 0.1 reduce_or.9
  70.7 8.7 %collective-permute-done.33 = bf16[256,512]{1,0:T(8,128)(2,1)S(1)} collective-permute-done((bf16[256,512]{1,0:T(8,128)(2,1)}, bf16[256,512]{1,0:T(8,128)(2,1)S(1)}, u32[]{:S(2)}, u32[]{:S(2)}) %collective-permute-start.33) | collective-permute-done | bytes 262176 | tf_op jit(solution)/shard_map/ppermute | solution.py:408
  79.4 14.0 %collective-permute-done.34 = bf16[256,512]{1,0:T(8,128)(2,1)S(1)} collective-permute-done((bf16[256,512]{1,0:T(8,128)(2,1)}, bf16[256,512]{1,0:T(8,128)(2,1)S(1)}, u32[]{:S(2)}, u32[]{:S(2)}) %collective-permute-start.34) | collective-permute-done | bytes 262176 | tf_op jit(solution)/shard_map/ppermute | solution.py:408
  93.4 0.1 pad_maximum_fusion.3
  93.5 0.9 dynamic-slice_bitcast_fusion.1
  94.4 0.9 collective-permute-start.36
  95.4 0.7 pad_add_fusion.1.place_ref.refs_0_
  96.1 0.5 compare_select_fusion.refs_4_
  96.6 2.7 %core_half.2 = bf16[1024,512]{1,0:T(8,128)(2,1)} custom-call(s32[2]{0:T(128)} %pad_add_fusion.1.place_ref.refs_0_, bf16[2048,512]{1,0:T(8,128)(2,1)} %copy-done.1), custom_call_target="tpu_custom_call" | custom-call | tf_op jit(solution)/shard_map/core_half/pallas_call | solution.py:367
  99.3 2.6 %fusion.8 = (f32[3,1,36,16,128]{4,3,2,1,0:T(8,128)}, f32[3,36,16,128]{3,2,1,0:T(8,128)}) fusion(f32[1,36,16,128]{3,2,1,0:T(8,128)} %bitcast.34, f32[1,36,16,128]{3,2,1,0:T(8,128)} %bitcast.119, f32[1,36,16,128]{3,2,1,0:T(8,128)S(1)} %bitcast.118), kind=kLoop, calls=%fused_computation.61 | loop fusion | flops 442368 | bytes 2654208 | tf_op jit(solution)/shard_map/stack | solution.py:424
  101.9 0.6 pad_add_fusion.7
  102.6 0.7 pad_add_fusion.6
  103.3 0.5 collective-permute-start.39
  103.8 0.7 pad_add_fusion.4.refs_2_
  104.4 0.1 copy.18
  104.6 0.7 fusion.4.refs_3_
  105.3 1.6 pad_maximum_fusion.1
  107.0 1.7 pad_maximum_fusion.refs_5_
  108.6 17.7 %section_step.5 = (bf16[256,2048]{1,0:T(8,128)(2,1)}, bf16[256,2048]{1,0:T(8,128)(2,1)}) custom-call(s32[4]{0:T(128)} %get-tuple-element.210.refs_0_, f32[256]{0:T(256)} %get-tuple-element.213.refs_1_, s32[17]{0:T(128)} %pad_add_fusion.4.refs_2_, s32[256,1]{1,0:T(8,128)} %fusion.4.refs_3_, s32[1,256]{1,0:T(1,128)} %compare_select_fusion.refs_4_, ...), custom_call_target="tpu_custom_call" | custom-call | flops 2147483648 | bytes 8388608 | tf_op jit(solution)/shard_map/section_step/pallas_call | solution.py:332
  126.3 0.8 collective-permute-done.37.refs_11_
  127.1 2.2 collective-permute-start.40
  129.3 2.7 %collective-permute-done.36.value_ref.refs_9_ = bf16[2048,512]{1,0:T(8,128)(2,1)} collective-permute-done((bf16[2048,512]{1,0:T(8,128)(2,1)}, bf16[2048,512]{1,0:T(8,128)(2,1)}, u32[]{:S(2)}, u32[]{:S(2)}) %collective-permute-start.36) | collective-permute-done | bytes 2097184 | tf_op jit(solution)/shard_map/ppermute | solution.py:434
  132.1 2.6 %core_half.3 = bf16[1024,512]{1,0:T(8,128)(2,1)} custom-call(s32[2]{0:T(128)} %pad_add_fusion.1.place_ref.refs_0_, bf16[2048,512]{1,0:T(8,128)(2,1)} %collective-permute-done.36.value_ref.refs_9_), custom_call_target="tpu_custom_call" | custom-call | tf_op jit(solution)/shard_map/core_half/pallas_call | solution.py:367
  134.8 0.9 collective-permute-start.42
  135.8 21.6 %section_step.6 = (bf16[256,2048]{1,0:T(8,128)(2,1)}, bf16[256,2048]{1,0:T(8,128)(2,1)}) custom-call(s32[4]{0:T(128)} %get-tuple-element.209.refs_0_, f32[256]{0:T(256)} %get-tuple-element.213.refs_1_, s32[17]{0:T(128)} %pad_add_fusion.4.refs_2_, s32[256,1]{1,0:T(8,128)} %fusion.4.refs_3_, s32[1,256]{1,0:T(1,128)} %compare_select_fusion.refs_4_, ...), custom_call_target="tpu_custom_call" | custom-call | flops 2147483648 | bytes 8388608 | tf_op jit(solution)/shard_map/section_step/pallas_call | solution.py:332
  157.3 3.8 %collective-permute-done.38.refs_11_ = bf16[1024,512]{1,0:T(8,128)(2,1)S(1)} collective-permute-done((bf16[1024,512]{1,0:T(8,128)(2,1)}, bf16[1024,512]{1,0:T(8,128)(2,1)S(1)}, u32[]{:S(2)}, u32[]{:S(2)}) %collective-permute-start.38) | collective-permute-done | bytes 1048608 | tf_op jit(solution)/shard_map/ppermute | solution.py:434
  161.1 0.9 collective-permute-start.41
  162.1 6.6 %collective-permute-done.42.refs_9_ = bf16[2048,512]{1,0:T(8,128)(2,1)} collective-permute-done((bf16[2048,512]{1,0:T(8,128)(2,1)}, bf16[2048,512]{1,0:T(8,128)(2,1)}, u32[]{:S(2)}, u32[]{:S(2)}) %collective-permute-start.42) | collective-permute-done | bytes 2097184 | tf_op jit(solution)/shard_map/ppermute | solution.py:434
  168.7 1.0 collective-permute-start.45
  169.7 1.0 copy-done.8
  170.7 21.8 %section_step.7 = (bf16[256,2048]{1,0:T(8,128)(2,1)}, bf16[256,2048]{1,0:T(8,128)(2,1)}) custom-call(s32[4]{0:T(128)} %get-tuple-element.184.refs_0_, f32[256]{0:T(256)} %get-tuple-element.213.refs_1_, s32[17]{0:T(128)} %pad_add_fusion.4.refs_2_, s32[256,1]{1,0:T(8,128)} %fusion.4.refs_3_, s32[1,256]{1,0:T(1,128)} %compare_select_fusion.refs_4_, ...), custom_call_target="tpu_custom_call" | custom-call | flops 2147483648 | bytes 8388608 | tf_op jit(solution)/shard_map/section_step/pallas_call | solution.py:332
  192.6 20.9 %section_step.8 = (bf16[128,2048]{1,0:T(8,128)(2,1)}, bf16[128,2048]{1,0:T(8,128)(2,1)}) custom-call(s32[4]{0:T(128)} %get-tuple-element.211.refs_0_, f32[256]{0:T(256)} %get-tuple-element.213.refs_1_, s32[17]{0:T(128)} %pad_add_fusion.4.refs_2_, s32[256,1]{1,0:T(8,128)} %fusion.4.refs_3_, s32[1,256]{1,0:T(1,128)} %compare_select_fusion.refs_4_, ...), custom_call_target="tpu_custom_call" | custom-call | flops 2147483648 | bytes 8388608 | tf_op jit(solution)/shard_map/section_step/pallas_call | solution.py:332
  213.5 5.8 %section_step.9 = bf16[128,2048]{1,0:T(8,128)(2,1)} custom-call(s32[2]{0:T(128)} %pad_add_fusion.1.place_ref.refs_0_, bf16[128,2048]{1,0:T(8,128)(2,1)} %get-tuple-element.180.refs_1_, bf16[128,2048]{1,0:T(8,128)(2,1)} %get-tuple-element.181.refs_2_, bf16[2048,512]{1,0:T(8,128)(2,1)} %all-gather.11.cloned.1.call-done.refs_3_, bf16[2048,512]{1,0:T(8,128)(2,1)} %copy-done.6, ...), custom_call_target="tpu_custom_call" | custom-call | flops 1073741824 | bytes 8388608 | tf_op jit(solution)/shard_map/section_step/pallas_call | solution.py:332
  (101 shorter events, 1.5 us)
Async XLA Ops:
  6.5 52.5 %copy-start = (s32[4,32]{1,0:T(4,128)S(1)}, s32[4,32]{1,0:T(4,128)}, u32[]{:S(2)}) copy-start(s32[4,32]{1,0:T(4,128)} %param.36) | copy-start | bytes 1540
  6.5 5.0 %copy-start.12 = (f32[1,2,16,2048]{3,2,1,0:T(8,128)S(1)}, f32[1,2,16,2048]{3,2,1,0:T(8,128)}, u32[]{:S(2)}) copy-start(f32[1,2,16,2048]{3,2,1,0:T(8,128)} %param.41) | copy-start | bytes 786436
  6.5 5.1 %copy-start.14 = (f32[1,16,2048]{2,1,0:T(8,128)S(1)}, f32[1,16,2048]{2,1,0:T(8,128)}, u32[]{:S(2)}) copy-start(f32[1,16,2048]{2,1,0:T(8,128)} %param.39) | copy-start | bytes 393220
  6.5 5.1 %copy-start.13 = (f32[1,16,2048]{2,1,0:T(8,128)S(1)}, f32[1,16,2048]{2,1,0:T(8,128)}, u32[]{:S(2)}) copy-start(f32[1,16,2048]{2,1,0:T(8,128)} %param.40) | copy-start | bytes 393220
  6.5 49.6 %all-gather.7.cloned.1.call-start = ((), (), s32[]{:S(2)}) async-start(), calls=%async_computation | async-start | bytes 2359296 | tf_op jit(solution)/shard_map/all_gather | solution.py:475
  8.0 4.4 %copy-start.17 = (f32[1,2048]{1,0:T(1,128)S(1)}, f32[1,2048]{1,0:T(1,128)}, u32[]{:S(2)}) copy-start(f32[1,2048]{1,0:T(1,128)} %param.38) | copy-start | bytes 24580
  8.0 4.4 %copy-start.16 = (f32[1,2,2048]{2,1,0:T(2,128)S(1)}, f32[1,2,2048]{2,1,0:T(2,128)}, u32[]{:S(2)}) copy-start(f32[1,2,2048]{2,1,0:T(2,128)} %param.43) | copy-start | bytes 49156
  8.0 4.4 %copy-start.15 = (f32[1,2048]{1,0:T(1,128)S(1)}, f32[1,2048]{1,0:T(1,128)}, u32[]{:S(2)}) copy-start(f32[1,2048]{1,0:T(1,128)} %param.42) | copy-start | bytes 24580
  8.0 9.3 %collective-permute-start.24 = (bf16[256,512]{1,0:T(8,128)(2,1)S(1)}, bf16[256,512]{1,0:T(8,128)(2,1)S(1)}, u32[]{:S(2)}, u32[]{:S(2)}) collective-permute-start(bf16[256,512]{1,0:T(8,128)(2,1)S(1)} %get-tuple-element.198), channel_id=1, source_target_pairs={{0,8},{8,0},{16,24},{24,16},{1,9},{9,1},{17,25},{25,17},{2,10},{10... | collective-permute-start | bytes 786440 | tf_op jit(solution)/shard_map/ppermute | solution.py:408
  9.6 13.4 %collective-permute-start.25 = (bf16[256,512]{1,0:T(8,128)(2,1)S(1)}, bf16[256,512]{1,0:T(8,128)(2,1)S(1)}, u32[]{:S(2)}, u32[]{:S(2)}) collective-permute-start(bf16[256,512]{1,0:T(8,128)(2,1)S(1)} %get-tuple-element.197), channel_id=1, source_target_pairs={{0,16},{8,24},{16,0},{24,8},{1,17},{9,25},{17,1},{25,9},{2,18},{10... | collective-permute-start | bytes 786440 | tf_op jit(solution)/shard_map/ppermute | solution.py:408
  11.1 11.9 %collective-permute-start.26 = (bf16[256,512]{1,0:T(8,128)(2,1)S(1)}, bf16[256,512]{1,0:T(8,128)(2,1)S(1)}, u32[]{:S(2)}, u32[]{:S(2)}) collective-permute-start(bf16[256,512]{1,0:T(8,128)(2,1)S(1)} %get-tuple-element.199), channel_id=1, source_target_pairs={{0,24},{8,16},{16,8},{24,0},{1,25},{9,17},{17,9},{25,1},{2,26},{10... | collective-permute-start | bytes 786440 | tf_op jit(solution)/shard_map/ppermute | solution.py:408
  11.6 0.9 copy-start.18
  11.6 0.9 copy-start.19
  12.5 28.3 %copy-start.4 = (f32[2,36,16,128]{3,2,1,0:T(8,128)}, f32[2,36,16,128]{3,2,1,0:T(8,128)S(1)}, u32[]{:S(2)}) copy-start(f32[2,36,16,128]{3,2,1,0:T(8,128)S(1)} %pad_maximum_fusion.5) | copy-start | bytes 1769476
  23.0 1.3 copy-start.20
  23.1 40.5 %copy-start.3 = (bf16[1,256,2048]{2,1,0:T(8,128)(2,1)S(1)}, bf16[1,256,2048]{2,1,0:T(8,128)(2,1)}, u32[]{:S(2)}) copy-start(bf16[1,256,2048]{2,1,0:T(8,128)(2,1)} %param.44) | copy-start | bytes 3145732
  24.2 70.2 %all-gather.9.cloned.1.call-start = ((), (), s32[]{:S(2)}) async-start(), calls=%async_computation.1 | async-start | bytes 2359296 | tf_op jit(solution)/shard_map/all_gather | solution.py:475
  24.9 14.6 %collective-permute-start.6 = (bf16[128,2048]{1,0:T(8,128)(2,1)S(1)}, bf16[128,2048]{1,0:T(8,128)(2,1)}, u32[]{:S(2)}, u32[]{:S(2)}) collective-permute-start(bf16[128,2048]{1,0:T(8,128)(2,1)S(1)} %param.6), channel_id=1, source_target_pairs={{8,0},{0,8},{16,16},{24,24},{9,1},{1,9},{17,17},{25,25},{10,2},{2,... | collective-permute-start | bytes 1572872 | tf_op jit(solution)/shard_map/cond/branch_6_fun/ppermute | solution.py:452
  39.5 89.9 %all-gather.13.cloned.1.call-start = ((), (), s32[]{:S(2)}) async-start(), calls=%async_computation.3 | async-start | bytes 2359296 | tf_op jit(solution)/shard_map/all_gather | solution.py:475
  40.2 120.9 %all-gather.11.cloned.1.call-start = ((), (), s32[]{:S(2)}) async-start(), calls=%async_computation.2 | async-start | bytes 2359296 | tf_op jit(solution)/shard_map/all_gather | solution.py:475
  40.8 151.8 %all-gather.15.cloned.1.call-start = ((), (), s32[]{:S(2)}) async-start(), calls=%async_computation.4 | async-start | bytes 2359296 | tf_op jit(solution)/shard_map/all_gather | solution.py:475
  40.9 10.0 %collective-permute-start.27 = (f32[36,16,128]{2,1,0:T(8,128)S(1)}, f32[36,16,128]{2,1,0:T(8,128)S(1)}, u32[]{:S(2)}, u32[]{:S(2)}) collective-permute-start(f32[36,16,128]{2,1,0:T(8,128)S(1)} %dynamic-slice_bitcast_fusion), channel_id=1, source_target_pairs={{0,8},{8,0},{16,24},{24,16},{1,9},{9,1},{17,25},{25,17},{2,10},{10... | collective-permute-start | bytes 884744 | tf_op jit(solution)/shard_map/ppermute | solution.py:389
  42.4 13.0 %collective-permute-start.28 = (f32[36,16,128]{2,1,0:T(8,128)S(1)}, f32[36,16,128]{2,1,0:T(8,128)S(1)}, u32[]{:S(2)}, u32[]{:S(2)}) collective-permute-start(f32[36,16,128]{2,1,0:T(8,128)S(1)} %dynamic-slice_bitcast_fusion), channel_id=1, source_target_pairs={{0,16},{8,24},{16,0},{24,8},{1,17},{9,25},{17,1},{25,9},{2,18},{10... | collective-permute-start | bytes 884744 | tf_op jit(solution)/shard_map/ppermute | solution.py:389
  42.4 13.7 %collective-permute-start.29 = (f32[36,16,128]{2,1,0:T(8,128)S(1)}, f32[36,16,128]{2,1,0:T(8,128)}, u32[]{:S(2)}, u32[]{:S(2)}) collective-permute-start(f32[36,16,128]{2,1,0:T(8,128)S(1)} %dynamic-slice_bitcast_fusion), channel_id=1, source_target_pairs={{0,24},{8,16},{16,8},{24,0},{1,25},{9,17},{17,9},{25,1},{2,26},{10... | collective-permute-start | bytes 884744 | tf_op jit(solution)/shard_map/ppermute | solution.py:389
  50.9 4.5 %copy-start.9 = (f32[36,16,128]{2,1,0:T(8,128)}, f32[36,16,128]{2,1,0:T(8,128)S(1)}, u32[]{:S(2)}) copy-start(f32[36,16,128]{2,1,0:T(8,128)S(1)} %collective-permute-done.27) | copy-start | bytes 884740
  55.4 0.7 copy-start.11
  56.1 38.3 %collective-permute-start.30 = (bf16[2048,512]{1,0:T(8,128)(2,1)}, bf16[2048,512]{1,0:T(8,128)(2,1)S(1)}, u32[]{:S(2)}, u32[]{:S(2)}) collective-permute-start(bf16[2048,512]{1,0:T(8,128)(2,1)} %all-gather.7.cloned.1.call-done.refs_8_), channel_id=1, source_target_pairs={{0,8},{1,17},{2,10},{3,19},{4,12},{5,21},{6,14},{7,23},{8,0},{9,25... | collective-permute-start | bytes 6291464 | tf_op jit(solution)/shard_map/ppermute | solution.py:434
  64.5 6.2 %collective-permute-start.32 = (bf16[256,512]{1,0:T(8,128)(2,1)}, bf16[256,512]{1,0:T(8,128)(2,1)S(1)}, u32[]{:S(2)}, u32[]{:S(2)}) collective-permute-start(bf16[256,512]{1,0:T(8,128)(2,1)} %get-tuple-element.191), channel_id=1, source_target_pairs={{16,24},{24,16},{17,25},{25,17},{18,26},{26,18},{19,27},{27,19},{2... | collective-permute-start | bytes 786440 | tf_op jit(solution)/shard_map/ppermute | solution.py:408
  65.2 14.2 %collective-permute-start.33 = (bf16[256,512]{1,0:T(8,128)(2,1)}, bf16[256,512]{1,0:T(8,128)(2,1)S(1)}, u32[]{:S(2)}, u32[]{:S(2)}) collective-permute-start(bf16[256,512]{1,0:T(8,128)(2,1)} %get-tuple-element.190), channel_id=1, source_target_pairs={{16,0},{24,8},{17,1},{25,9},{18,2},{26,10},{19,3},{27,11},{20,4},{... | collective-permute-start | bytes 786440 | tf_op jit(solution)/shard_map/ppermute | solution.py:408
  66.5 26.9 %collective-permute-start.34 = (bf16[256,512]{1,0:T(8,128)(2,1)}, bf16[256,512]{1,0:T(8,128)(2,1)S(1)}, u32[]{:S(2)}, u32[]{:S(2)}) collective-permute-start(bf16[256,512]{1,0:T(8,128)(2,1)} %get-tuple-element.189), channel_id=1, source_target_pairs={{16,8},{24,0},{17,9},{25,1},{18,10},{26,2},{19,11},{27,3},{20,12},... | collective-permute-start | bytes 786440 | tf_op jit(solution)/shard_map/ppermute | solution.py:408
  67.8 26.6 %collective-permute-start.31 = (bf16[128,2048]{1,0:T(8,128)(2,1)}, bf16[128,2048]{1,0:T(8,128)(2,1)}, u32[]{:S(2)}, u32[]{:S(2)}) collective-permute-start(bf16[128,2048]{1,0:T(8,128)(2,1)} %get-tuple-element.214.refs_7_), channel_id=1, source_target_pairs={{0,1},{1,2},{2,3},{3,4},{4,5},{5,6},{6,7},{8,9},{9,10},{10,11},{11... | collective-permute-start | bytes 1572872 | tf_op jit(solution)/shard_map/ppermute | solution.py:485
  93.5 5.8 %copy-start.10 = (f32[36,16,128]{2,1,0:T(8,128)S(1)}, f32[36,16,128]{2,1,0:T(8,128)}, u32[]{:S(2)}) copy-start(f32[36,16,128]{2,1,0:T(8,128)} %copy-done.9) | copy-start | bytes 884740
  94.4 2.2 copy-start.1
  94.4 37.7 %collective-permute-start.36 = (bf16[2048,512]{1,0:T(8,128)(2,1)}, bf16[2048,512]{1,0:T(8,128)(2,1)}, u32[]{:S(2)}, u32[]{:S(2)}) collective-permute-start(bf16[2048,512]{1,0:T(8,128)(2,1)} %all-gather.9.cloned.1.call-done.refs_8_), channel_id=1, source_target_pairs={{0,8},{1,17},{2,10},{3,19},{4,12},{5,21},{6,14},{7,23},{8,0},{9,25... | collective-permute-start | bytes 6291464 | tf_op jit(solution)/shard_map/ppermute | solution.py:434
  95.4 118.1 %all-gather.17.cloned.1.call-start = ((), (), s32[]{:S(2)}) async-start(), calls=%async_computation.5 | async-start | bytes 2359296 | tf_op jit(solution)/shard_map/all_gather | solution.py:475
  99.3 4.0 %copy-start.2 = (bf16[2048,512]{1,0:T(8,128)(2,1)S(1)}, bf16[2048,512]{1,0:T(8,128)(2,1)}, u32[]{:S(2)}) copy-start(bf16[2048,512]{1,0:T(8,128)(2,1)} %copy-done.1) | copy-start | bytes 6291460
  99.3 6.0 %copy-start.5 = (f32[2,36,16,128]{3,2,1,0:T(8,128)S(1)}, f32[2,36,16,128]{3,2,1,0:T(8,128)}, u32[]{:S(2)}) copy-start(f32[2,36,16,128]{3,2,1,0:T(8,128)} %copy-done.4) | copy-start | bytes 1769476
  101.9 3.4 %collective-permute-start.35 = (f32[3,36,16,128]{3,2,1,0:T(8,128)}, f32[3,36,16,128]{3,2,1,0:T(8,128)}, u32[]{:S(2)}, u32[]{:S(2)}) collective-permute-start(f32[3,36,16,128]{3,2,1,0:T(8,128)} %get-tuple-element.201), channel_id=1, source_target_pairs={{0,1},{1,0},{2,3},{3,2},{4,5},{5,4},{6,7},{7,6},{8,9},{9,8},{10,11... | collective-permute-start | bytes 2654216 | tf_op jit(solution)/shard_map/ppermute | solution.py:394
  103.3 32.5 %collective-permute-start.39 = (bf16[2048,512]{1,0:T(8,128)(2,1)S(1)}, bf16[2048,512]{1,0:T(8,128)(2,1)}, u32[]{:S(2)}, u32[]{:S(2)}) collective-permute-start(bf16[2048,512]{1,0:T(8,128)(2,1)S(1)} %copy-done.2), channel_id=1, source_target_pairs={{0,1},{1,0},{2,3},{3,2},{4,5},{5,4},{6,7},{7,6},{8,9},{9,8},{10,11... | collective-permute-start | bytes 6291464 | tf_op jit(solution)/shard_map/ppermute | solution.py:394
  103.8 23.4 %collective-permute-start.37 = (bf16[1024,512]{1,0:T(8,128)(2,1)}, bf16[1024,512]{1,0:T(8,128)(2,1)}, u32[]{:S(2)}, u32[]{:S(2)}) collective-permute-start(bf16[1024,512]{1,0:T(8,128)(2,1)} %core_half.2), channel_id=1, source_target_pairs={{0,16},{1,9},{2,18},{3,11},{4,20},{5,13},{6,22},{7,15},{8,24},{9,1... | collective-permute-start | bytes 3145736 | tf_op jit(solution)/shard_map/ppermute | solution.py:434
  127.1 8.6 %collective-permute-start.40 = (bf16[1024,512]{1,0:T(8,128)(2,1)}, bf16[1024,512]{1,0:T(8,128)(2,1)}, u32[]{:S(2)}, u32[]{:S(2)}) collective-permute-start(bf16[1024,512]{1,0:T(8,128)(2,1)} %collective-permute-done.37.refs_11_), channel_id=1, source_target_pairs={{0,1},{1,0},{2,3},{3,2},{4,5},{5,4},{6,7},{7,6},{8,9},{9,8},{10,11... | collective-permute-start | bytes 3145736 | tf_op jit(solution)/shard_map/ppermute | solution.py:394
  134.7 26.4 %collective-permute-start.38 = (bf16[1024,512]{1,0:T(8,128)(2,1)}, bf16[1024,512]{1,0:T(8,128)(2,1)S(1)}, u32[]{:S(2)}, u32[]{:S(2)}) collective-permute-start(bf16[1024,512]{1,0:T(8,128)(2,1)} %core_half.3), channel_id=1, source_target_pairs={{0,16},{1,9},{2,18},{3,11},{4,20},{5,13},{6,22},{7,15},{8,24},{9,1... | collective-permute-start | bytes 3145736 | tf_op jit(solution)/shard_map/ppermute | solution.py:434
  134.8 33.9 %collective-permute-start.42 = (bf16[2048,512]{1,0:T(8,128)(2,1)}, bf16[2048,512]{1,0:T(8,128)(2,1)}, u32[]{:S(2)}, u32[]{:S(2)}) collective-permute-start(bf16[2048,512]{1,0:T(8,128)(2,1)} %all-gather.13.cloned.1.call-done.refs_8_), channel_id=1, source_target_pairs={{0,8},{1,17},{2,10},{3,19},{4,12},{5,21},{6,14},{7,23},{8,0},{9,25... | collective-permute-start | bytes 6291464 | tf_op jit(solution)/shard_map/ppermute | solution.py:434
  135.7 34.9 %collective-permute-start.43 = (bf16[2048,512]{1,0:T(8,128)(2,1)}, bf16[2048,512]{1,0:T(8,128)(2,1)}, u32[]{:S(2)}, u32[]{:S(2)}) collective-permute-start(bf16[2048,512]{1,0:T(8,128)(2,1)} %collective-permute-done.36.value_ref.refs_9_), channel_id=1, source_target_pairs={{0,1},{1,0},{2,3},{3,2},{4,5},{5,4},{6,7},{7,6},{8,9},{9,8},{10,11... | collective-permute-start | bytes 6291464 | tf_op jit(solution)/shard_map/ppermute | solution.py:394
  161.1 9.6 %copy-start.7 = (bf16[1024,512]{1,0:T(8,128)(2,1)}, bf16[1024,512]{1,0:T(8,128)(2,1)S(1)}, u32[]{:S(2)}) copy-start(bf16[1024,512]{1,0:T(8,128)(2,1)S(1)} %collective-permute-done.38.refs_11_) | copy-start | bytes 3145732
  161.1 31.4 %collective-permute-start.41 = (bf16[2048,512]{1,0:T(8,128)(2,1)}, bf16[2048,512]{1,0:T(8,128)(2,1)S(1)}, u32[]{:S(2)}, u32[]{:S(2)}) collective-permute-start(bf16[2048,512]{1,0:T(8,128)(2,1)} %all-gather.11.cloned.1.call-done.refs_3_), channel_id=1, source_target_pairs={{0,8},{1,17},{2,10},{3,19},{4,12},{5,21},{6,14},{7,23},{8,0},{9,25... | collective-permute-start | bytes 6291464 | tf_op jit(solution)/shard_map/ppermute | solution.py:434
  162.0 7.7 %collective-permute-start.44 = (bf16[1024,512]{1,0:T(8,128)(2,1)S(1)}, bf16[1024,512]{1,0:T(8,128)(2,1)S(1)}, u32[]{:S(2)}, u32[]{:S(2)}) collective-permute-start(bf16[1024,512]{1,0:T(8,128)(2,1)S(1)} %collective-permute-done.38.refs_11_), channel_id=1, source_target_pairs={{0,1},{1,0},{2,3},{3,2},{4,5},{5,4},{6,7},{7,6},{8,9},{9,8},{10,11... | collective-permute-start | bytes 3145736 | tf_op jit(solution)/shard_map/ppermute | solution.py:394
  168.7 23.9 %collective-permute-start.45 = (bf16[2048,512]{1,0:T(8,128)(2,1)}, bf16[2048,512]{1,0:T(8,128)(2,1)}, u32[]{:S(2)}, u32[]{:S(2)}) collective-permute-start(bf16[2048,512]{1,0:T(8,128)(2,1)} %collective-permute-done.42.refs_9_), channel_id=1, source_target_pairs={{0,1},{1,0},{2,3},{3,2},{4,5},{5,4},{6,7},{7,6},{8,9},{9,8},{10,11... | collective-permute-start | bytes 6291464 | tf_op jit(solution)/shard_map/ppermute | solution.py:394
  169.7 1.0 copy-start.8
  192.5 21.0 %copy-start.6 = (bf16[2048,512]{1,0:T(8,128)(2,1)}, bf16[2048,512]{1,0:T(8,128)(2,1)S(1)}, u32[]{:S(2)}) copy-start(bf16[2048,512]{1,0:T(8,128)(2,1)S(1)} %collective-permute-done.41.refs_4_) | copy-start | bytes 6291460
  192.5 21.0 %collective-permute-start.46 = (bf16[2048,512]{1,0:T(8,128)(2,1)S(1)}, bf16[2048,512]{1,0:T(8,128)(2,1)}, u32[]{:S(2)}, u32[]{:S(2)}) collective-permute-start(bf16[2048,512]{1,0:T(8,128)(2,1)S(1)} %collective-permute-done.41.refs_4_), channel_id=1, source_target_pairs={{0,1},{1,0},{2,3},{3,2},{4,5},{5,4},{6,7},{7,6},{8,9},{9,8},{10,11... | collective-permute-start | bytes 6291464 | tf_op jit(solution)/shard_map/ppermute | solution.py:394
Sparse Core Ops, SparseCore 0:
  24.3 27.7 all-gather.6
  53.7 30.5 all-gather.8
  85.9 28.2 all-gather.12
  115.7 28.5 all-gather.10
  145.7 28.5 all-gather.14
  175.8 28.6 all-gather.16
